TPU v7x, 32 devices: a whole 2x2x4 slice. The times are simulated.
32 devices in a mesh: gx: 8 (over y, x, core), gy: 4 (over z).
Axes of the slice: x: 2, y: 2, z: 4, core: 2. Of those that a mesh axis runs over, the one named last changes fastest.
Arguments:
- prior_fields: bfloat16 [512, 16, 1024], P('gx', 'gy'), may hold values from -17 to 17
- measured_spread: bfloat16 [512, 4, 1024], P(None, 'gy', 'gx'), may hold values from -10 to 10
- scaled_misfit: bfloat16 [4, 1024], P('gy', 'gx'), may hold values from -12 to 12
- sensor_line_inside: int32 [4, 1024], P('gy', 'gx'), may hold values from 0 to 3
Outputs:
- analysis: bfloat16 [512, 16, 1024], P(None, 'gy', 'gx')
All inputs are finite; a program needn't handle non-finite values. Where the computation divides by a largest or mean magnitude, that divisor is 1e-20 or more.
Results may differ from a plain program's by a relative error of at most 0.0053.
Values may be sent and summed in bfloat16 or wider, within the bound.
No kernel may reach another device: no remote copies, remote signals or barrier semaphores. Data moves between devices by JAX's collectives and lax.ppermute only.
A program may use at most 64 MiB of HBM per device.

v0:
```python
import jax
import jax.numpy as jnp
from jax import lax
from jax.sharding import PartitionSpec as P

CP = 2
NEWTON = 2


highest = lax.Precision.HIGHEST


def with_halo(shard, sides, width):
    for axis, dim in sides:
        size, length = (lax.axis_size(axis), shard.shape[dim])
        up = [(i, (i + 1) % size) for i in range(size - 1)]
        down = [(j, i) for i, j in up]
        last = lax.slice_in_dim(shard, length - width, length, axis=dim)
        leading = lax.slice_in_dim(shard, 0, width, axis=dim)
        before = lax.ppermute(last, axis, up)
        after = lax.ppermute(leading, axis, down)
        shard = jnp.concatenate([before, shard, after], axis=dim)
    return shard


def localize(positions, centre, radius):
    distance = (positions - centre) / radius
    return jnp.exp(-0.5 * distance * distance)


def newton_weights(gram_matrix, drive_vector, sweeps):
    sample_count = gram_matrix.shape[0]
    identity = jnp.eye(sample_count, dtype=jnp.float32)
    scaled_gram = identity + gram_matrix / (sample_count - 1.0)
    row_bound = jnp.max(jnp.sum(jnp.abs(scaled_gram), axis=1))
    iterate = scaled_gram / row_bound
    inverse = identity
    for newton_step in range(sweeps):
        if newton_step == 0:
            factor = 0.5 * (3.0 * identity - iterate)
            inverse = factor
        else:
            factor = 0.5 * (3.0 * identity - jnp.dot(inverse, iterate, precision=highest))
            inverse = jnp.dot(factor, inverse, precision=highest)
        if newton_step + 1 < sweeps:
            iterate = jnp.dot(iterate, factor, precision=highest)
    first_pass = jnp.dot(inverse, drive_vector, precision=highest)
    mean_weights = jnp.dot(inverse, first_pass, precision=highest) / (
        row_bound * (sample_count - 1.0)
    )
    return (inverse / jnp.sqrt(row_bound) + mean_weights[:, None]).astype(jnp.bfloat16)


def coarse_weights(obs_block, innov_block, positions, centre, radius):
    locality = localize(positions, centre, radius)
    scaled = (obs_block.astype(jnp.float32) * locality[None, :]).astype(jnp.bfloat16)
    gram_matrix = lax.dot_general(
        scaled, obs_block, (((1,), (1,)), ((), ())), preferred_element_type=jnp.float32
    )
    drive_vector = jnp.dot(scaled, innov_block, preferred_element_type=jnp.float32)
    return newton_weights(gram_matrix, drive_vector, NEWTON)


def hat_weights(row_centres, centre, spacing, height):
    clipped = jnp.clip(row_centres, 0.5 * spacing, height - 0.5 * spacing)
    return jnp.maximum(0.0, 1.0 - jnp.abs(clipped - centre) / spacing)


def apply_weights(transform, state_block, interp):
    sample_count, row_count, cell_count = state_block.shape
    product = lax.dot_general(
        transform,
        state_block.reshape(sample_count, row_count * cell_count),
        (((0,), (0,)), ((), ())),
        preferred_element_type=jnp.float32,
    )
    return product.reshape(sample_count, row_count, cell_count) * interp[None, :, None]


def on_device(prior_fields, measured_spread, scaled_misfit, sensor_line_inside):
    sorted_pieces = lax.all_to_all(prior_fields, "gx", split_axis=2, concat_axis=0, tiled=True)
    sample_count, tile_rows, tile_cells = sorted_pieces.shape
    spacing = tile_rows // CP
    half_gap = spacing // 2
    height = tile_rows * lax.axis_size("gy")
    tile_index = lax.axis_index("gy")
    obs_rows = measured_spread.shape[1]
    packed = jnp.concatenate(
        [measured_spread, scaled_misfit[None], sensor_line_inside.astype(jnp.bfloat16)[None]],
        axis=0,
    )
    nearby = with_halo(packed, (("gy", 1),), obs_rows)
    obs_block = nearby[:sample_count].reshape(sample_count, -1)
    innov_block = nearby[sample_count].reshape(-1)
    tile_offset = jnp.arange(3 * obs_rows, dtype=jnp.int32) // obs_rows - 1
    base_rows = ((tile_index + tile_offset) * tile_rows).astype(jnp.float32)
    positions = (base_rows[:, None] + nearby[sample_count + 1].astype(jnp.float32) + 0.5).reshape(
        -1
    )
    own_list = []
    for point_slot in range(CP):
        centre = ((tile_index * CP + point_slot).astype(jnp.float32) + 0.5) * spacing
        own_list.append(coarse_weights(obs_block, innov_block, positions, centre, float(tile_rows)))
    own_weights = jnp.stack(own_list)
    state_mean = jnp.sum(sorted_pieces, axis=0, dtype=jnp.float32) / sample_count
    deviation = (sorted_pieces.astype(jnp.float32) - state_mean[None]).astype(jnp.bfloat16)

    def centres_of(first_row, last_row):
        return (tile_index * tile_rows + jnp.arange(first_row, last_row, dtype=jnp.int32)).astype(
            jnp.float32
        ) + 0.5

    def centre_of(column):
        return ((tile_index * CP + column - 1).astype(jnp.float32) + 0.5) * spacing

    increment = jnp.zeros((sample_count, tile_rows, tile_cells), jnp.float32)
    for column in range(1, CP + 1):
        first_row = max(0, (column - 1) * spacing - half_gap)
        last_row = min(tile_rows, (column - 1) * spacing + spacing + half_gap)
        interp = hat_weights(centres_of(first_row, last_row), centre_of(column), spacing, height)
        increment = increment.at[:, first_row:last_row].add(
            apply_weights(own_weights[column - 1], deviation[:, first_row:last_row], interp)
        )
    state_rims = with_halo(deviation, (("gy", 1),), half_gap)
    below_rows = state_rims[:, :half_gap]
    above_rows = state_rims[:, tile_rows + half_gap :]
    below_interp = hat_weights(centres_of(-half_gap, 0), centre_of(1), spacing, height)
    above_interp = hat_weights(
        centres_of(tile_rows, tile_rows + half_gap), centre_of(CP), spacing, height
    )
    for_previous = apply_weights(own_weights[0], below_rows, below_interp)
    for_next = apply_weights(own_weights[CP - 1], above_rows, above_interp)
    returned = with_halo(
        jnp.concatenate([for_previous, for_next], axis=1).astype(jnp.bfloat16),
        (("gy", 1),),
        half_gap,
    ).astype(jnp.float32)
    increment = increment.at[:, :half_gap].add(returned[:, :half_gap])
    increment = increment.at[:, tile_rows - half_gap :].add(returned[:, 3 * half_gap :])
    return (state_mean[None] + increment).astype(jnp.bfloat16)


def solution(mesh):
    return jax.shard_map(
        on_device,
        mesh=mesh,
        in_specs=(P("gx", "gy", None), P(None, "gy", "gx"), P("gy", "gx"), P("gy", "gx")),
        out_specs=P(None, "gy", "gx"),
        check_vma=False,
    )
```

profile of v0, /device:TPU:0, one launch (start us, length us, event | category | flops | bytes accessed | tf_op | source)
XLA Modules:
  0.0 74.7 jit_solution(15659941551766881761)
XLA Ops:
  0.0 0.7 convert_bitcast_fusion
  0.7 0.9 %pad_maximum_fusion.1 = bf16[514,1,128]{2,0,1:T(8,128)(2,1)S(1)} fusion(bf16[1,1,128]{2,0,1:T(2,128)(2,1)S(1)} %convert_bitcast_fusion, bf16[1,1,128]{2,0,1:T(2,128)(2,1)} %bitcast.114, bf16[512,1,128]{2,0,1:T(8,128)(2,1)} %param.13), kind=kLoop, calls=%fused_computation.76 | loop fusion | flops 394752 | bytes 263168 | tf_op jit(solution)/shard_map/concatenate | solution.py:88
  1.6 1.3 %collective-permute-start.1 = (bf16[514,1,128]{2,0,1:T(8,128)(2,1)S(1)}, bf16[514,1,128]{2,0,1:T(8,128)(2,1)S(1)}, u32[]{:S(2)}, u32[]{:S(2)}) collective-permute-start(bf16[514,1,128]{2,0,1:T(8,128)(2,1)S(1)} %pad_maximum_fusion.1), channel_id=1, source_target_pairs={{1,0},{2,1},{3,2},{5,4},{6,5},{7,6},{9,8},{10,9},{11,10},{13,12},{... | collective-permute-start | bytes 394760 | tf_op jit(solution)/shard_map/ppermute | solution.py:21
  2.9 5.6 %collective-permute-start = (bf16[514,1,128]{2,0,1:T(8,128)(2,1)S(1)}, bf16[514,1,128]{2,0,1:T(8,128)(2,1)S(1)}, u32[]{:S(2)}, u32[]{:S(2)}) collective-permute-start(bf16[514,1,128]{2,0,1:T(8,128)(2,1)S(1)} %pad_maximum_fusion.1), channel_id=1, source_target_pairs={{0,1},{1,2},{2,3},{4,5},{5,6},{6,7},{8,9},{9,10},{10,11},{12,13},{... | collective-permute-start | bytes 394760 | tf_op jit(solution)/shard_map/ppermute | solution.py:20
  8.5 1.9 %copy.63 = bf16[64,4,1024]{0,1,2:T(4,128)(2,1)S(1)} copy(bf16[64,4,1024]{2,1,0:T(4,128)(2,1)} %param.12) | data formatting | bytes 1048576 | tf_op args[0]
  10.4 1.5 %reshape.303 = bf16[8,2,16384]{2,1,0:T(2,128)(2,1)} reshape(bf16[1024,4,64]{2,1,0:T(4,128)(2,1)S(1)} %bitcast.108) | data formatting | bytes 1048576
  11.9 4.2 %all-to-all-start = ((bf16[8,2,16384]{2,1,0:T(2,128)(2,1)}), bf16[8,2,16384]{2,1,0:T(2,128)(2,1)S(1)}, u32[]{:S(2)}, u32[]{:S(2)}) async-start(bf16[8,2,16384]{2,1,0:T(2,128)(2,1)} %reshape.303), calls=%async_computation | async-start | bytes 1048576 | tf_op jit(solution)/shard_map/all_to_all | solution.py:81
  16.3 0.1 fusion.24
  16.4 0.2 copy.69
  16.6 1.5 %abs_reduce_fusion.1 = (f32[512]{0:T(512)S(1)}, f32[512,512]{0,1:T(8,128)}) fusion(bf16[512,3,128]{2,0,1:T(8,128)(2,1)S(1)} %get-tuple-element.58, bf16[514,3,128]{2,0,1:T(8,128)(2,1)S(1)} %pad_maximum_fusion), kind=kOutput, calls=%fused_computation.38 | convolution fusion | flops 202898944 | bytes 1837056 | tf_op jit(solution)/shard_map/dot_general | solution.py:57
  18.1 0.2 copy.74
  18.3 1.5 %abs_reduce_fusion = (f32[512]{0:T(512)S(1)}, f32[512,512]{0,1:T(8,128)}) fusion(bf16[512,3,128]{2,0,1:T(8,128)(2,1)S(1)} %get-tuple-element.57, bf16[514,3,128]{2,0,1:T(8,128)(2,1)S(1)} %pad_maximum_fusion), kind=kOutput, calls=%fused_computation.36 | convolution fusion | flops 202898944 | bytes 1837056 | tf_op jit(solution)/shard_map/dot_general | solution.py:57
  19.8 0.6 reduce_max.18
  21.7 0.6 reduce_max.19
  23.4 0.2 convolution_bitcast_fusion.3
  23.5 0.2 convolution_bitcast_fusion.5
  23.7 5.8 %fusion.20 = f32[512,512]{1,0:T(8,128)S(1)} fusion(f32[512,512]{0,1:T(8,128)} %get-tuple-element.66, f32[]{:T(128)} %reduce_max.19), kind=kOutput, calls=%fused_computation.31 | convolution fusion | flops 1612185600 | bytes 2097156 | tf_op jit(solution)/shard_map/dot_general | solution.py:46
  29.5 2.5 %fusion.3 = f32[512,512]{0,1:T(8,128)S(1)} fusion(f32[512,512]{1,0:T(8,128)S(1)} %fusion.20, f32[512,512]{0,1:T(8,128)S(1)} %copy-done.3, f32[]{:T(128)} %reduce_max.19), kind=kOutput, calls=%fused_computation.11 | convolution fusion | flops 1612972032 | bytes 3145732 | tf_op jit(solution)/shard_map/dot_general | solution.py:43
  32.0 4.0 %fusion.17 = f32[512,512]{1,0:T(8,128)S(1)} fusion(f32[512,512]{0,1:T(8,128)S(1)} %fusion.3, f32[512,512]{0,1:T(8,128)S(1)} %copy-done.3, f32[]{:T(128)} %reduce_max.19), kind=kOutput, calls=%fused_computation.30 | convolution fusion | flops 1611923456 | bytes 3145732 | tf_op jit(solution)/shard_map/dot_general | solution.py:44
  36.1 1.0 %convolution_bitcast_fusion.2 = f32[512,1]{0,1:T(1,128)S(1)} fusion(f32[512,512]{1,0:T(8,128)S(1)} %fusion.17, f32[512,1]{0,1:T(1,128)S(1)} %convolution_bitcast_fusion.3), kind=kOutput, calls=%fused_computation.22 | convolution fusion | flops 3145728 | bytes 1052672 | tf_op jit(solution)/shard_map/dot_general | solution.py:47
  37.1 1.0 %fusion.75 = f32[1,512]{1,0:T(1,128)S(1)} fusion(f32[512,512]{1,0:T(8,128)S(1)} %fusion.17, f32[512,1]{0,1:T(1,128)S(1)} %convolution_bitcast_fusion.2), kind=kOutput, calls=%fused_computation.116 | convolution fusion | flops 3145728 | bytes 1052672 | tf_op jit(solution)/shard_map/dot_general | solution.py:48
  38.1 4.3 %fusion.14 = f32[512,512]{1,0:T(8,128)S(1)} fusion(f32[512,512]{0,1:T(8,128)S(1)} %copy-done.2, f32[]{:T(128)} %reduce_max.18), kind=kOutput, calls=%fused_computation.28 | convolution fusion | flops 1612185600 | bytes 2097156 | tf_op jit(solution)/shard_map/dot_general | solution.py:46
  42.4 2.6 %fusion.2 = f32[512,512]{0,1:T(8,128)S(1)} fusion(f32[512,512]{1,0:T(8,128)S(1)} %fusion.14, f32[512,512]{0,1:T(8,128)S(1)} %copy-done.2, f32[]{:T(128)} %reduce_max.18), kind=kOutput, calls=%fused_computation.10 | convolution fusion | flops 1612972032 | bytes 3145732 | tf_op jit(solution)/shard_map/dot_general | solution.py:43
  45.0 4.1 %fusion.11 = f32[512,512]{1,0:T(8,128)S(1)} fusion(f32[512,512]{0,1:T(8,128)S(1)} %fusion.2, f32[512,512]{0,1:T(8,128)S(1)} %copy-done.2, f32[]{:T(128)} %reduce_max.18), kind=kOutput, calls=%fused_computation.27 | convolution fusion | flops 1611923456 | bytes 3145732 | tf_op jit(solution)/shard_map/dot_general | solution.py:44
  49.1 1.0 %convolution_bitcast_fusion.4 = f32[512,1]{0,1:T(1,128)S(1)} fusion(f32[512,512]{1,0:T(8,128)S(1)} %fusion.11, f32[512,1]{0,1:T(1,128)S(1)} %convolution_bitcast_fusion.5), kind=kOutput, calls=%fused_computation.24 | convolution fusion | flops 3145728 | bytes 1052672 | tf_op jit(solution)/shard_map/dot_general | solution.py:47
  50.0 1.0 %fusion.74 = f32[1,512]{1,0:T(1,128)S(1)} fusion(f32[512,512]{1,0:T(8,128)S(1)} %fusion.11, f32[512,1]{0,1:T(1,128)S(1)} %convolution_bitcast_fusion.4), kind=kOutput, calls=%fused_computation.115 | convolution fusion | flops 3145728 | bytes 1052672 | tf_op jit(solution)/shard_map/dot_general | solution.py:48
  51.0 0.2 add_convert_fusion.1
  51.2 0.1 add_convert_fusion.2
  51.4 0.7 reshape.304
  52.1 1.2 %convert_reduce_fusion = f32[4,1024]{0,1:T(8,128)S(1)} fusion(bf16[1024,4,64]{2,1,0:T(4,128)(2,1)S(1)} %reshape.304), kind=kLoop, calls=%fused_computation.66 | loop fusion | flops 520192 | bytes 540672 | tf_op jit(solution)/shard_map/reduce_sum | solution.py:105
  53.3 0.9 %copy.70 = f32[64,4,8,128]{3,0,2,1:T(8,128)S(1)} copy(bf16[64,4,8,128]{0,1,3,2:T(4,128)(2,1)S(1)} %bitcast.107) | data formatting | bytes 1572864 | tf_op jit(solution)/shard_map/convert_element_type | solution.py:105
  54.2 0.1 fusion.22
  54.3 0.1 fusion.73
  54.4 1.3 %collective-permute-start.2 = (bf16[512,1,128]{2,0,1:T(8,128)(2,1)S(1)}, bf16[512,1,128]{2,0,1:T(8,128)(2,1)S(1)}, u32[]{:S(2)}, u32[]{:S(2)}) collective-permute-start(bf16[512,1,128]{2,0,1:T(8,128)(2,1)S(1)} %get-tuple-element.53), channel_id=1, source_target_pairs={{1,0},{2,1},{3,2},{5,4},{6,5},{7,6},{9,8},{10,9},{11,10},{13,12},{... | collective-permute-start | bytes 393224 | tf_op jit(solution)/shard_map/ppermute | solution.py:21
  55.7 4.6 %collective-permute-start.4 = (bf16[512,1,128]{2,0,1:T(8,128)(2,1)S(1)}, bf16[512,1,128]{2,0,1:T(8,128)(2,1)S(1)}, u32[]{:S(2)}, u32[]{:S(2)}) collective-permute-start(bf16[512,1,128]{2,0,1:T(8,128)(2,1)S(1)} %get-tuple-element.54), channel_id=1, source_target_pairs={{0,1},{1,2},{2,3},{4,5},{5,6},{6,7},{8,9},{9,10},{10,11},{12,13},{... | collective-permute-start | bytes 393224 | tf_op jit(solution)/shard_map/ppermute | solution.py:20
  60.3 0.2 copy.71
  60.5 0.5 convolution_multiply_fusion.1
  61.0 0.2 copy.75
  61.2 1.0 %collective-permute-done.2 = bf16[512,1,128]{2,0,1:T(8,128)(2,1)S(1)} collective-permute-done((bf16[512,1,128]{2,0,1:T(8,128)(2,1)S(1)}, bf16[512,1,128]{2,0,1:T(8,128)(2,1)S(1)}, u32[]{:S(2)}, u32[]{:S(2)}) %collective-permute-start.2) | collective-permute-done | bytes 131104 | tf_op jit(solution)/shard_map/ppermute | solution.py:21
  62.2 0.3 fusion.9
  62.6 3.5 %collective-permute-start.3 = (bf16[512,1,128]{2,0,1:T(8,128)(2,1)S(1)}, bf16[512,1,128]{2,0,1:T(8,128)(2,1)S(1)}, u32[]{:S(2)}, u32[]{:S(2)}) collective-permute-start(bf16[512,1,128]{2,0,1:T(8,128)(2,1)S(1)} %fusion.9), channel_id=1, source_target_pairs={{0,1},{1,2},{2,3},{4,5},{5,6},{6,7},{8,9},{9,10},{10,11},{12,13},{... | collective-permute-start | bytes 393224 | tf_op jit(solution)/shard_map/ppermute | solution.py:20
  66.1 0.3 fusion.8
  66.4 1.3 %collective-permute-start.5 = (bf16[512,1,128]{2,0,1:T(8,128)(2,1)S(1)}, bf16[512,1,128]{2,0,1:T(8,128)(2,1)S(1)}, u32[]{:S(2)}, u32[]{:S(2)}) collective-permute-start(bf16[512,1,128]{2,0,1:T(8,128)(2,1)S(1)} %fusion.8), channel_id=1, source_target_pairs={{1,0},{2,1},{3,2},{5,4},{6,5},{7,6},{9,8},{10,9},{11,10},{13,12},{... | collective-permute-start | bytes 393224 | tf_op jit(solution)/shard_map/ppermute | solution.py:21
  67.7 0.5 fusion.5
  68.2 0.4 collective-permute-done.3
  68.7 4.6 %collective-permute-done.5 = bf16[512,1,128]{2,0,1:T(8,128)(2,1)S(1)} collective-permute-done((bf16[512,1,128]{2,0,1:T(8,128)(2,1)S(1)}, bf16[512,1,128]{2,0,1:T(8,128)(2,1)S(1)}, u32[]{:S(2)}, u32[]{:S(2)}) %collective-permute-start.5) | collective-permute-done | bytes 131104 | tf_op jit(solution)/shard_map/ppermute | solution.py:21
  73.4 0.1 add_convert_fusion
  73.5 1.2 %copy.77 = bf16[512,4,128]{2,1,0:T(4,128)(2,1)} copy(bf16[512,4,128]{2,0,1:T(8,128)(2,1)S(1)} %add_convert_fusion) | data formatting | bytes 1048576 | tf_op jit(solution)/shard_map/convert_element_type | solution.py:140
  (27 shorter events, 0.5 us)
Async XLA Ops:
  1.6 14.5 %collective-permute-start.1 = (bf16[514,1,128]{2,0,1:T(8,128)(2,1)S(1)}, bf16[514,1,128]{2,0,1:T(8,128)(2,1)S(1)}, u32[]{:S(2)}, u32[]{:S(2)}) collective-permute-start(bf16[514,1,128]{2,0,1:T(8,128)(2,1)S(1)} %pad_maximum_fusion.1), channel_id=1, source_target_pairs={{1,0},{2,1},{3,2},{5,4},{6,5},{7,6},{9,8},{10,9},{11,10},{13,12},{... | collective-permute-start | bytes 394760 | tf_op jit(solution)/shard_map/ppermute | solution.py:21
  2.9 13.2 %collective-permute-start = (bf16[514,1,128]{2,0,1:T(8,128)(2,1)S(1)}, bf16[514,1,128]{2,0,1:T(8,128)(2,1)S(1)}, u32[]{:S(2)}, u32[]{:S(2)}) collective-permute-start(bf16[514,1,128]{2,0,1:T(8,128)(2,1)S(1)} %pad_maximum_fusion.1), channel_id=1, source_target_pairs={{0,1},{1,2},{2,3},{4,5},{5,6},{6,7},{8,9},{9,10},{10,11},{12,13},{... | collective-permute-start | bytes 394760 | tf_op jit(solution)/shard_map/ppermute | solution.py:20
  10.3 5.8 %copy-start = (bf16[512,1,128]{2,0,1:T(8,128)(2,1)S(1)}, bf16[512,1,128]{2,0,1:T(8,128)(2,1)}, u32[]{:S(2)}) copy-start(bf16[512,1,128]{2,0,1:T(8,128)(2,1)} %param.13) | copy-start | bytes 393220
  10.4 5.8 %copy-start.1 = (bf16[1,128]{1,0:T(2,128)(2,1)S(1)}, bf16[1,128]{1,0:T(2,128)(2,1)}, u32[]{:S(2)}) copy-start(bf16[1,128]{1,0:T(2,128)(2,1)} %param.14) | copy-start | bytes 772
  11.9 39.5 %all-to-all-start = ((bf16[8,2,16384]{2,1,0:T(2,128)(2,1)}), bf16[8,2,16384]{2,1,0:T(2,128)(2,1)S(1)}, u32[]{:S(2)}, u32[]{:S(2)}) async-start(bf16[8,2,16384]{2,1,0:T(2,128)(2,1)} %reshape.303), calls=%async_computation | async-start | bytes 1048576 | tf_op jit(solution)/shard_map/all_to_all | solution.py:81
  23.7 5.8 %copy-start.3 = (f32[512,512]{0,1:T(8,128)S(1)}, f32[512,512]{0,1:T(8,128)}, u32[]{:S(2)}) copy-start(f32[512,512]{0,1:T(8,128)} %get-tuple-element.66) | copy-start | bytes 3145732
  36.1 2.0 %copy-start.2 = (f32[512,512]{0,1:T(8,128)S(1)}, f32[512,512]{0,1:T(8,128)}, u32[]{:S(2)}) copy-start(f32[512,512]{0,1:T(8,128)} %get-tuple-element.64) | copy-start | bytes 3145732
  54.4 7.8 %collective-permute-start.2 = (bf16[512,1,128]{2,0,1:T(8,128)(2,1)S(1)}, bf16[512,1,128]{2,0,1:T(8,128)(2,1)S(1)}, u32[]{:S(2)}, u32[]{:S(2)}) collective-permute-start(bf16[512,1,128]{2,0,1:T(8,128)(2,1)S(1)} %get-tuple-element.53), channel_id=1, source_target_pairs={{1,0},{2,1},{3,2},{5,4},{6,5},{7,6},{9,8},{10,9},{11,10},{13,12},{... | collective-permute-start | bytes 393224 | tf_op jit(solution)/shard_map/ppermute | solution.py:21
  55.7 10.3 %collective-permute-start.4 = (bf16[512,1,128]{2,0,1:T(8,128)(2,1)S(1)}, bf16[512,1,128]{2,0,1:T(8,128)(2,1)S(1)}, u32[]{:S(2)}, u32[]{:S(2)}) collective-permute-start(bf16[512,1,128]{2,0,1:T(8,128)(2,1)S(1)} %get-tuple-element.54), channel_id=1, source_target_pairs={{0,1},{1,2},{2,3},{4,5},{5,6},{6,7},{8,9},{9,10},{10,11},{12,13},{... | collective-permute-start | bytes 393224 | tf_op jit(solution)/shard_map/ppermute | solution.py:20
  62.6 6.1 %collective-permute-start.3 = (bf16[512,1,128]{2,0,1:T(8,128)(2,1)S(1)}, bf16[512,1,128]{2,0,1:T(8,128)(2,1)S(1)}, u32[]{:S(2)}, u32[]{:S(2)}) collective-permute-start(bf16[512,1,128]{2,0,1:T(8,128)(2,1)S(1)} %fusion.9), channel_id=1, source_target_pairs={{0,1},{1,2},{2,3},{4,5},{5,6},{6,7},{8,9},{9,10},{10,11},{12,13},{... | collective-permute-start | bytes 393224 | tf_op jit(solution)/shard_map/ppermute | solution.py:20
  66.4 6.9 %collective-permute-start.5 = (bf16[512,1,128]{2,0,1:T(8,128)(2,1)S(1)}, bf16[512,1,128]{2,0,1:T(8,128)(2,1)S(1)}, u32[]{:S(2)}, u32[]{:S(2)}) collective-permute-start(bf16[512,1,128]{2,0,1:T(8,128)(2,1)S(1)} %fusion.8), channel_id=1, source_target_pairs={{1,0},{2,1},{3,2},{5,4},{6,5},{7,6},{9,8},{10,9},{11,10},{13,12},{... | collective-permute-start | bytes 393224 | tf_op jit(solution)/shard_map/ppermute | solution.py:21
where the time goes:
time: 75.1 us; the launch traced here: 74.7 us
  matrix products  32.3 us (43%)
  starting transfers between devices  21.6 us (29%)
  local copies, waits for them, and re-layouts  7.07 us (9%)
  waiting for transfers between devices  6.03 us (8%)
  other arithmetic  4.85 us (6%)
  between operations  2.84 us (4%)
    ppermute x3, starting transfers between devices, with_halo(): before = lax.ppermute(last, axis, up)  13.6 us
    dot_general x2, matrix products, newton_weights(): iterate = jnp.dot(iterate, factor, precision=highest)  10.1 us
    dot_general x2, matrix products, newton_weights(): inverse = jnp.dot(factor, inverse, precision=highest)  8.11 us
    ppermute x3, waiting for transfers between devices, with_halo(): after = lax.ppermute(leading, axis, down)  5.6 us
    dot_general x2, matrix products, newton_weights(): jnp.dot(inverse, iterate, precision=highest)  5.11 us
    all_to_all x1, starting transfers between devices, on_device(): lax.all_to_all(prior_fields, 'gx', split_axis=2, concat_axis=0, tiled=True)  4.16 us
    unnamed x11, local copies, waits for them, and re-layouts  4.05 us
    ppermute x3, starting transfers between devices, with_halo(): after = lax.ppermute(leading, axis, down)  3.88 us
  transfers between devices with their start and end apart: 7, of which 3 were waited for; matrix products, arithmetic and copies ran while one was open for 51% of the time, Pallas kernels for 0%

commit v1 on v0

v1 whole, which is shorter than its diff:
```python
import functools

import jax
import jax.numpy as jnp
from jax import lax
from jax.experimental import pallas as pl
from jax.experimental.pallas import tpu as pltpu
from jax.sharding import PartitionSpec as P

CP = 2
PAD = 16
MIB = 1 << 20

VMEM = pl.BlockSpec(memory_space=pltpu.VMEM)


def swap_pairs(size, reach, phase):
    lows = [i for i in range(size - reach) if (i // reach) % 2 == phase]
    return [pair for i in lows for pair in ((i, i + reach), (i + reach, i))]


def prepare_kernel(parts, rows, prior_ref, spread_ref, misfit_ref, line_ref, packed_ref, sorted_ref, wide):
    members = prior_ref.shape[0] // (parts * rows)
    count = spread_ref.shape[0]
    packed_ref[0:count, :] = spread_ref[...]
    width = spread_ref.shape[1]
    which = lax.broadcasted_iota(jnp.int32, (PAD, width), 0)
    misfit = jnp.broadcast_to(misfit_ref[...].astype(jnp.float32), (PAD, width))
    line = jnp.broadcast_to(line_ref[...].astype(jnp.float32), (PAD, width))
    extra = jnp.where(which == 0, misfit, jnp.where(which == 1, line, 0.0))
    packed_ref[count:, :] = extra.astype(jnp.bfloat16)
    wide[...] = prior_ref[...].astype(jnp.float32)
    for part in range(parts):
        for row in range(rows):
            lines = wide[pl.ds(part * rows + row, members, stride=parts * rows), :]
            sorted_ref[part, row] = lines.astype(jnp.bfloat16)


def prepare(prior, spread, misfit, line, parts):
    members, rows, cells = prior.shape
    width = cells // parts
    count, obs = spread.shape
    flat = prior.reshape(members, rows, parts, width).transpose(0, 2, 1, 3).reshape(-1, width)
    return pl.pallas_call(
        functools.partial(prepare_kernel, parts, rows),
        out_shape=(
            jax.ShapeDtypeStruct((count + PAD, obs), jnp.bfloat16),
            jax.ShapeDtypeStruct((parts, rows, members, width), jnp.bfloat16),
        ),
        in_specs=[VMEM] * 4,
        out_specs=(VMEM, VMEM),
        scratch_shapes=[pltpu.VMEM(flat.shape, jnp.float32)],
        compiler_params=pltpu.CompilerParams(vmem_limit_bytes=24 * MIB),
        name="prepare",
    )(flat, spread, misfit, line)


def select_flag(condition):
    return jnp.where(condition, jnp.float32(1.0), jnp.float32(0.0))


def point_weights(left, count, radius, centre, bases, present):
    line = left[count + 1 : count + 2, :].astype(jnp.float32)
    obs = line.shape[1] // 3
    where = lax.broadcasted_iota(jnp.int32, line.shape, 1) // obs
    base = jnp.where(where == 0, bases[0], jnp.where(where == 1, bases[1], bases[2]))
    alive = jnp.where(where == 0, present[0], jnp.where(where == 1, present[1], present[2]))
    distance = (base + line + 0.5 - centre) / radius
    locality = jnp.exp(-0.5 * distance * distance) * alive
    scaled = (left[0:count, :].astype(jnp.float32) * locality).astype(jnp.bfloat16)
    both = lax.dot_general(
        left[...], scaled, (((1,), (1,)), ((), ())), preferred_element_type=jnp.float32
    )
    gram = both[0:count]
    drive = both[count : count + 1]
    share = 1.0 / (count - 1.0)
    on_diagonal = lax.broadcasted_iota(jnp.int32, gram.shape, 0) == lax.broadcasted_iota(
        jnp.int32, gram.shape, 1
    )
    sizes = jnp.abs(jnp.where(on_diagonal, 1.0, 0.0) + gram * share)
    bound = jnp.max(jnp.sum(sizes, axis=0, keepdims=True), axis=1, keepdims=True)
    rounded = gram.astype(jnp.bfloat16)
    square = jnp.dot(rounded, rounded, preferred_element_type=jnp.float32)
    s = 1.0 / bound
    g = s * share
    first = jnp.broadcast_to(g, (1, count))
    second = jnp.broadcast_to(g * g, (1, count))
    beta = s * s - 9.0 * s
    quad = second * square
    x = (2.0 * s) * first * gram + quad
    w = (2.0 * s - 9.0) * first * gram + quad
    product = jnp.dot(x.astype(jnp.bfloat16), w.astype(jnp.bfloat16), preferred_element_type=jnp.float32)
    on_gram = (-39.0 + (27.0 + beta) * (2.0 * s) + s * s * (2.0 * s - 9.0)) * first / 16.0
    on_square = (27.0 + beta + s * s) * second / 16.0
    rest = on_gram * gram + on_square * square + product * (1.0 / 16.0)
    scalar_part = (36.0 + s * (-39.0 + s * (27.0 + s * (-9.0 + s)))) / 16.0
    rest_rounded = rest.astype(jnp.bfloat16)

    def row_times(row):
        high = row.astype(jnp.bfloat16).astype(jnp.float32)
        which = lax.broadcasted_iota(jnp.int32, (PAD, count), 0)
        two = jnp.where(which == 0, high, jnp.where(which == 1, row - high, 0.0))
        out = jnp.dot(two.astype(jnp.bfloat16), rest_rounded, preferred_element_type=jnp.float32)
        return out[0:1] + out[1:2] + scalar_part * row

    mean_weights = row_times(row_times(drive)) * g
    root = lax.rsqrt(bound)
    return rest * jnp.broadcast_to(root, (1, count)), scalar_part * root, mean_weights


def weights_kernel(size, rows, spacing, has_far, *refs):
    own_ref, first_ref, other_ref = refs[:3]
    far_refs = refs[3 : 3 + sum(has_far)]
    mix_ref, diag_ref, left = refs[3 + sum(has_far) :]
    tile = lax.axis_index("gy")
    count = own_ref.shape[0] - PAD
    obs = own_ref.shape[1]
    even = lax.rem(tile, 2) == 0
    low_half = lax.rem(tile // 2, 2) == 0
    slots = CP + 2
    far = []
    index = 0
    for there in has_far:
        far.append(far_refs[index][...] if there else None)
        index += 1 if there else 0
    left[:, 2 * obs : 3 * obs] = own_ref[...]
    left[:, obs : 2 * obs] = jnp.where(even, other_ref[...], first_ref[...])
    left[:, 3 * obs : 4 * obs] = jnp.where(even, first_ref[...], other_ref[...])
    blank = jnp.zeros(own_ref.shape, jnp.bfloat16)
    near, beyond = [blank if block is None else block for block in far]
    left[:, 0:obs] = jnp.where(low_half, beyond, near)
    left[:, 4 * obs :] = jnp.where(low_half, near, beyond)
    present = []
    for offset in range(-2, 3):
        present.append(select_flag((tile + offset >= 0) & (tile + offset < size)))
    parts = []
    for slot in range(slots):
        point = slot - 1
        owner = point // CP
        centre = (point + 0.5) * spacing
        bases = [float((owner + step) * rows) for step in (-1, 0, 1)]
        parts.append(
            point_weights(
                left.at[:, (owner + 1) * obs : (owner + 4) * obs],
                count,
                float(rows),
                centre,
                bases,
                present[owner + 1 : owner + 4],
            )
        )
    height = float(rows * size)
    start = (tile * rows).astype(jnp.float32)
    for row in range(rows):
        low = int((row + 0.5) / spacing + 0.5)
        shares = []
        for slot in (low, low + 1):
            place = jnp.clip(start + (row + 0.5), 0.5 * spacing, height - 0.5 * spacing)
            centre = start + (slot - 0.5) * spacing
            shares.append(jnp.maximum(0.0, 1.0 - jnp.abs(place - centre) / spacing))
        mixed = shares[0] * parts[low][0] + shares[1] * parts[low + 1][0]
        mix_ref[row, 0:count, :] = mixed.astype(jnp.bfloat16)
        mean_row = shares[0] * parts[low][2] + shares[1] * parts[low + 1][2]
        high = mean_row.astype(jnp.bfloat16).astype(jnp.float32)
        which = lax.broadcasted_iota(jnp.int32, (PAD, count), 0)
        two = jnp.where(which == 0, high, jnp.where(which == 1, mean_row - high, 0.0))
        mix_ref[row, count:, :] = two.astype(jnp.bfloat16)
        diag = shares[0] * parts[low][1] + shares[1] * parts[low + 1][1]
        diag_ref[row] = jnp.broadcast_to(diag, (8, 128))


def weights(own, first, other, far, size, rows):
    count = own.shape[0] - PAD
    has_far = tuple(block is not None for block in far)
    blocks = [own, first, other] + [block for block in far if block is not None]
    cube = count * count * count
    return pl.pallas_call(
        functools.partial(weights_kernel, size, rows, rows // CP, has_far),
        out_shape=(
            jax.ShapeDtypeStruct((rows, count + PAD, count), jnp.bfloat16),
            jax.ShapeDtypeStruct((rows, 8, 128), jnp.float32),
        ),
        in_specs=[VMEM] * len(blocks),
        out_specs=(VMEM, VMEM),
        scratch_shapes=[pltpu.VMEM((own.shape[0], 5 * own.shape[1]), jnp.bfloat16)],
        compiler_params=pltpu.CompilerParams(vmem_limit_bytes=48 * MIB),
        cost_estimate=pl.CostEstimate(
            flops=24 * cube, bytes_accessed=8 * count * count, transcendentals=0
        ),
        name="weights",
    )(*blocks)


def analyse_kernel(rows, sorted_ref, mix_ref, diag_ref, out_ref, wide):
    parts, _, members, width = sorted_ref.shape
    count = parts * members
    for row in range(rows):
        prior = sorted_ref[:, row].reshape(count, width).astype(jnp.float32)
        mean = jnp.sum(prior, axis=0, keepdims=True) / count
        deviation = (prior - mean).astype(jnp.bfloat16)
        term = jnp.dot(mix_ref[row], deviation, preferred_element_type=jnp.float32)
        shift = mean + term[count : count + 1] + term[count + 1 : count + 2]
        diag = jnp.broadcast_to(diag_ref[row, 0:1, 0:1], (1, width))
        wide[pl.ds(row, count, stride=rows), :] = (
            term[0:count] + diag * deviation.astype(jnp.float32) + shift
        )
    out_ref[...] = wide[...].astype(jnp.bfloat16)


def analyse(blocks, mix, diag):
    parts, rows, members, width = blocks.shape
    count = parts * members
    flat = pl.pallas_call(
        functools.partial(analyse_kernel, rows),
        out_shape=jax.ShapeDtypeStruct((count * rows, width), jnp.bfloat16),
        in_specs=[VMEM] * 3,
        out_specs=VMEM,
        scratch_shapes=[pltpu.VMEM((count * rows, width), jnp.float32)],
        compiler_params=pltpu.CompilerParams(vmem_limit_bytes=24 * MIB),
        name="analyse",
    )(blocks, mix, diag)
    return flat.reshape(count, rows, width)


def on_device(prior_fields, measured_spread, scaled_misfit, sensor_line_inside):
    parts = lax.axis_size("gx")
    size = lax.axis_size("gy")
    count = measured_spread.shape[0]
    rows = prior_fields.shape[1]
    packed, to_send = prepare(
        prior_fields,
        measured_spread.reshape(count, -1),
        scaled_misfit.reshape(1, -1),
        sensor_line_inside.reshape(1, -1),
        parts,
    )

    def trade(pairs):
        return lax.ppermute(packed, "gy", pairs) if pairs else None

    first = trade(swap_pairs(size, 1, 0))
    other = trade(swap_pairs(size, 1, 1))
    far = [trade(swap_pairs(size, 2, 0)), trade(swap_pairs(size, 2, 1))]
    blocks = lax.all_to_all(to_send, "gx", split_axis=0, concat_axis=0, tiled=True)
    mix, diag = weights(packed, first, other, far, size, rows)
    return analyse(blocks, mix, diag)


def solution(mesh):
    return jax.shard_map(
        on_device,
        mesh=mesh,
        in_specs=(P("gx", "gy", None), P(None, "gy", "gx"), P("gy", "gx"), P("gy", "gx")),
        out_specs=P(None, "gy", "gx"),
        check_vma=False,
    )
```

time: 75.1 us -> 30.6 us (0.41)
  matrix products: 32.3 us -> 0 us
  starting transfers between devices: 21.6 us -> 11.3 us
  Pallas kernels: 0 us -> 10 us
  other arithmetic: 4.85 us -> 0 us
  local copies, waits for them, and re-layouts: 7.07 us -> 3.25 us
  between operations: 2.84 us -> 0.03 us
    dot_general x18 -> x0, matrix products: 32.3 us -> none  [the longest x2 10.1 us: newton_weights(): iterate = jnp.dot(iterate, factor, precision=highest)]
    ppermute x6 -> x3, starting transfers between devices: 17.5 us -> 6.14 us  [trade(): return lax.ppermute(packed, 'gy', pairs) if pairs else None]
    pallas_call x0 -> x3, Pallas kernels: none -> 10 us  [the longest x1 6.76 us: weights(): pl.pallas_call(functools.partial(weights_kernel, size, rows, rows // CP,...]
    convert_element_type x4 -> x0, local copies, waits for them, and re-layouts: 2.43 us -> none  [the longest x1 1.2 us: on_device(): return (state_mean[None] + increment).astype(jnp.bfloat16)]
    reduce_sum x2 -> x0, other arithmetic: 1.19 us -> none  [on_device(): jnp.sum(sorted_pieces, axis=0, dtype=jnp.float32) / sample_count]
    reduce_max x2 -> x0, other arithmetic: 1.18 us -> none  [newton_weights(): row_bound = jnp.max(jnp.sum(jnp.abs(scaled_gram), axis=1))]
    all_to_all x1, starting transfers between devices: 4.16 us -> 5.17 us  [on_device(): lax.all_to_all(to_send, 'gx', split_axis=0, concat_axis=0, tiled=True)]
    concatenate x2 -> x0, other arithmetic: 0.96 us -> none  [the longest x1 0.93 us: on_device(): jnp.concatenate([measured_spread, scaled_misfit[None], sensor_line_inside...]
  transfers between devices with their start and end apart: 7 -> 4, of which waited for: 3 -> 2; matrix products, arithmetic and copies ran while one was open for 51% -> 0% of each run, Pallas kernels for 0% -> 22%
where the time goes in v1:
time: 30.6 us; the launch traced here: 30.4 us
  starting transfers between devices  11.3 us (37%)
  Pallas kernels  10 us (33%)
  waiting for transfers between devices  5.76 us (19%)
  local copies, waits for them, and re-layouts  3.25 us (11%)
    pallas_call x1, Pallas kernels, weights(): pl.pallas_call(functools.partial(weights_kernel, size, rows, rows // CP,...  6.76 us
    ppermute x3, starting transfers between devices, trade(): return lax.ppermute(packed, 'gy', pairs) if pairs else None  6.14 us
    ppermute x3, waiting for transfers between devices, trade(): return lax.ppermute(packed, 'gy', pairs) if pairs else None  5.76 us
    all_to_all x1, starting transfers between devices, on_device(): lax.all_to_all(to_send, 'gx', split_axis=0, concat_axis=0, tiled=True)  5.17 us
    unnamed x8, local copies, waits for them, and re-layouts  3.25 us
    pallas_call x1, Pallas kernels, analyse(): pl.pallas_call(functools.partial(analyse_kernel, rows), out_shape=jax.Sha...  1.8 us
    pallas_call x1, Pallas kernels, prepare(): pl.pallas_call(functools.partial(prepare_kernel, parts, rows), out_shape=...  1.45 us
  transfers between devices with their start and end apart: 4, of which 2 were waited for; matrix products, arithmetic and copies ran while one was open for 0% of the time, Pallas kernels for 22%

profile of v1, /device:TPU:0, one launch (start us, length us, event | category | flops | bytes accessed | tf_op | source)
XLA Modules:
  0.0 30.4 jit_solution(12785397130296363513)
XLA Ops:
  0.0 0.0 copy-start
  0.0 1.0 %copy-done = bf16[64,4,1024]{2,1,0:T(4,128)(2,1)S(1)} copy-done((bf16[64,4,1024]{2,1,0:T(4,128)(2,1)S(1)}, bf16[64,4,1024]{2,1,0:T(4,128)(2,1)}, u32[]{:S(2)}) %copy-start) | copy-done | bytes 524312
  1.0 0.0 copy-start.1
  1.0 0.9 %copy-done.1 = bf16[512,1,128]{2,0,1:T(8,128)(2,1)S(1)} copy-done((bf16[512,1,128]{2,0,1:T(8,128)(2,1)S(1)}, bf16[512,1,128]{2,0,1:T(8,128)(2,1)}, u32[]{:S(2)}) %copy-start.1) | copy-done | bytes 131096
  1.9 0.0 copy-start.2
  1.9 0.7 %copy-done.2 = bf16[1,128]{1,0:T(2,128)(2,1)S(1)} copy-done((bf16[1,128]{1,0:T(2,128)(2,1)S(1)}, bf16[1,128]{1,0:T(2,128)(2,1)}, u32[]{:S(2)}) %copy-start.2) | copy-done | bytes 280
  2.6 0.0 copy-start.3
  2.6 0.7 %copy-done.3 = s32[1,128]{1,0:T(1,128)S(1)} copy-done((s32[1,128]{1,0:T(1,128)S(1)}, s32[1,128]{1,0:T(1,128)}, u32[]{:S(2)}) %copy-start.3) | copy-done | bytes 536
  3.3 1.4 %prepare.1 = (bf16[528,128]{1,0:T(8,128)(2,1)S(1)}, bf16[8,4,64,128]{3,2,1,0:T(8,128)(2,1)}) custom-call(bf16[2048,128]{1,0:T(8,128)(2,1)S(1)} %bitcast.7, bf16[512,128]{1,0:T(8,128)(2,1)S(1)} %bitcast.8, bf16[1,128]{1,0:T(2,128)(2,1)S(1)} %copy-done.2, s32[1,128]{1,0:T(1,128)S(1)} %copy-done.3), custom_call_target="tpu_custom_call" | custom-call | tf_op jit(solution)/shard_map/prepare/pallas_call | solution.py:44
  4.7 5.2 %all-to-all-start = ((bf16[8,4,64,128]{3,2,1,0:T(8,128)(2,1)}), bf16[8,4,64,128]{3,2,1,0:T(8,128)(2,1)S(1)}, u32[]{:S(2)}, u32[]{:S(2)}) async-start(bf16[8,4,64,128]{3,2,1,0:T(8,128)(2,1)} %get-tuple-element.9), calls=%async_computation | async-start | bytes 1048576 | tf_op jit(solution)/shard_map/all_to_all | solution.py:244
  9.9 2.6 %collective-permute-start.2 = (bf16[528,128]{1,0:T(8,128)(2,1)S(1)}, bf16[528,128]{1,0:T(8,128)(2,1)S(1)}, u32[]{:S(2)}, u32[]{:S(2)}) collective-permute-start(bf16[528,128]{1,0:T(8,128)(2,1)S(1)} %get-tuple-element.10.refs_0_), channel_id=1, source_target_pairs={{0,2},{2,0},{1,3},{3,1},{4,6},{6,4},{5,7},{7,5},{8,10},{10,8},{9,1... | collective-permute-start | bytes 405512 | tf_op jit(solution)/shard_map/ppermute | solution.py:239
  12.5 0.7 %collective-permute-start.1 = (bf16[528,128]{1,0:T(8,128)(2,1)S(1)}, bf16[528,128]{1,0:T(8,128)(2,1)S(1)}, u32[]{:S(2)}, u32[]{:S(2)}) collective-permute-start(bf16[528,128]{1,0:T(8,128)(2,1)S(1)} %get-tuple-element.10.refs_0_), channel_id=1, source_target_pairs={{1,2},{2,1},{5,6},{6,5},{9,10},{10,9},{13,14},{14,13},{17,18},{18,... | collective-permute-start | bytes 405512 | tf_op jit(solution)/shard_map/ppermute | solution.py:239
  13.1 2.9 %collective-permute-start = (bf16[528,128]{1,0:T(8,128)(2,1)S(1)}, bf16[528,128]{1,0:T(8,128)(2,1)S(1)}, u32[]{:S(2)}, u32[]{:S(2)}) collective-permute-start(bf16[528,128]{1,0:T(8,128)(2,1)S(1)} %get-tuple-element.10.refs_0_), channel_id=1, source_target_pairs={{0,1},{1,0},{2,3},{3,2},{4,5},{5,4},{6,7},{7,6},{8,9},{9,8},{10,11... | collective-permute-start | bytes 405512 | tf_op jit(solution)/shard_map/ppermute | solution.py:239
  16.0 4.1 %collective-permute-done.2.refs_3_ = bf16[528,128]{1,0:T(8,128)(2,1)S(1)} collective-permute-done((bf16[528,128]{1,0:T(8,128)(2,1)S(1)}, bf16[528,128]{1,0:T(8,128)(2,1)S(1)}, u32[]{:S(2)}, u32[]{:S(2)}) %collective-permute-start.2) | collective-permute-done | bytes 135200 | tf_op jit(solution)/shard_map/ppermute | solution.py:239
  20.1 0.0 collective-permute-done.1.refs_2_
  20.1 1.7 %collective-permute-done.refs_1_ = bf16[528,128]{1,0:T(8,128)(2,1)S(1)} collective-permute-done((bf16[528,128]{1,0:T(8,128)(2,1)S(1)}, bf16[528,128]{1,0:T(8,128)(2,1)S(1)}, u32[]{:S(2)}, u32[]{:S(2)}) %collective-permute-start) | collective-permute-done | bytes 135200 | tf_op jit(solution)/shard_map/ppermute | solution.py:239
  21.8 6.8 %weights.1 = (bf16[4,528,512]{2,1,0:T(8,128)(2,1)S(1)}, f32[4,8,128]{2,1,0:T(8,128)S(1)}) custom-call(bf16[528,128]{1,0:T(8,128)(2,1)S(1)} %get-tuple-element.10.refs_0_, bf16[528,128]{1,0:T(8,128)(2,1)S(1)} %collective-permute-done.refs_1_, bf16[528,128]{1,0:T(8,128)(2,1)S(1)} %collective-permute-done.1.refs_2_, ...), custom_call_target="tpu_custom_call" | custom-call | flops 3221225472 | bytes 2097152 | tf_op jit(solution)/shard_map/weights/pallas_call | solution.py:177
  28.6 0.0 all-to-all-done.sorted_ref
  28.6 1.8 %analyse.1 = bf16[2048,128]{1,0:T(8,128)(2,1)} custom-call(bf16[8,4,64,128]{3,2,1,0:T(8,128)(2,1)S(1)} %all-to-all-done.sorted_ref, bf16[4,528,512]{2,1,0:T(8,128)(2,1)S(1)} %get-tuple-element.11.mix_ref, f32[4,8,128]{2,1,0:T(8,128)S(1)} %get-tuple-element.12.diag_ref), custom_call_target="tpu_custom_call" | custom-call | tf_op jit(solution)/shard_map/analyse/pallas_call | solution.py:213
Async XLA Ops:
  0.0 1.0 %copy-start = (bf16[64,4,1024]{2,1,0:T(4,128)(2,1)S(1)}, bf16[64,4,1024]{2,1,0:T(4,128)(2,1)}, u32[]{:S(2)}) copy-start(bf16[64,4,1024]{2,1,0:T(4,128)(2,1)} %param.4) | copy-start | bytes 1572868
  1.0 0.9 %copy-start.1 = (bf16[512,1,128]{2,0,1:T(8,128)(2,1)S(1)}, bf16[512,1,128]{2,0,1:T(8,128)(2,1)}, u32[]{:S(2)}) copy-start(bf16[512,1,128]{2,0,1:T(8,128)(2,1)} %param.5) | copy-start | bytes 393220
  1.9 0.7 %copy-start.2 = (bf16[1,128]{1,0:T(2,128)(2,1)S(1)}, bf16[1,128]{1,0:T(2,128)(2,1)}, u32[]{:S(2)}) copy-start(bf16[1,128]{1,0:T(2,128)(2,1)} %misfit_ref.1) | copy-start | bytes 772
  2.6 0.7 %copy-start.3 = (s32[1,128]{1,0:T(1,128)S(1)}, s32[1,128]{1,0:T(1,128)}, u32[]{:S(2)}) copy-start(s32[1,128]{1,0:T(1,128)} %line_ref.1) | copy-start | bytes 1540
  4.7 23.8 %all-to-all-start = ((bf16[8,4,64,128]{3,2,1,0:T(8,128)(2,1)}), bf16[8,4,64,128]{3,2,1,0:T(8,128)(2,1)S(1)}, u32[]{:S(2)}, u32[]{:S(2)}) async-start(bf16[8,4,64,128]{3,2,1,0:T(8,128)(2,1)} %get-tuple-element.9), calls=%async_computation | async-start | bytes 1048576 | tf_op jit(solution)/shard_map/all_to_all | solution.py:244
  9.9 10.2 %collective-permute-start.2 = (bf16[528,128]{1,0:T(8,128)(2,1)S(1)}, bf16[528,128]{1,0:T(8,128)(2,1)S(1)}, u32[]{:S(2)}, u32[]{:S(2)}) collective-permute-start(bf16[528,128]{1,0:T(8,128)(2,1)S(1)} %get-tuple-element.10.refs_0_), channel_id=1, source_target_pairs={{0,2},{2,0},{1,3},{3,1},{4,6},{6,4},{5,7},{7,5},{8,10},{10,8},{9,1... | collective-permute-start | bytes 405512 | tf_op jit(solution)/shard_map/ppermute | solution.py:239
  12.5 7.6 %collective-permute-start.1 = (bf16[528,128]{1,0:T(8,128)(2,1)S(1)}, bf16[528,128]{1,0:T(8,128)(2,1)S(1)}, u32[]{:S(2)}, u32[]{:S(2)}) collective-permute-start(bf16[528,128]{1,0:T(8,128)(2,1)S(1)} %get-tuple-element.10.refs_0_), channel_id=1, source_target_pairs={{1,2},{2,1},{5,6},{6,5},{9,10},{10,9},{13,14},{14,13},{17,18},{18,... | collective-permute-start | bytes 405512 | tf_op jit(solution)/shard_map/ppermute | solution.py:239
  13.1 8.7 %collective-permute-start = (bf16[528,128]{1,0:T(8,128)(2,1)S(1)}, bf16[528,128]{1,0:T(8,128)(2,1)S(1)}, u32[]{:S(2)}, u32[]{:S(2)}) collective-permute-start(bf16[528,128]{1,0:T(8,128)(2,1)S(1)} %get-tuple-element.10.refs_0_), channel_id=1, source_target_pairs={{0,1},{1,0},{2,3},{3,2},{4,5},{5,4},{6,7},{7,6},{8,9},{9,8},{10,11... | collective-permute-start | bytes 405512 | tf_op jit(solution)/shard_map/ppermute | solution.py:239

commit v2 on v1

--- a/solution.py
+++ b/solution.py
@@ -12,6 +12,7 @@
 MIB = 1 << 20
 
 VMEM = pl.BlockSpec(memory_space=pltpu.VMEM)
+HBM = pl.BlockSpec(memory_space=pltpu.HBM)
 
 
 def swap_pairs(size, reach, phase):
@@ -19,40 +20,80 @@
     return [pair for i in lows for pair in ((i, i + reach), (i + reach, i))]
 
 
-def prepare_kernel(parts, rows, prior_ref, spread_ref, misfit_ref, line_ref, packed_ref, sorted_ref, wide):
-    members = prior_ref.shape[0] // (parts * rows)
-    count = spread_ref.shape[0]
-    packed_ref[0:count, :] = spread_ref[...]
-    width = spread_ref.shape[1]
+def pack_kernel(spread_ref, misfit_ref, line_ref, packed_ref, misfit, line, sems):
+    count, width = spread_ref.shape
+    copies = [
+        pltpu.make_async_copy(spread_ref, packed_ref.at[0:count], sems.at[0]),
+        pltpu.make_async_copy(misfit_ref, misfit, sems.at[1]),
+        pltpu.make_async_copy(line_ref, line, sems.at[2]),
+    ]
+    for copy in copies:
+        copy.start()
+    for copy in copies[1:]:
+        copy.wait()
     which = lax.broadcasted_iota(jnp.int32, (PAD, width), 0)
-    misfit = jnp.broadcast_to(misfit_ref[...].astype(jnp.float32), (PAD, width))
-    line = jnp.broadcast_to(line_ref[...].astype(jnp.float32), (PAD, width))
-    extra = jnp.where(which == 0, misfit, jnp.where(which == 1, line, 0.0))
+    misfits = jnp.broadcast_to(misfit[...].astype(jnp.float32), (PAD, width))
+    lines = jnp.broadcast_to(line[...].astype(jnp.float32), (PAD, width))
+    extra = jnp.where(which == 0, misfits, jnp.where(which == 1, lines, 0.0))
     packed_ref[count:, :] = extra.astype(jnp.bfloat16)
-    wide[...] = prior_ref[...].astype(jnp.float32)
-    for part in range(parts):
-        for row in range(rows):
-            lines = wide[pl.ds(part * rows + row, members, stride=parts * rows), :]
-            sorted_ref[part, row] = lines.astype(jnp.bfloat16)
-
-
-def prepare(prior, spread, misfit, line, parts):
+    copies[0].wait()
+
+
+def pack(spread, misfit, line):
+    count, obs = spread.shape
+    return pl.pallas_call(
+        pack_kernel,
+        out_shape=pltpu.VMEM((count + PAD, obs), jnp.bfloat16),
+        in_specs=[HBM] * 3,
+        out_specs=VMEM,
+        scratch_shapes=[
+            pltpu.VMEM(misfit.shape, misfit.dtype),
+            pltpu.VMEM(line.shape, line.dtype),
+            pltpu.SemaphoreType.DMA((3,)),
+        ],
+        name="pack",
+    )(*[pltpu.with_memory_space_constraint(array, pltpu.HBM) for array in (spread, misfit, line)])
+
+
+def sort_kernel(parts, rows, prior_ref, sorted_ref, held, wide, sems):
+    stride = parts * rows
+    members = prior_ref.shape[0] // stride
+    step = min(members, PAD)
+    chunks = members // step
+    copies = []
+    for chunk in range(chunks):
+        span = pl.ds(chunk * step * stride, step * stride)
+        copies.append(pltpu.make_async_copy(prior_ref.at[span], held.at[span], sems.at[chunk]))
+        copies[-1].start()
+    for chunk in range(chunks):
+        span = pl.ds(chunk * step * stride, step * stride)
+        copies[chunk].wait()
+        wide[span, :] = held[span, :].astype(jnp.float32)
+        for part in range(parts):
+            for row in range(rows):
+                first = chunk * step * stride + part * rows + row
+                lines = wide[pl.ds(first, step, stride=stride), :]
+                sorted_ref[part, row, pl.ds(chunk * step, step), :] = lines.astype(jnp.bfloat16)
+
+
+def sort(prior, parts):
     members, rows, cells = prior.shape
     width = cells // parts
-    count, obs = spread.shape
     flat = prior.reshape(members, rows, parts, width).transpose(0, 2, 1, 3).reshape(-1, width)
     return pl.pallas_call(
-        functools.partial(prepare_kernel, parts, rows),
-        out_shape=(
-            jax.ShapeDtypeStruct((count + PAD, obs), jnp.bfloat16),
-            jax.ShapeDtypeStruct((parts, rows, members, width), jnp.bfloat16),
-        ),
-        in_specs=[VMEM] * 4,
-        out_specs=(VMEM, VMEM),
-        scratch_shapes=[pltpu.VMEM(flat.shape, jnp.float32)],
+        functools.partial(sort_kernel, parts, rows),
+        out_shape=jax.ShapeDtypeStruct((parts, rows, members, width), jnp.bfloat16),
+        in_specs=[HBM],
+        out_specs=VMEM,
+        scratch_shapes=[
+            pltpu.VMEM(flat.shape, jnp.bfloat16),
+            pltpu.VMEM(flat.shape, jnp.float32),
+            pltpu.SemaphoreType.DMA((members // min(members, PAD),)),
+        ],
         compiler_params=pltpu.CompilerParams(vmem_limit_bytes=24 * MIB),
-        name="prepare",
-    )(flat, spread, misfit, line)
+        cost_estimate=pl.CostEstimate(flops=0, bytes_accessed=4 * MIB, transcendentals=0),
+        name="sort",
+    )(pltpu.with_memory_space_constraint(flat, pltpu.HBM))
 
 
 def select_flag(condition):
@@ -185,7 +226,7 @@
         scratch_shapes=[pltpu.VMEM((own.shape[0], 5 * own.shape[1]), jnp.bfloat16)],
         compiler_params=pltpu.CompilerParams(vmem_limit_bytes=48 * MIB),
         cost_estimate=pl.CostEstimate(
-            flops=24 * cube, bytes_accessed=8 * count * count, transcendentals=0
+            flops=240 * cube, bytes_accessed=8 * count * count, transcendentals=0
         ),
         name="weights",
     )(*blocks)
@@ -227,13 +268,12 @@
     size = lax.axis_size("gy")
     count = measured_spread.shape[0]
     rows = prior_fields.shape[1]
-    packed, to_send = prepare(
-        prior_fields,
+    packed = pack(
         measured_spread.reshape(count, -1),
         scaled_misfit.reshape(1, -1),
         sensor_line_inside.reshape(1, -1),
-        parts,
-    )
+    )
+    to_send = sort(prior_fields, parts)
 
     def trade(pairs):
         return lax.ppermute(packed, "gy", pairs) if pairs else None

time: 30.6 us -> 26.5 us (0.87)
  local copies, waits for them, and re-layouts: 3.25 us -> 0 us
  waiting for transfers between devices: 5.76 us -> 2.97 us
  Pallas kernels: 10 us -> 11.9 us
    unnamed x8 -> x0, local copies, waits for them, and re-layouts: 3.25 us -> none
    ppermute x3, waiting for transfers between devices: 5.76 us -> 2.85 us  [trade(): return lax.ppermute(packed, 'gy', pairs) if pairs else None]
    pallas_call x1 -> x2, Pallas kernels: 1.45 us -> 3.33 us  [the longest x1 2.4 us: sort(): pl.pallas_call(functools.partial(sort_kernel, parts, rows), out_shape=jax...]
    ppermute x3, starting transfers between devices: 6.14 us -> 7.65 us  [trade(): return lax.ppermute(packed, 'gy', pairs) if pairs else None]
    all_to_all x1, starting transfers between devices: 5.17 us -> 3.74 us  [on_device(): lax.all_to_all(to_send, 'gx', split_axis=0, concat_axis=0, tiled=True)]
  transfers between devices with their start and end apart: 4 -> 4, of which waited for: 2 -> 2; matrix products, arithmetic and copies ran while one was open for 0% -> 0% of each run, Pallas kernels for 22% -> 35%
where the time goes in v2:
time: 26.5 us; the launch traced here: 26.3 us
  Pallas kernels  11.9 us (45%)
  starting transfers between devices  11.4 us (43%)
  waiting for transfers between devices  2.97 us (11%)
    ppermute x3, starting transfers between devices, trade(): return lax.ppermute(packed, 'gy', pairs) if pairs else None  7.65 us
    pallas_call x1, Pallas kernels, weights(): pl.pallas_call(functools.partial(weights_kernel, size, rows, rows // CP,...  6.76 us
    all_to_all x1, starting transfers between devices, on_device(): lax.all_to_all(to_send, 'gx', split_axis=0, concat_axis=0, tiled=True)  3.74 us
    ppermute x3, waiting for transfers between devices, trade(): return lax.ppermute(packed, 'gy', pairs) if pairs else None  2.85 us
    pallas_call x1, Pallas kernels, sort(): pl.pallas_call(functools.partial(sort_kernel, parts, rows), out_shape=jax...  2.4 us
    pallas_call x1, Pallas kernels, analyse(): pl.pallas_call(functools.partial(analyse_kernel, rows), out_shape=jax.Sha...  1.81 us
    pallas_call x1, Pallas kernels, pack(): pl.pallas_call(pack_kernel, out_shape=pltpu.VMEM((count + PAD, obs), jnp....  0.93 us
  transfers between devices with their start and end apart: 4, of which 2 were waited for; matrix products, arithmetic and copies ran while one was open for 0% of the time, Pallas kernels for 35%

profile of v2, /device:TPU:0, one launch (start us, length us, event | category | flops | bytes accessed | tf_op | source)
XLA Modules:
  0.0 26.3 jit_solution(1615644216449782734)
XLA Ops:
  0.0 0.9 %pack.1.refs_0_ = bf16[528,128]{1,0:T(8,128)(2,1)S(1)} custom-call(bf16[512,128]{1,0:T(8,128)(2,1)} %bitcast.8, bf16[1,128]{1,0:T(2,128)(2,1)} %misfit_ref.1, s32[1,128]{1,0:T(1,128)} %line_ref.1), custom_call_target="tpu_custom_call" | custom-call | tf_op jit(solution)/shard_map/pack/pallas_call | solution.py:44
  0.9 3.1 %collective-permute-start = (bf16[528,128]{1,0:T(8,128)(2,1)S(1)}, bf16[528,128]{1,0:T(8,128)(2,1)S(1)}, u32[]{:S(2)}, u32[]{:S(2)}) collective-permute-start(bf16[528,128]{1,0:T(8,128)(2,1)S(1)} %pack.1.refs_0_), channel_id=1, source_target_pairs={{0,1},{1,0},{2,3},{3,2},{4,5},{5,4},{6,7},{7,6},{8,9},{9,8},{10,11... | collective-permute-start | bytes 405512 | tf_op jit(solution)/shard_map/ppermute | solution.py:279
  4.0 0.7 %collective-permute-start.1 = (bf16[528,128]{1,0:T(8,128)(2,1)S(1)}, bf16[528,128]{1,0:T(8,128)(2,1)S(1)}, u32[]{:S(2)}, u32[]{:S(2)}) collective-permute-start(bf16[528,128]{1,0:T(8,128)(2,1)S(1)} %pack.1.refs_0_), channel_id=1, source_target_pairs={{1,2},{2,1},{5,6},{6,5},{9,10},{10,9},{13,14},{14,13},{17,18},{18,... | collective-permute-start | bytes 405512 | tf_op jit(solution)/shard_map/ppermute | solution.py:279
  4.7 3.9 %collective-permute-start.2 = (bf16[528,128]{1,0:T(8,128)(2,1)S(1)}, bf16[528,128]{1,0:T(8,128)(2,1)S(1)}, u32[]{:S(2)}, u32[]{:S(2)}) collective-permute-start(bf16[528,128]{1,0:T(8,128)(2,1)S(1)} %pack.1.refs_0_), channel_id=1, source_target_pairs={{0,2},{2,0},{1,3},{3,1},{4,6},{6,4},{5,7},{7,5},{8,10},{10,8},{9,1... | collective-permute-start | bytes 405512 | tf_op jit(solution)/shard_map/ppermute | solution.py:279
  8.6 2.4 %sort.1 = bf16[8,4,64,128]{3,2,1,0:T(8,128)(2,1)} custom-call(bf16[2048,128]{1,0:T(8,128)(2,1)} %bitcast.7), custom_call_target="tpu_custom_call" | custom-call | bytes 4194304 | tf_op jit(solution)/shard_map/sort/pallas_call | solution.py:83
  11.0 3.7 %all-to-all-start = ((bf16[8,4,64,128]{3,2,1,0:T(8,128)(2,1)}), bf16[8,4,64,128]{3,2,1,0:T(8,128)(2,1)S(1)}, u32[]{:S(2)}, u32[]{:S(2)}) async-start(bf16[8,4,64,128]{3,2,1,0:T(8,128)(2,1)} %sort.1), calls=%async_computation | async-start | bytes 1048576 | tf_op jit(solution)/shard_map/all_to_all | solution.py:284
  14.7 0.0 collective-permute-done.refs_1_
  14.7 0.0 collective-permute-done.1.refs_2_
  14.8 2.8 %collective-permute-done.2.refs_3_ = bf16[528,128]{1,0:T(8,128)(2,1)S(1)} collective-permute-done((bf16[528,128]{1,0:T(8,128)(2,1)S(1)}, bf16[528,128]{1,0:T(8,128)(2,1)S(1)}, u32[]{:S(2)}, u32[]{:S(2)}) %collective-permute-start.2) | collective-permute-done | bytes 135200 | tf_op jit(solution)/shard_map/ppermute | solution.py:279
  17.6 6.8 %weights.1 = (bf16[4,528,512]{2,1,0:T(8,128)(2,1)S(1)}, f32[4,8,128]{2,1,0:T(8,128)S(1)}) custom-call(bf16[528,128]{1,0:T(8,128)(2,1)S(1)} %pack.1.refs_0_, bf16[528,128]{1,0:T(8,128)(2,1)S(1)} %collective-permute-done.refs_1_, bf16[528,128]{1,0:T(8,128)(2,1)S(1)} %collective-permute-done.1.refs_2_, bf16[528,128]{1,0:T(8,128)(2,1)S(1)} %collective-permute-done.2.refs_3_), custom_call_target="tpu_custom_call" | custom-call | flops 32212254720 | bytes 2097152 | tf_op jit(solution)/shard_map/weights/pallas_call | solution.py:218
  24.4 0.1 all-to-all-done.sorted_ref
  24.5 1.8 %analyse.1 = bf16[2048,128]{1,0:T(8,128)(2,1)} custom-call(bf16[8,4,64,128]{3,2,1,0:T(8,128)(2,1)S(1)} %all-to-all-done.sorted_ref, bf16[4,528,512]{2,1,0:T(8,128)(2,1)S(1)} %get-tuple-element.7.mix_ref, f32[4,8,128]{2,1,0:T(8,128)S(1)} %get-tuple-element.8.diag_ref), custom_call_target="tpu_custom_call" | custom-call | tf_op jit(solution)/shard_map/analyse/pallas_call | solution.py:254
Async XLA Ops:
  0.9 13.8 %collective-permute-start = (bf16[528,128]{1,0:T(8,128)(2,1)S(1)}, bf16[528,128]{1,0:T(8,128)(2,1)S(1)}, u32[]{:S(2)}, u32[]{:S(2)}) collective-permute-start(bf16[528,128]{1,0:T(8,128)(2,1)S(1)} %pack.1.refs_0_), channel_id=1, source_target_pairs={{0,1},{1,0},{2,3},{3,2},{4,5},{5,4},{6,7},{7,6},{8,9},{9,8},{10,11... | collective-permute-start | bytes 405512 | tf_op jit(solution)/shard_map/ppermute | solution.py:279
  4.0 10.7 %collective-permute-start.1 = (bf16[528,128]{1,0:T(8,128)(2,1)S(1)}, bf16[528,128]{1,0:T(8,128)(2,1)S(1)}, u32[]{:S(2)}, u32[]{:S(2)}) collective-permute-start(bf16[528,128]{1,0:T(8,128)(2,1)S(1)} %pack.1.refs_0_), channel_id=1, source_target_pairs={{1,2},{2,1},{5,6},{6,5},{9,10},{10,9},{13,14},{14,13},{17,18},{18,... | collective-permute-start | bytes 405512 | tf_op jit(solution)/shard_map/ppermute | solution.py:279
  4.7 12.9 %collective-permute-start.2 = (bf16[528,128]{1,0:T(8,128)(2,1)S(1)}, bf16[528,128]{1,0:T(8,128)(2,1)S(1)}, u32[]{:S(2)}, u32[]{:S(2)}) collective-permute-start(bf16[528,128]{1,0:T(8,128)(2,1)S(1)} %pack.1.refs_0_), channel_id=1, source_target_pairs={{0,2},{2,0},{1,3},{3,1},{4,6},{6,4},{5,7},{7,5},{8,10},{10,8},{9,1... | collective-permute-start | bytes 405512 | tf_op jit(solution)/shard_map/ppermute | solution.py:279
  11.0 13.5 %all-to-all-start = ((bf16[8,4,64,128]{3,2,1,0:T(8,128)(2,1)}), bf16[8,4,64,128]{3,2,1,0:T(8,128)(2,1)S(1)}, u32[]{:S(2)}, u32[]{:S(2)}) async-start(bf16[8,4,64,128]{3,2,1,0:T(8,128)(2,1)} %sort.1), calls=%async_computation | async-start | bytes 1048576 | tf_op jit(solution)/shard_map/all_to_all | solution.py:284

commit v3 on v2

v3 whole, which is shorter than its diff:
```python
import functools

import jax
import jax.numpy as jnp
from jax import lax
from jax.experimental import pallas as pl
from jax.experimental.pallas import tpu as pltpu
from jax.sharding import PartitionSpec as P

CP = 2
PAD = 16
MIB = 1 << 20
NEAR_FLOPS = 180
FAR_FLOPS = 2

VMEM = pl.BlockSpec(memory_space=pltpu.VMEM)
HBM = pl.BlockSpec(memory_space=pltpu.HBM)


def swap_pairs(size, reach, phase):
    lows = [i for i in range(size - reach) if (i // reach) % 2 == phase]
    return [pair for i in lows for pair in ((i, i + reach), (i + reach, i))]


def target_chip(chip, step, chips):
    if chips & (chips - 1) == 0:
        return chip ^ step
    return (chip + step) % chips if isinstance(chip, int) else lax.rem(chip + step, chips)


def source_chip(chip, step, chips):
    return target_chip(chip, step if chips & (chips - 1) == 0 else chips - step, chips)


def split_kernel(chips, prior_ref, spread_ref, misfit_ref, line_ref, *refs):
    packed_ref, keep_ref, give_ref, misfit, line, sems = refs
    count, width = spread_ref.shape
    copies = [
        pltpu.make_async_copy(spread_ref, packed_ref.at[0:count], sems.at[0]),
        pltpu.make_async_copy(misfit_ref, misfit, sems.at[1]),
        pltpu.make_async_copy(line_ref, line, sems.at[2]),
    ]
    core = lax.rem(lax.axis_index("gx"), 2)
    cells = prior_ref.shape[2] // (2 * chips)
    for chip in range(chips):
        for place, (side, ref) in enumerate(((core, keep_ref), (1 - core, give_ref))):
            first = pl.multiple_of((2 * chip + side) * cells, cells)
            copies.append(
                pltpu.make_async_copy(
                    prior_ref.at[:, :, pl.ds(first, cells)],
                    ref.at[chip],
                    sems.at[3 + 2 * chip + place],
                )
            )
    for copy in copies:
        copy.start()
    for copy in copies[1:3]:
        copy.wait()
    which = lax.broadcasted_iota(jnp.int32, (PAD, width), 0)
    misfits = jnp.broadcast_to(misfit[...].astype(jnp.float32), (PAD, width))
    lines = jnp.broadcast_to(line[...].astype(jnp.float32), (PAD, width))
    extra = jnp.where(which == 0, misfits, jnp.where(which == 1, lines, 0.0))
    packed_ref[count:, :] = extra.astype(jnp.bfloat16)
    copies[0].wait()
    for copy in copies[3:]:
        copy.wait()


def split(prior, spread, misfit, line, chips):
    members, rows, cells = prior.shape
    count, obs = spread.shape
    half = (chips, members, rows, cells // (2 * chips))
    inputs = (prior, spread, misfit, line)
    return pl.pallas_call(
        functools.partial(split_kernel, chips),
        out_shape=(
            pltpu.VMEM((count + PAD, obs), jnp.bfloat16),
            pltpu.VMEM(half, jnp.bfloat16),
            pltpu.VMEM(half, jnp.bfloat16),
        ),
        in_specs=[HBM] * 4,
        out_specs=(VMEM,) * 3,
        scratch_shapes=[
            pltpu.VMEM(misfit.shape, misfit.dtype),
            pltpu.VMEM(line.shape, line.dtype),
            pltpu.SemaphoreType.DMA((3 + 2 * chips,)),
        ],
        name="split",
    )(*[pltpu.with_memory_space_constraint(array, pltpu.HBM) for array in inputs])


def sort_kernel(chips, rows, keep_ref, got_ref, *refs):
    sorted_refs, wide = refs[:chips], refs[chips]
    members = keep_ref.shape[0] // (chips * rows)
    index = lax.axis_index("gx")
    core = lax.rem(index, 2)
    chip = index // 2
    for half, ref in enumerate((keep_ref, got_ref)):
        wide[half] = ref[...].astype(jnp.float32)
    for step in range(chips):
        first = target_chip(chip, step, chips) * (members * rows)
        for half, side in enumerate((core, 1 - core)):
            for row in range(rows):
                lines = wide[half, pl.ds(first + row, members, stride=rows), :]
                sorted_refs[step][side, row] = lines.astype(jnp.bfloat16)


def sort(keep, got):
    chips, members, rows, cells = keep.shape
    flat = (chips * members * rows, cells)
    return pl.pallas_call(
        functools.partial(sort_kernel, chips, rows),
        out_shape=[pltpu.VMEM((2, rows, members, cells), jnp.bfloat16)] * chips,
        in_specs=[VMEM] * 2,
        out_specs=[VMEM] * chips,
        scratch_shapes=[pltpu.VMEM((2,) + flat, jnp.float32)],
        compiler_params=pltpu.CompilerParams(vmem_limit_bytes=16 * MIB),
        cost_estimate=pl.CostEstimate(flops=0, bytes_accessed=4 * MIB, transcendentals=0),
        name="sort",
    )(keep.reshape(flat), got.reshape(flat))


def select_flag(condition):
    return jnp.where(condition, jnp.float32(1.0), jnp.float32(0.0))


def point_weights(left, count, radius, centre, bases, present):
    line = left[count + 1 : count + 2, :].astype(jnp.float32)
    obs = line.shape[1] // 3
    where = lax.broadcasted_iota(jnp.int32, line.shape, 1) // obs
    base = jnp.where(where == 0, bases[0], jnp.where(where == 1, bases[1], bases[2]))
    alive = jnp.where(where == 0, present[0], jnp.where(where == 1, present[1], present[2]))
    distance = (base + line + 0.5 - centre) / radius
    locality = jnp.exp(-0.5 * distance * distance) * alive
    scaled = (left[0:count, :].astype(jnp.float32) * locality).astype(jnp.bfloat16)
    both = lax.dot_general(
        left[...], scaled, (((1,), (1,)), ((), ())), preferred_element_type=jnp.float32
    )
    gram = both[0:count]
    drive = both[count : count + 1]
    share = 1.0 / (count - 1.0)
    on_diagonal = lax.broadcasted_iota(jnp.int32, gram.shape, 0) == lax.broadcasted_iota(
        jnp.int32, gram.shape, 1
    )
    sizes = jnp.abs(jnp.where(on_diagonal, 1.0, 0.0) + gram * share)
    bound = jnp.max(jnp.sum(sizes, axis=0, keepdims=True), axis=1, keepdims=True)
    rounded = gram.astype(jnp.bfloat16)
    square = jnp.dot(rounded, rounded, preferred_element_type=jnp.float32)
    s = 1.0 / bound
    g = s * share
    first = jnp.broadcast_to(g, (1, count))
    second = jnp.broadcast_to(g * g, (1, count))
    beta = s * s - 9.0 * s
    quad = second * square
    x = (2.0 * s) * first * gram + quad
    w = (2.0 * s - 9.0) * first * gram + quad
    product = jnp.dot(x.astype(jnp.bfloat16), w.astype(jnp.bfloat16), preferred_element_type=jnp.float32)
    on_gram = (-39.0 + (27.0 + beta) * (2.0 * s) + s * s * (2.0 * s - 9.0)) * first / 16.0
    on_square = (27.0 + beta + s * s) * second / 16.0
    rest = on_gram * gram + on_square * square + product * (1.0 / 16.0)
    scalar_part = (36.0 + s * (-39.0 + s * (27.0 + s * (-9.0 + s)))) / 16.0
    rest_rounded = rest.astype(jnp.bfloat16)

    def row_times(row):
        out = jnp.dot(two_rows(row), rest_rounded, preferred_element_type=jnp.float32)
        return out[0:1] + out[1:2] + scalar_part * row

    mean_weights = row_times(row_times(drive)) * g
    root = lax.rsqrt(bound)
    return rest * jnp.broadcast_to(root, (1, count)), scalar_part * root, mean_weights


def two_rows(row):
    high = row.astype(jnp.bfloat16).astype(jnp.float32)
    which = lax.broadcasted_iota(jnp.int32, (PAD, row.shape[1]), 0)
    return jnp.where(which == 0, high, jnp.where(which == 1, row - high, 0.0)).astype(jnp.bfloat16)


class Place:
    def __init__(self, size, rows):
        self.size, self.rows = size, rows
        self.spacing = rows // CP
        self.edge = self.spacing // 2
        self.tile = lax.axis_index("gy")
        self.upward = lax.rem(self.tile // 2, 2) == 0
        self.even = lax.rem(self.tile, 2) == 0
        self.sign = jnp.where(self.upward, 1, -1)

    def present(self, offset):
        there = (self.tile + offset >= 0) & (self.tile + offset < self.size)
        return select_flag(there)

    def share(self, row, point):
        start = (self.tile * self.rows).astype(jnp.float32)
        height = float(self.rows * self.size)
        place = jnp.clip(start + row + 0.5, 0.5 * self.spacing, height - 0.5 * self.spacing)
        centre = start + (point + 0.5) * self.spacing
        return jnp.maximum(0.0, 1.0 - jnp.abs(place - centre) / self.spacing)

    def edge_row(self, ahead, step):
        first, last = step, self.rows - 1 - step
        return jnp.where(self.upward == ahead, last, first)

    def side_point(self, ahead):
        return jnp.where(self.upward == ahead, jnp.float32(CP), jnp.float32(-1))

    def own_point(self, ahead):
        return jnp.where(self.upward == ahead, jnp.float32(CP - 1), jnp.float32(0))

    def side(self, left, count, ahead):
        sign = self.sign if ahead else -self.sign
        offsets = (sign, 2 * sign, 0 * sign)
        bases = [(offset * self.rows).astype(jnp.float32) for offset in offsets]
        present = [self.present(offset) for offset in offsets]
        centre = (self.side_point(ahead) + 0.5) * self.spacing
        return point_weights(left, count, float(self.rows), centre, bases, present)


def write_mix(mix_ref, diag_ref, row, terms, count):
    mix_ref[row, 0:count, :] = sum(share * part[0] for share, part in terms).astype(jnp.bfloat16)
    mix_ref[row, count:, :] = two_rows(sum(share * part[2] for share, part in terms))
    diag_ref[row] = jnp.broadcast_to(sum(share * part[1] for share, part in terms), (8, 128))


def near_kernel(size, rows, has_far, *refs):
    own_ref, first_ref, other_ref = refs[:3]
    mix_ref, diag_ref, beside_ref, small_ref, left = refs[4 if has_far else 3 :]
    count, obs = own_ref.shape[0] - PAD, own_ref.shape[1]
    at = Place(size, rows)
    ahead_is_first = at.even == at.upward
    left[:, 0:obs] = jnp.where(ahead_is_first, first_ref[...], other_ref[...])
    left[:, obs : 2 * obs] = own_ref[...]
    left[:, 2 * obs : 3 * obs] = jnp.where(ahead_is_first, other_ref[...], first_ref[...])
    far = refs[3][...] if has_far else jnp.zeros(own_ref.shape, jnp.bfloat16)
    left[:, 3 * obs : 4 * obs] = far
    left[:, 4 * obs :] = own_ref[...]
    offsets = (at.sign, 0 * at.sign, -at.sign)
    bases = [(offset * rows).astype(jnp.float32) for offset in offsets]
    present = [at.present(offset) for offset in offsets]
    own = []
    for point in range(CP):
        centre = (point + 0.5) * at.spacing
        own.append(
            point_weights(left.at[:, 0 : 3 * obs], count, float(rows), centre, bases, present)
        )
    behind = at.side(left.at[:, 2 * obs :], count, False)
    for row in range(at.edge, rows - at.edge):
        low = int((row + 0.5) / at.spacing - 0.5)
        terms = [(at.share(row, low + step), own[low + step]) for step in (0, 1)]
        write_mix(mix_ref, diag_ref, row, terms, count)

    def pick(ahead):
        flag = at.upward == ahead
        return [jnp.where(flag, last, first) for first, last in zip(own[0], own[CP - 1])]

    for step in range(at.edge):
        row = at.edge_row(False, step)
        terms = [
            (at.share(row, at.own_point(False)), pick(False)),
            (at.share(row, at.side_point(False)), behind),
        ]
        write_mix(mix_ref, diag_ref, row, terms, count)
    beside = pick(True)
    beside_ref[...] = beside[0]
    small_ref[0:8, :] = jnp.broadcast_to(beside[1], (8, count))
    small_ref[8:16, :] = jnp.broadcast_to(beside[2], (8, count))


def far_kernel(size, rows, own_ref, first_ref, other_ref, far_ref, beside_ref, small_ref, *refs):
    mix_ref, diag_ref, left = refs
    count, obs = own_ref.shape[0] - PAD, own_ref.shape[1]
    at = Place(size, rows)
    left[:, 0:obs] = jnp.where(at.even == at.upward, first_ref[...], other_ref[...])
    left[:, obs : 2 * obs] = far_ref[...]
    left[:, 2 * obs :] = own_ref[...]
    ahead = at.side(left, count, True)
    beside = (beside_ref[...], small_ref[0:1, 0:1], small_ref[8:9, :])
    for step in range(at.edge):
        row = at.edge_row(True, step)
        terms = [
            (at.share(row, at.own_point(True)), beside),
            (at.share(row, at.side_point(True)), ahead),
        ]
        write_mix(mix_ref, diag_ref, step, terms, count)


def weights(own, first, other, far, beyond, size, rows):
    count, obs = own.shape[0] - PAD, own.shape[1]
    edge = rows // CP // 2
    near_inputs = [own, first, other] + ([] if beyond is None else [beyond])
    mix, diag, beside, small = pl.pallas_call(
        functools.partial(near_kernel, size, rows, beyond is not None),
        out_shape=(
            pltpu.VMEM((rows, count + PAD, count), jnp.bfloat16),
            pltpu.VMEM((rows, 8, 128), jnp.float32),
            pltpu.VMEM((count, count), jnp.float32),
            pltpu.VMEM((16, count), jnp.float32),
        ),
        in_specs=[VMEM] * len(near_inputs),
        out_specs=(VMEM,) * 4,
        scratch_shapes=[pltpu.VMEM((count + PAD, 5 * obs), jnp.bfloat16)],
        compiler_params=pltpu.CompilerParams(vmem_limit_bytes=40 * MIB),
        cost_estimate=pl.CostEstimate(
            flops=NEAR_FLOPS * count**3, bytes_accessed=8 * count * count, transcendentals=0
        ),
        name="near",
    )(*near_inputs)
    edge_mix, edge_diag = pl.pallas_call(
        functools.partial(far_kernel, size, rows),
        out_shape=(
            pltpu.VMEM((edge, count + PAD, count), jnp.bfloat16),
            pltpu.VMEM((edge, 8, 128), jnp.float32),
        ),
        in_specs=[VMEM] * 6,
        out_specs=(VMEM,) * 2,
        scratch_shapes=[pltpu.VMEM((count + PAD, 3 * obs), jnp.bfloat16)],
        compiler_params=pltpu.CompilerParams(vmem_limit_bytes=32 * MIB),
        cost_estimate=pl.CostEstimate(
            flops=FAR_FLOPS * count**3, bytes_accessed=8 * count * count, transcendentals=0
        ),
        name="far",
    )(own, first, other, far, beside, small)
    return mix, diag, edge_mix, edge_diag


def analyse_kernel(size, *refs):
    mix_ref, diag_ref, edge_mix_ref, edge_diag_ref = refs[:4]
    block_refs = refs[4:-3]
    out_ref, deviations, wide = refs[-3:]
    chips = len(block_refs)
    _, rows, members, width = block_refs[0].shape
    count = 2 * chips * members
    at = Place(size, rows)
    chip = lax.axis_index("gx") // 2

    def one_row(row, mix, diag):
        halves = [(step, side) for step in range(chips) for side in range(2)]
        blocks = [block_refs[step][side, row].astype(jnp.float32) for step, side in halves]
        total = sum(jnp.sum(block, axis=0, keepdims=True) for block in blocks)
        mean = total / count
        for (step, side), block in zip(halves, blocks):
            first = (2 * source_chip(chip, step, chips) + side) * members
            deviations[pl.ds(pl.multiple_of(first, members), members), :] = (block - mean).astype(
                jnp.bfloat16
            )
        deviation = deviations[...]
        term = jnp.dot(mix, deviation, preferred_element_type=jnp.float32)
        shift = mean + term[count : count + 1] + term[count + 1 : count + 2]
        wide[pl.ds(row, count, stride=rows), :] = (
            term[0:count] + diag * deviation.astype(jnp.float32) + shift
        )

    for row in range(at.edge, rows - at.edge):
        one_row(row, mix_ref[row], diag_ref[row, 0:1, 0:width])
    for step in range(at.edge):
        row = at.edge_row(False, step)
        one_row(row, mix_ref[row], diag_ref[row, 0:1, 0:width])
    for step in range(at.edge):
        row = at.edge_row(True, step)
        one_row(row, edge_mix_ref[step], edge_diag_ref[step, 0:1, 0:width])
    out_ref[...] = wide[...].astype(jnp.bfloat16)


def analyse(blocks, mixes, size):
    _, rows, members, width = blocks[0].shape
    count = 2 * len(blocks) * members
    flat = pl.pallas_call(
        functools.partial(analyse_kernel, size),
        out_shape=jax.ShapeDtypeStruct((count * rows, width), jnp.bfloat16),
        in_specs=[VMEM] * (4 + len(blocks)),
        out_specs=VMEM,
        scratch_shapes=[
            pltpu.VMEM((count, width), jnp.bfloat16),
            pltpu.VMEM((count * rows, width), jnp.float32),
        ],
        compiler_params=pltpu.CompilerParams(vmem_limit_bytes=24 * MIB),
        name="analyse",
    )(*mixes, *blocks)
    return flat.reshape(count, rows, width)


def on_device(prior_fields, measured_spread, scaled_misfit, sensor_line_inside):
    parts = lax.axis_size("gx")
    chips = parts // 2
    size = lax.axis_size("gy")
    count = measured_spread.shape[0]
    rows = prior_fields.shape[1]
    packed, keep, give = split(
        prior_fields,
        measured_spread.reshape(count, -1),
        scaled_misfit.reshape(1, -1),
        sensor_line_inside.reshape(1, -1),
        chips,
    )

    def trade(pairs):
        return lax.ppermute(packed, "gy", pairs) if pairs else None

    got = lax.ppermute(give, "gx", [(index, index ^ 1) for index in range(parts)])
    first = trade(swap_pairs(size, 1, 0))
    other = trade(swap_pairs(size, 1, 1))
    far, beyond = trade(swap_pairs(size, 2, 0)), trade(swap_pairs(size, 2, 1))
    own, *sent = sort(keep, got)
    blocks = [own]
    for step, block in enumerate(sent, 1):
        pairs = [
            (index, 2 * target_chip(index // 2, step, chips) + index % 2) for index in range(parts)
        ]
        blocks.append(lax.ppermute(block, "gx", pairs))
    mixes = weights(packed, first, other, far, beyond, size, rows)
    return analyse(blocks, mixes, size)


def solution(mesh):
    return jax.shard_map(
        on_device,
        mesh=mesh,
        in_specs=(P("gx", "gy", None), P(None, "gy", "gx"), P("gy", "gx"), P("gy", "gx")),
        out_specs=P(None, "gy", "gx"),
        check_vma=False,
    )
```

time: 26.5 us -> 21.8 us (0.82)
  waiting for transfers between devices: 2.97 us -> 1.01 us
  Pallas kernels: 11.9 us -> 10.3 us
  starting transfers between devices: 11.4 us -> 10.2 us
    ppermute x0 -> x4, starting transfers between devices: none -> 4.07 us  [the longest x3 3.55 us: on_device(): blocks.append(lax.ppermute(block, 'gx', pairs))]
    all_to_all x1 -> x0, starting transfers between devices: 3.74 us -> none  [on_device(): lax.all_to_all(to_send, 'gx', split_axis=0, concat_axis=0, tiled=True)]
    ppermute x3, waiting for transfers between devices: 2.85 us -> 1 us  [trade(): return lax.ppermute(packed, 'gy', pairs) if pairs else None]
    pallas_call x4 -> x5, Pallas kernels: 11.9 us -> 10.3 us  [the longest x1 5.21 us: weights(): pl.pallas_call(functools.partial(near_kernel, size, rows, beyond is not N...]
    ppermute x3, starting transfers between devices: 7.65 us -> 6.14 us  [trade(): return lax.ppermute(packed, 'gy', pairs) if pairs else None]
  transfers between devices with their start and end apart: 4 -> 7, of which waited for: 2 -> 1; matrix products, arithmetic and copies ran while one was open for 0% -> 0% of each run, Pallas kernels for 35% -> 33%
where the time goes in v3:
time: 21.8 us; the launch traced here: 21.6 us
  Pallas kernels  10.3 us (47%)
  starting transfers between devices  10.2 us (47%)
  waiting for transfers between devices  1.01 us (5%)
    ppermute x3, starting transfers between devices, trade(): return lax.ppermute(packed, 'gy', pairs) if pairs else None  6.14 us
    pallas_call x1, Pallas kernels, weights(): pl.pallas_call(functools.partial(near_kernel, size, rows, beyond is not N...  5.21 us
    ppermute x3, starting transfers between devices, on_device(): blocks.append(lax.ppermute(block, 'gx', pairs))  3.55 us
    pallas_call x1, Pallas kernels, weights(): pl.pallas_call(functools.partial(far_kernel, size, rows), out_shape=(pltp...  1.87 us
    pallas_call x1, Pallas kernels, analyse(): pl.pallas_call(functools.partial(analyse_kernel, size), out_shape=jax.Sha...  1.84 us
    pallas_call x1, Pallas kernels, split(): pl.pallas_call(functools.partial(split_kernel, chips), out_shape=(pltpu.V...  1.27 us
    ppermute x3, waiting for transfers between devices, trade(): return lax.ppermute(packed, 'gy', pairs) if pairs else None  1 us
    ppermute x1, starting transfers between devices, on_device(): lax.ppermute(give, 'gx', [(index, index ^ 1) for index in range(parts)])  0.52 us
  transfers between devices with their start and end apart: 7, of which 1 were waited for; matrix products, arithmetic and copies ran while one was open for 0% of the time, Pallas kernels for 33%

profile of v3, /device:TPU:0, one launch (start us, length us, event | category | flops | bytes accessed | tf_op | source)
XLA Modules:
  0.0 21.6 jit_solution(14819147721681197989)
XLA Ops:
  0.0 1.3 %split.1 = (bf16[528,128]{1,0:T(8,128)(2,1)S(1)}, bf16[4,64,4,128]{3,2,1,0:T(4,128)(2,1)S(1)}, bf16[4,64,4,128]{3,2,1,0:T(4,128)(2,1)S(1)}) custom-call(bf16[64,4,1024]{2,1,0:T(4,128)(2,1)} %prior_ref.1, bf16[512,128]{1,0:T(8,128)(2,1)} %bitcast.6, bf16[1,128]{1,0:T(2,128)(2,1)} %misfit_ref.1, s32[1,128]{1,0:T(1,128)} %line_ref.1), custom_call_target="tpu_custom_call" | custom-call | tf_op jit(solution)/shard_map/split/pallas_call | solution.py:74
  1.3 0.5 %collective-permute-start.3 = (bf16[4,64,4,128]{3,2,1,0:T(4,128)(2,1)S(1)}, bf16[4,64,4,128]{3,2,1,0:T(4,128)(2,1)S(1)}, u32[]{:S(2)}, u32[]{:S(2)}) collective-permute-start(bf16[4,64,4,128]{3,2,1,0:T(4,128)(2,1)S(1)} %get-tuple-element.26), channel_id=1, source_target_pairs={{0,4},{4,0},{8,12},{12,8},{16,20},{20,16},{24,28},{28,24},{1,5},{5... | collective-permute-start | bytes 786440 | tf_op jit(solution)/shard_map/ppermute | solution.py:399
  1.8 0.7 %collective-permute-start.1 = (bf16[528,128]{1,0:T(8,128)(2,1)S(1)}, bf16[528,128]{1,0:T(8,128)(2,1)S(1)}, u32[]{:S(2)}, u32[]{:S(2)}) collective-permute-start(bf16[528,128]{1,0:T(8,128)(2,1)S(1)} %get-tuple-element.18.refs_0_.own_ref), channel_id=1, source_target_pairs={{1,2},{2,1},{5,6},{6,5},{9,10},{10,9},{13,14},{14,13},{17,18},{18,... | collective-permute-start | bytes 405512 | tf_op jit(solution)/shard_map/ppermute | solution.py:397
  2.5 5.5 %collective-permute-start = (bf16[528,128]{1,0:T(8,128)(2,1)S(1)}, bf16[528,128]{1,0:T(8,128)(2,1)S(1)}, u32[]{:S(2)}, u32[]{:S(2)}) collective-permute-start(bf16[528,128]{1,0:T(8,128)(2,1)S(1)} %get-tuple-element.18.refs_0_.own_ref), channel_id=1, source_target_pairs={{0,1},{1,0},{2,3},{3,2},{4,5},{5,4},{6,7},{7,6},{8,9},{9,8},{10,11... | collective-permute-start | bytes 405512 | tf_op jit(solution)/shard_map/ppermute | solution.py:397
  7.9 0.0 collective-permute-start.2
  7.9 0.0 collective-permute-done.3
  7.9 0.1 sort.1
  8.1 1.6 %collective-permute-start.4 = (bf16[2,4,64,128]{3,2,1,0:T(8,128)(2,1)S(1)}, bf16[2,4,64,128]{3,2,1,0:T(8,128)(2,1)S(1)}, u32[]{:S(2)}, u32[]{:S(2)}) collective-permute-start(bf16[2,4,64,128]{3,2,1,0:T(8,128)(2,1)S(1)} %get-tuple-element.28), channel_id=1, source_target_pairs={{0,8},{4,12},{8,0},{12,4},{16,24},{20,28},{24,16},{28,20},{1,9},{5... | collective-permute-start | bytes 393224 | tf_op jit(solution)/shard_map/ppermute | solution.py:409
  9.6 1.5 %collective-permute-start.5 = (bf16[2,4,64,128]{3,2,1,0:T(8,128)(2,1)S(1)}, bf16[2,4,64,128]{3,2,1,0:T(8,128)(2,1)S(1)}, u32[]{:S(2)}, u32[]{:S(2)}) collective-permute-start(bf16[2,4,64,128]{3,2,1,0:T(8,128)(2,1)S(1)} %get-tuple-element.29), channel_id=1, source_target_pairs={{0,16},{4,20},{8,24},{12,28},{16,0},{20,4},{24,8},{28,12},{1,17},{... | collective-permute-start | bytes 393224 | tf_op jit(solution)/shard_map/ppermute | solution.py:409
  11.2 0.0 collective-permute-done.1.refs_2_.other_ref
  11.2 0.5 %collective-permute-start.6 = (bf16[2,4,64,128]{3,2,1,0:T(8,128)(2,1)S(1)}, bf16[2,4,64,128]{3,2,1,0:T(8,128)(2,1)S(1)}, u32[]{:S(2)}, u32[]{:S(2)}) collective-permute-start(bf16[2,4,64,128]{3,2,1,0:T(8,128)(2,1)S(1)} %get-tuple-element.30), channel_id=1, source_target_pairs={{0,24},{4,28},{8,16},{12,20},{16,8},{20,12},{24,0},{28,4},{1,25},{... | collective-permute-start | bytes 393224 | tf_op jit(solution)/shard_map/ppermute | solution.py:409
  11.6 1.0 %collective-permute-done.refs_1_.first_ref = bf16[528,128]{1,0:T(8,128)(2,1)S(1)} collective-permute-done((bf16[528,128]{1,0:T(8,128)(2,1)S(1)}, bf16[528,128]{1,0:T(8,128)(2,1)S(1)}, u32[]{:S(2)}, u32[]{:S(2)}) %collective-permute-start) | collective-permute-done | bytes 135200 | tf_op jit(solution)/shard_map/ppermute | solution.py:397
  12.6 5.2 %near.1 = (bf16[4,528,512]{2,1,0:T(8,128)(2,1)S(1)}, f32[4,8,128]{2,1,0:T(8,128)S(1)}, f32[512,512]{1,0:T(8,128)S(1)}, f32[16,512]{1,0:T(8,128)S(1)}) custom-call(bf16[528,128]{1,0:T(8,128)(2,1)S(1)} %get-tuple-element.18.refs_0_.own_ref, bf16[528,128]{1,0:T(8,128)(2,1)S(1)} %collective-permute-done.refs_1_.first_ref, ...), custom_call_target="tpu_custom_call" | custom-call | flops 24159191040 | bytes 2097152 | tf_op jit(solution)/shard_map/near/pallas_call | solution.py:291
  17.9 0.0 collective-permute-done.2.far_ref
  17.9 1.9 %far.1 = (bf16[1,528,512]{2,1,0:T(8,128)(2,1)S(1)}, f32[1,8,128]{2,1,0:T(8,128)S(1)}) custom-call(bf16[528,128]{1,0:T(8,128)(2,1)S(1)} %get-tuple-element.18.refs_0_.own_ref, bf16[528,128]{1,0:T(8,128)(2,1)S(1)} %collective-permute-done.refs_1_.first_ref, bf16[528,128]{1,0:T(8,128)(2,1)S(1)} %collective-permute-done.1.refs_2_.other_ref, ...), custom_call_target="tpu_custom_call" | custom-call | flops 268435456 | bytes 2097152 | tf_op jit(solution)/shard_map/far/pallas_call | solution.py:308
  19.7 0.0 collective-permute-done.4.refs_5_
  19.8 0.0 collective-permute-done.5.refs_6_
  19.8 0.0 collective-permute-done.6.refs_7_
  19.8 1.8 %analyse.1 = bf16[2048,128]{1,0:T(8,128)(2,1)} custom-call(bf16[4,528,512]{2,1,0:T(8,128)(2,1)S(1)} %get-tuple-element.19.refs_0_, f32[4,8,128]{2,1,0:T(8,128)S(1)} %get-tuple-element.20.refs_1_, bf16[1,528,512]{2,1,0:T(8,128)(2,1)S(1)} %get-tuple-element.23.refs_2_, f32[1,8,128]{2,1,0:T(8,128)S(1)} %get-tuple-element.24.refs_3_, ...), custom_call_target="tpu_custom_call" | custom-call | tf_op jit(solution)/shard_map/analyse/pallas_call | solution.py:367
Async XLA Ops:
  1.3 6.7 %collective-permute-start.3 = (bf16[4,64,4,128]{3,2,1,0:T(4,128)(2,1)S(1)}, bf16[4,64,4,128]{3,2,1,0:T(4,128)(2,1)S(1)}, u32[]{:S(2)}, u32[]{:S(2)}) collective-permute-start(bf16[4,64,4,128]{3,2,1,0:T(4,128)(2,1)S(1)} %get-tuple-element.26), channel_id=1, source_target_pairs={{0,4},{4,0},{8,12},{12,8},{16,20},{20,16},{24,28},{28,24},{1,5},{5... | collective-permute-start | bytes 786440 | tf_op jit(solution)/shard_map/ppermute | solution.py:399
  1.8 9.4 %collective-permute-start.1 = (bf16[528,128]{1,0:T(8,128)(2,1)S(1)}, bf16[528,128]{1,0:T(8,128)(2,1)S(1)}, u32[]{:S(2)}, u32[]{:S(2)}) collective-permute-start(bf16[528,128]{1,0:T(8,128)(2,1)S(1)} %get-tuple-element.18.refs_0_.own_ref), channel_id=1, source_target_pairs={{1,2},{2,1},{5,6},{6,5},{9,10},{10,9},{13,14},{14,13},{17,18},{18,... | collective-permute-start | bytes 405512 | tf_op jit(solution)/shard_map/ppermute | solution.py:397
  2.5 10.2 %collective-permute-start = (bf16[528,128]{1,0:T(8,128)(2,1)S(1)}, bf16[528,128]{1,0:T(8,128)(2,1)S(1)}, u32[]{:S(2)}, u32[]{:S(2)}) collective-permute-start(bf16[528,128]{1,0:T(8,128)(2,1)S(1)} %get-tuple-element.18.refs_0_.own_ref), channel_id=1, source_target_pairs={{0,1},{1,0},{2,3},{3,2},{4,5},{5,4},{6,7},{7,6},{8,9},{9,8},{10,11... | collective-permute-start | bytes 405512 | tf_op jit(solution)/shard_map/ppermute | solution.py:397
  7.9 9.9 %collective-permute-start.2 = (bf16[528,128]{1,0:T(8,128)(2,1)S(1)}, bf16[528,128]{1,0:T(8,128)(2,1)S(1)}, u32[]{:S(2)}, u32[]{:S(2)}) collective-permute-start(bf16[528,128]{1,0:T(8,128)(2,1)S(1)} %get-tuple-element.18.refs_0_.own_ref), channel_id=1, source_target_pairs={{0,2},{2,0},{1,3},{3,1},{4,6},{6,4},{5,7},{7,5},{8,10},{10,8},{9,1... | collective-permute-start | bytes 405512 | tf_op jit(solution)/shard_map/ppermute | solution.py:397
  8.1 11.7 %collective-permute-start.4 = (bf16[2,4,64,128]{3,2,1,0:T(8,128)(2,1)S(1)}, bf16[2,4,64,128]{3,2,1,0:T(8,128)(2,1)S(1)}, u32[]{:S(2)}, u32[]{:S(2)}) collective-permute-start(bf16[2,4,64,128]{3,2,1,0:T(8,128)(2,1)S(1)} %get-tuple-element.28), channel_id=1, source_target_pairs={{0,8},{4,12},{8,0},{12,4},{16,24},{20,28},{24,16},{28,20},{1,9},{5... | collective-permute-start | bytes 393224 | tf_op jit(solution)/shard_map/ppermute | solution.py:409
  9.6 10.1 %collective-permute-start.5 = (bf16[2,4,64,128]{3,2,1,0:T(8,128)(2,1)S(1)}, bf16[2,4,64,128]{3,2,1,0:T(8,128)(2,1)S(1)}, u32[]{:S(2)}, u32[]{:S(2)}) collective-permute-start(bf16[2,4,64,128]{3,2,1,0:T(8,128)(2,1)S(1)} %get-tuple-element.29), channel_id=1, source_target_pairs={{0,16},{4,20},{8,24},{12,28},{16,0},{20,4},{24,8},{28,12},{1,17},{... | collective-permute-start | bytes 393224 | tf_op jit(solution)/shard_map/ppermute | solution.py:409
  11.2 8.6 %collective-permute-start.6 = (bf16[2,4,64,128]{3,2,1,0:T(8,128)(2,1)S(1)}, bf16[2,4,64,128]{3,2,1,0:T(8,128)(2,1)S(1)}, u32[]{:S(2)}, u32[]{:S(2)}) collective-permute-start(bf16[2,4,64,128]{3,2,1,0:T(8,128)(2,1)S(1)} %get-tuple-element.30), channel_id=1, source_target_pairs={{0,24},{4,28},{8,16},{12,20},{16,8},{20,12},{24,0},{28,4},{1,25},{... | collective-permute-start | bytes 393224 | tf_op jit(solution)/shard_map/ppermute | solution.py:409

commit v4 on v3

--- a/solution.py
+++ b/solution.py
@@ -124,50 +124,97 @@
     return jnp.where(condition, jnp.float32(1.0), jnp.float32(0.0))
 
 
-def point_weights(left, count, radius, centre, bases, present):
-    line = left[count + 1 : count + 2, :].astype(jnp.float32)
-    obs = line.shape[1] // 3
-    where = lax.broadcasted_iota(jnp.int32, line.shape, 1) // obs
-    base = jnp.where(where == 0, bases[0], jnp.where(where == 1, bases[1], bases[2]))
-    alive = jnp.where(where == 0, present[0], jnp.where(where == 1, present[1], present[2]))
-    distance = (base + line + 0.5 - centre) / radius
-    locality = jnp.exp(-0.5 * distance * distance) * alive
-    scaled = (left[0:count, :].astype(jnp.float32) * locality).astype(jnp.bfloat16)
-    both = lax.dot_general(
-        left[...], scaled, (((1,), (1,)), ((), ())), preferred_element_type=jnp.float32
+class Point:
+    def __init__(self, left, centre, bases, present):
+        self.left, self.centre, self.bases, self.present = left, centre, bases, present
+
+
+def turn(row, eye):
+    block = eye.shape[0]
+    pieces = [row[:, i : i + block] for i in range(0, row.shape[1], block)]
+    return jnp.concatenate(
+        [jnp.sum(eye * piece, axis=1, keepdims=True) for piece in pieces], axis=0
     )
-    gram = both[0:count]
-    drive = both[count : count + 1]
+
+
+def lay(column, eye):
+    block = eye.shape[0]
+    pieces = [column[i : i + block] for i in range(0, column.shape[0], block)]
+    return jnp.concatenate(
+        [jnp.sum(eye * piece, axis=0, keepdims=True) for piece in pieces], axis=1
+    )
+
+
+def point_weights(points, count, radius, gram_ref, square_ref, last_ref, rest_ref):
     share = 1.0 / (count - 1.0)
-    on_diagonal = lax.broadcasted_iota(jnp.int32, gram.shape, 0) == lax.broadcasted_iota(
-        jnp.int32, gram.shape, 1
+    slots = range(len(points))
+    block = min(count, 128)
+    eye = jnp.where(
+        lax.broadcasted_iota(jnp.int32, (block, block), 0)
+        == lax.broadcasted_iota(jnp.int32, (block, block), 1),
+        1.0,
+        0.0,
     )
-    sizes = jnp.abs(jnp.where(on_diagonal, 1.0, 0.0) + gram * share)
-    bound = jnp.max(jnp.sum(sizes, axis=0, keepdims=True), axis=1, keepdims=True)
-    rounded = gram.astype(jnp.bfloat16)
-    square = jnp.dot(rounded, rounded, preferred_element_type=jnp.float32)
-    s = 1.0 / bound
-    g = s * share
-    first = jnp.broadcast_to(g, (1, count))
-    second = jnp.broadcast_to(g * g, (1, count))
-    beta = s * s - 9.0 * s
-    quad = second * square
-    x = (2.0 * s) * first * gram + quad
-    w = (2.0 * s - 9.0) * first * gram + quad
-    product = jnp.dot(x.astype(jnp.bfloat16), w.astype(jnp.bfloat16), preferred_element_type=jnp.float32)
-    on_gram = (-39.0 + (27.0 + beta) * (2.0 * s) + s * s * (2.0 * s - 9.0)) * first / 16.0
-    on_square = (27.0 + beta + s * s) * second / 16.0
-    rest = on_gram * gram + on_square * square + product * (1.0 / 16.0)
-    scalar_part = (36.0 + s * (-39.0 + s * (27.0 + s * (-9.0 + s)))) / 16.0
-    rest_rounded = rest.astype(jnp.bfloat16)
-
-    def row_times(row):
-        out = jnp.dot(two_rows(row), rest_rounded, preferred_element_type=jnp.float32)
-        return out[0:1] + out[1:2] + scalar_part * row
-
-    mean_weights = row_times(row_times(drive)) * g
-    root = lax.rsqrt(bound)
-    return rest * jnp.broadcast_to(root, (1, count)), scalar_part * root, mean_weights
+    drives, bounds = [], []
+    for slot in slots:
+        point = points[slot]
+        left = point.left
+        line = left[count + 1 : count + 2, :].astype(jnp.float32)
+        obs = line.shape[1] // 3
+        where = lax.broadcasted_iota(jnp.int32, line.shape, 1) // obs
+        first, second, third = point.bases
+        base = jnp.where(where == 0, first, jnp.where(where == 1, second, third))
+        first, second, third = point.present
+        alive = jnp.where(where == 0, first, jnp.where(where == 1, second, third))
+        distance = (base + line + 0.5 - point.centre) / radius
+        locality = jnp.exp(-0.5 * distance * distance) * alive
+        scaled = (left[0:count, :].astype(jnp.float32) * locality).astype(jnp.bfloat16)
+        both = lax.dot_general(
+            left[...], scaled, (((1,), (1,)), ((), ())), preferred_element_type=jnp.float32
+        )
+        gram = both[0:count]
+        drives.append(both[count : count + 1])
+        gram_ref[slot] = gram.astype(jnp.bfloat16)
+        sizes = jnp.sum(jnp.abs(gram), axis=0, keepdims=True)
+        bounds.append(1.0 + share * jnp.max(sizes, axis=1, keepdims=True))
+    factors = []
+    for slot in slots:
+        s = 1.0 / bounds[slot]
+        g = s * share
+        root = lax.rsqrt(bounds[slot])
+        wide = lambda value: jnp.broadcast_to(value, (1, count))
+        third = wide((4.0 * s - 9.0) * (g * g) * g * (root / 16.0))
+        fourth = wide((g * g) * (g * g) * (root / 16.0))
+        linear = wide((-39.0 + s * (54.0 + s * (-27.0 + 4.0 * s))) * g * (root / 16.0))
+        quadratic = wide((27.0 + s * (-27.0 + 6.0 * s)) * (g * g) * (root / 16.0))
+        scalar_part = (36.0 + s * (-39.0 + s * (27.0 + s * (-9.0 + s)))) * (root / 16.0)
+        factors.append((linear, quadratic, scalar_part, g * bounds[slot]))
+        gram = gram_ref[slot]
+        square = jnp.dot(gram, gram, preferred_element_type=jnp.float32)
+        square_ref[slot] = square.astype(jnp.bfloat16)
+        last = third * gram.astype(jnp.float32) + fourth * square
+        last_ref[slot] = last.astype(jnp.bfloat16)
+    firsts = []
+    for slot in slots:
+        linear, quadratic, scalar_part, _ = factors[slot]
+        product = jnp.dot(square_ref[slot], last_ref[slot], preferred_element_type=jnp.float32)
+        rest = (
+            linear * gram_ref[slot].astype(jnp.float32)
+            + quadratic * square_ref[slot].astype(jnp.float32)
+            + product
+        )
+        rest_ref[slot] = rest.astype(jnp.bfloat16)
+
+    results = []
+    for slot in slots:
+        _, _, scalar_part, g = factors[slot]
+        mean_weights = drives[slot]
+        for _ in range(2):
+            out = jnp.dot(two_rows(mean_weights), rest_ref[slot], preferred_element_type=jnp.float32)
+            mean_weights = out[0:1] + out[1:2] + scalar_part * mean_weights
+        mean_weights = mean_weights * g
+        results.append((scalar_part, mean_weights))
+    return results
 
 
 def two_rows(row):
@@ -207,24 +254,29 @@
     def own_point(self, ahead):
         return jnp.where(self.upward == ahead, jnp.float32(CP - 1), jnp.float32(0))
 
-    def side(self, left, count, ahead):
+    def side(self, left, ahead):
         sign = self.sign if ahead else -self.sign
         offsets = (sign, 2 * sign, 0 * sign)
+        centre = (self.side_point(ahead) + 0.5) * self.spacing
+        return self.point(left, centre, offsets)
+
+    def point(self, left, centre, offsets):
         bases = [(offset * self.rows).astype(jnp.float32) for offset in offsets]
-        present = [self.present(offset) for offset in offsets]
-        centre = (self.side_point(ahead) + 0.5) * self.spacing
-        return point_weights(left, count, float(self.rows), centre, bases, present)
+        return Point(left, centre, bases, [self.present(offset) for offset in offsets])
 
 
 def write_mix(mix_ref, diag_ref, row, terms, count):
-    mix_ref[row, 0:count, :] = sum(share * part[0] for share, part in terms).astype(jnp.bfloat16)
-    mix_ref[row, count:, :] = two_rows(sum(share * part[2] for share, part in terms))
-    diag_ref[row] = jnp.broadcast_to(sum(share * part[1] for share, part in terms), (8, 128))
+    mixed = sum(share * rest.astype(jnp.float32) for share, rest, _, _ in terms)
+    mix_ref[row, 0:count, :] = mixed.astype(jnp.bfloat16)
+    mix_ref[row, count:, :] = two_rows(sum(share * mean for share, _, _, mean in terms))
+    diag_ref[row] = jnp.broadcast_to(sum(share * diag for share, _, diag, _ in terms), (8, 128))
 
 
 def near_kernel(size, rows, has_far, *refs):
     own_ref, first_ref, other_ref = refs[:3]
-    mix_ref, diag_ref, beside_ref, small_ref, left = refs[4 if has_far else 3 :]
+    mix_ref, diag_ref, beside_ref, small_ref, left, gram, square, last, rest = refs[
+        4 if has_far else 3 :
+    ]
     count, obs = own_ref.shape[0] - PAD, own_ref.shape[1]
     at = Place(size, rows)
     ahead_is_first = at.even == at.upward
@@ -235,52 +287,46 @@
     left[:, 3 * obs : 4 * obs] = far
     left[:, 4 * obs :] = own_ref[...]
     offsets = (at.sign, 0 * at.sign, -at.sign)
-    bases = [(offset * rows).astype(jnp.float32) for offset in offsets]
-    present = [at.present(offset) for offset in offsets]
-    own = []
+    points = []
     for point in range(CP):
-        centre = (point + 0.5) * at.spacing
-        own.append(
-            point_weights(left.at[:, 0 : 3 * obs], count, float(rows), centre, bases, present)
-        )
-    behind = at.side(left.at[:, 2 * obs :], count, False)
+        points.append(at.point(left.at[:, 0 : 3 * obs], (point + 0.5) * at.spacing, offsets))
+    points.append(at.side(left.at[:, 2 * obs :], False))
+    results = point_weights(points, count, float(rows), gram, square, last, rest)
+
+    def term(row, point, slot):
+        return (at.share(row, point), rest[slot], *results[slot])
+
     for row in range(at.edge, rows - at.edge):
         low = int((row + 0.5) / at.spacing - 0.5)
-        terms = [(at.share(row, low + step), own[low + step]) for step in (0, 1)]
+        terms = [term(row, low + step, low + step) for step in (0, 1)]
         write_mix(mix_ref, diag_ref, row, terms, count)
-
-    def pick(ahead):
-        flag = at.upward == ahead
-        return [jnp.where(flag, last, first) for first, last in zip(own[0], own[CP - 1])]
-
     for step in range(at.edge):
         row = at.edge_row(False, step)
-        terms = [
-            (at.share(row, at.own_point(False)), pick(False)),
-            (at.share(row, at.side_point(False)), behind),
-        ]
+        terms = [term(row, point, point) for point in range(CP)]
+        terms.append(term(row, at.side_point(False), CP))
         write_mix(mix_ref, diag_ref, row, terms, count)
-    beside = pick(True)
-    beside_ref[...] = beside[0]
-    small_ref[0:8, :] = jnp.broadcast_to(beside[1], (8, count))
-    small_ref[8:16, :] = jnp.broadcast_to(beside[2], (8, count))
+    for point in range(CP):
+        beside_ref[point] = rest[point]
+        scalar_part, mean_weights = results[point]
+        small_ref[point, 0:8, :] = jnp.broadcast_to(scalar_part, (8, count))
+        small_ref[point, 8:16, :] = jnp.broadcast_to(mean_weights, (8, count))
 
 
 def far_kernel(size, rows, own_ref, first_ref, other_ref, far_ref, beside_ref, small_ref, *refs):
-    mix_ref, diag_ref, left = refs
+    mix_ref, diag_ref, left, gram, square, last, rest = refs
     count, obs = own_ref.shape[0] - PAD, own_ref.shape[1]
     at = Place(size, rows)
     left[:, 0:obs] = jnp.where(at.even == at.upward, first_ref[...], other_ref[...])
     left[:, obs : 2 * obs] = far_ref[...]
     left[:, 2 * obs :] = own_ref[...]
-    ahead = at.side(left, count, True)
-    beside = (beside_ref[...], small_ref[0:1, 0:1], small_ref[8:9, :])
+    points = [at.side(left, True)]
+    results = point_weights(points, count, float(rows), gram, square, last, rest)
     for step in range(at.edge):
         row = at.edge_row(True, step)
-        terms = [
-            (at.share(row, at.own_point(True)), beside),
-            (at.share(row, at.side_point(True)), ahead),
-        ]
+        terms = [(at.share(row, at.side_point(True)), rest[0], *results[0])]
+        for point in range(CP):
+            small = (small_ref[point, 0:1, 0:1], small_ref[point, 8:9, :])
+            terms.append((at.share(row, point), beside_ref[point], *small))
         write_mix(mix_ref, diag_ref, step, terms, count)
 
 
@@ -293,12 +339,13 @@
         out_shape=(
             pltpu.VMEM((rows, count + PAD, count), jnp.bfloat16),
             pltpu.VMEM((rows, 8, 128), jnp.float32),
-            pltpu.VMEM((count, count), jnp.float32),
-            pltpu.VMEM((16, count), jnp.float32),
+            pltpu.VMEM((CP, count, count), jnp.bfloat16),
+            pltpu.VMEM((CP, 16, count), jnp.float32),
         ),
         in_specs=[VMEM] * len(near_inputs),
         out_specs=(VMEM,) * 4,
-        scratch_shapes=[pltpu.VMEM((count + PAD, 5 * obs), jnp.bfloat16)],
+        scratch_shapes=[pltpu.VMEM((count + PAD, 5 * obs), jnp.bfloat16)]
+        + [pltpu.VMEM((CP + 1, count, count), jnp.bfloat16)] * 4,
         compiler_params=pltpu.CompilerParams(vmem_limit_bytes=40 * MIB),
         cost_estimate=pl.CostEstimate(
             flops=NEAR_FLOPS * count**3, bytes_accessed=8 * count * count, transcendentals=0
@@ -313,7 +360,8 @@
         ),
         in_specs=[VMEM] * 6,
         out_specs=(VMEM,) * 2,
-        scratch_shapes=[pltpu.VMEM((count + PAD, 3 * obs), jnp.bfloat16)],
+        scratch_shapes=[pltpu.VMEM((count + PAD, 3 * obs), jnp.bfloat16)]
+        + [pltpu.VMEM((1, count, count), jnp.bfloat16)] * 4,
         compiler_params=pltpu.CompilerParams(vmem_limit_bytes=32 * MIB),
         cost_estimate=pl.CostEstimate(
             flops=FAR_FLOPS * count**3, bytes_accessed=8 * count * count, transcendentals=0

time: 21.8 us -> 21.4 us (0.982)
  Pallas kernels: 10.3 us -> 9.57 us
  waiting for transfers between devices: 1.01 us -> 1.45 us
    pallas_call x1, Pallas kernels: 5.21 us -> 4.39 us  [weights(): pl.pallas_call(functools.partial(near_kernel, size, rows, beyond is not N...]
    ppermute x3, waiting for transfers between devices: 1 us -> 1.44 us  [trade(): return lax.ppermute(packed, 'gy', pairs) if pairs else None]
  transfers between devices with their start and end apart: 7 -> 7, of which waited for: 1 -> 2; matrix products, arithmetic and copies ran while one was open for 0% -> 0% of each run, Pallas kernels for 33% -> 30%
where the time goes in v4:
time: 21.4 us; the launch traced here: 21.3 us
  starting transfers between devices  10.2 us (48%)
  Pallas kernels  9.57 us (45%)
  waiting for transfers between devices  1.45 us (7%)
    ppermute x3, starting transfers between devices, trade(): return lax.ppermute(packed, 'gy', pairs) if pairs else None  6.14 us
    pallas_call x1, Pallas kernels, weights(): pl.pallas_call(functools.partial(near_kernel, size, rows, beyond is not N...  4.39 us
    ppermute x3, starting transfers between devices, on_device(): blocks.append(lax.ppermute(block, 'gx', pairs))  3.55 us
    pallas_call x1, Pallas kernels, weights(): pl.pallas_call(functools.partial(far_kernel, size, rows), out_shape=(pltp...  1.93 us
    pallas_call x1, Pallas kernels, analyse(): pl.pallas_call(functools.partial(analyse_kernel, size), out_shape=jax.Sha...  1.84 us
    ppermute x3, waiting for transfers between devices, trade(): return lax.ppermute(packed, 'gy', pairs) if pairs else None  1.44 us
    pallas_call x1, Pallas kernels, split(): pl.pallas_call(functools.partial(split_kernel, chips), out_shape=(pltpu.V...  1.27 us
    ppermute x1, starting transfers between devices, on_device(): lax.ppermute(give, 'gx', [(index, index ^ 1) for index in range(parts)])  0.52 us
  transfers between devices with their start and end apart: 7, of which 2 were waited for; matrix products, arithmetic and copies ran while one was open for 0% of the time, Pallas kernels for 30%

profile of v4, /device:TPU:0, one launch (start us, length us, event | category | flops | bytes accessed | tf_op | source)
XLA Modules:
  0.0 21.3 jit_solution(17543971907851556710)
XLA Ops:
  0.0 1.3 %split.1 = (bf16[528,128]{1,0:T(8,128)(2,1)S(1)}, bf16[4,64,4,128]{3,2,1,0:T(4,128)(2,1)S(1)}, bf16[4,64,4,128]{3,2,1,0:T(4,128)(2,1)S(1)}) custom-call(bf16[64,4,1024]{2,1,0:T(4,128)(2,1)} %prior_ref.1, bf16[512,128]{1,0:T(8,128)(2,1)} %bitcast.6, bf16[1,128]{1,0:T(2,128)(2,1)} %misfit_ref.1, s32[1,128]{1,0:T(1,128)} %line_ref.1), custom_call_target="tpu_custom_call" | custom-call | tf_op jit(solution)/shard_map/split/pallas_call | solution.py:74
  1.3 0.5 %collective-permute-start.3 = (bf16[4,64,4,128]{3,2,1,0:T(4,128)(2,1)S(1)}, bf16[4,64,4,128]{3,2,1,0:T(4,128)(2,1)S(1)}, u32[]{:S(2)}, u32[]{:S(2)}) collective-permute-start(bf16[4,64,4,128]{3,2,1,0:T(4,128)(2,1)S(1)} %get-tuple-element.26), channel_id=1, source_target_pairs={{0,4},{4,0},{8,12},{12,8},{16,20},{20,16},{24,28},{28,24},{1,5},{5... | collective-permute-start | bytes 786440 | tf_op jit(solution)/shard_map/ppermute | solution.py:447
  1.8 0.7 %collective-permute-start.1 = (bf16[528,128]{1,0:T(8,128)(2,1)S(1)}, bf16[528,128]{1,0:T(8,128)(2,1)S(1)}, u32[]{:S(2)}, u32[]{:S(2)}) collective-permute-start(bf16[528,128]{1,0:T(8,128)(2,1)S(1)} %get-tuple-element.18.refs_0_.own_ref), channel_id=1, source_target_pairs={{1,2},{2,1},{5,6},{6,5},{9,10},{10,9},{13,14},{14,13},{17,18},{18,... | collective-permute-start | bytes 405512 | tf_op jit(solution)/shard_map/ppermute | solution.py:445
  2.5 5.5 %collective-permute-start = (bf16[528,128]{1,0:T(8,128)(2,1)S(1)}, bf16[528,128]{1,0:T(8,128)(2,1)S(1)}, u32[]{:S(2)}, u32[]{:S(2)}) collective-permute-start(bf16[528,128]{1,0:T(8,128)(2,1)S(1)} %get-tuple-element.18.refs_0_.own_ref), channel_id=1, source_target_pairs={{0,1},{1,0},{2,3},{3,2},{4,5},{5,4},{6,7},{7,6},{8,9},{9,8},{10,11... | collective-permute-start | bytes 405512 | tf_op jit(solution)/shard_map/ppermute | solution.py:445
  7.9 0.0 collective-permute-start.2
  7.9 0.0 collective-permute-done.3
  7.9 0.1 sort.1
  8.1 1.6 %collective-permute-start.4 = (bf16[2,4,64,128]{3,2,1,0:T(8,128)(2,1)S(1)}, bf16[2,4,64,128]{3,2,1,0:T(8,128)(2,1)S(1)}, u32[]{:S(2)}, u32[]{:S(2)}) collective-permute-start(bf16[2,4,64,128]{3,2,1,0:T(8,128)(2,1)S(1)} %get-tuple-element.28), channel_id=1, source_target_pairs={{0,8},{4,12},{8,0},{12,4},{16,24},{20,28},{24,16},{28,20},{1,9},{5... | collective-permute-start | bytes 393224 | tf_op jit(solution)/shard_map/ppermute | solution.py:457
  9.6 1.5 %collective-permute-start.5 = (bf16[2,4,64,128]{3,2,1,0:T(8,128)(2,1)S(1)}, bf16[2,4,64,128]{3,2,1,0:T(8,128)(2,1)S(1)}, u32[]{:S(2)}, u32[]{:S(2)}) collective-permute-start(bf16[2,4,64,128]{3,2,1,0:T(8,128)(2,1)S(1)} %get-tuple-element.29), channel_id=1, source_target_pairs={{0,16},{4,20},{8,24},{12,28},{16,0},{20,4},{24,8},{28,12},{1,17},{... | collective-permute-start | bytes 393224 | tf_op jit(solution)/shard_map/ppermute | solution.py:457
  11.2 0.0 collective-permute-done.1.refs_2_.other_ref
  11.2 0.5 %collective-permute-start.6 = (bf16[2,4,64,128]{3,2,1,0:T(8,128)(2,1)S(1)}, bf16[2,4,64,128]{3,2,1,0:T(8,128)(2,1)S(1)}, u32[]{:S(2)}, u32[]{:S(2)}) collective-permute-start(bf16[2,4,64,128]{3,2,1,0:T(8,128)(2,1)S(1)} %get-tuple-element.30), channel_id=1, source_target_pairs={{0,24},{4,28},{8,16},{12,20},{16,8},{20,12},{24,0},{28,4},{1,25},{... | collective-permute-start | bytes 393224 | tf_op jit(solution)/shard_map/ppermute | solution.py:457
  11.6 1.0 %collective-permute-done.refs_1_.first_ref = bf16[528,128]{1,0:T(8,128)(2,1)S(1)} collective-permute-done((bf16[528,128]{1,0:T(8,128)(2,1)S(1)}, bf16[528,128]{1,0:T(8,128)(2,1)S(1)}, u32[]{:S(2)}, u32[]{:S(2)}) %collective-permute-start) | collective-permute-done | bytes 135200 | tf_op jit(solution)/shard_map/ppermute | solution.py:445
  12.6 4.4 %near.1 = (bf16[4,528,512]{2,1,0:T(8,128)(2,1)S(1)}, f32[4,8,128]{2,1,0:T(8,128)S(1)}, bf16[2,512,512]{2,1,0:T(8,128)(2,1)S(1)}, f32[2,16,512]{2,1,0:T(8,128)S(1)}) custom-call(bf16[528,128]{1,0:T(8,128)(2,1)S(1)} %get-tuple-element.18.refs_0_.own_ref, bf16[528,128]{1,0:T(8,128)(2,1)S(1)} %collective-permute-done.refs_1_.first_ref, ...), custom_call_target="tpu_custom_call" | custom-call | flops 24159191040 | bytes 2097152 | tf_op jit(solution)/shard_map/near/pallas_call | solution.py:337
  17.0 0.4 %collective-permute-done.2.far_ref = bf16[528,128]{1,0:T(8,128)(2,1)S(1)} collective-permute-done((bf16[528,128]{1,0:T(8,128)(2,1)S(1)}, bf16[528,128]{1,0:T(8,128)(2,1)S(1)}, u32[]{:S(2)}, u32[]{:S(2)}) %collective-permute-start.2) | collective-permute-done | bytes 135200 | tf_op jit(solution)/shard_map/ppermute | solution.py:445
  17.5 1.9 %far.1 = (bf16[1,528,512]{2,1,0:T(8,128)(2,1)S(1)}, f32[1,8,128]{2,1,0:T(8,128)S(1)}) custom-call(bf16[528,128]{1,0:T(8,128)(2,1)S(1)} %get-tuple-element.18.refs_0_.own_ref, bf16[528,128]{1,0:T(8,128)(2,1)S(1)} %collective-permute-done.refs_1_.first_ref, bf16[528,128]{1,0:T(8,128)(2,1)S(1)} %collective-permute-done.1.refs_2_.other_ref, ...), custom_call_target="tpu_custom_call" | custom-call | flops 268435456 | bytes 2097152 | tf_op jit(solution)/shard_map/far/pallas_call | solution.py:355
  19.4 0.0 collective-permute-done.4.refs_5_
  19.4 0.0 collective-permute-done.5.refs_6_
  19.4 0.0 collective-permute-done.6.refs_7_
  19.4 1.8 %analyse.1 = bf16[2048,128]{1,0:T(8,128)(2,1)} custom-call(bf16[4,528,512]{2,1,0:T(8,128)(2,1)S(1)} %get-tuple-element.19.refs_0_, f32[4,8,128]{2,1,0:T(8,128)S(1)} %get-tuple-element.20.refs_1_, bf16[1,528,512]{2,1,0:T(8,128)(2,1)S(1)} %get-tuple-element.23.refs_2_, f32[1,8,128]{2,1,0:T(8,128)S(1)} %get-tuple-element.24.refs_3_, ...), custom_call_target="tpu_custom_call" | custom-call | tf_op jit(solution)/shard_map/analyse/pallas_call | solution.py:415
Async XLA Ops:
  1.3 6.7 %collective-permute-start.3 = (bf16[4,64,4,128]{3,2,1,0:T(4,128)(2,1)S(1)}, bf16[4,64,4,128]{3,2,1,0:T(4,128)(2,1)S(1)}, u32[]{:S(2)}, u32[]{:S(2)}) collective-permute-start(bf16[4,64,4,128]{3,2,1,0:T(4,128)(2,1)S(1)} %get-tuple-element.26), channel_id=1, source_target_pairs={{0,4},{4,0},{8,12},{12,8},{16,20},{20,16},{24,28},{28,24},{1,5},{5... | collective-permute-start | bytes 786440 | tf_op jit(solution)/shard_map/ppermute | solution.py:447
  1.8 9.4 %collective-permute-start.1 = (bf16[528,128]{1,0:T(8,128)(2,1)S(1)}, bf16[528,128]{1,0:T(8,128)(2,1)S(1)}, u32[]{:S(2)}, u32[]{:S(2)}) collective-permute-start(bf16[528,128]{1,0:T(8,128)(2,1)S(1)} %get-tuple-element.18.refs_0_.own_ref), channel_id=1, source_target_pairs={{1,2},{2,1},{5,6},{6,5},{9,10},{10,9},{13,14},{14,13},{17,18},{18,... | collective-permute-start | bytes 405512 | tf_op jit(solution)/shard_map/ppermute | solution.py:445
  2.5 10.2 %collective-permute-start = (bf16[528,128]{1,0:T(8,128)(2,1)S(1)}, bf16[528,128]{1,0:T(8,128)(2,1)S(1)}, u32[]{:S(2)}, u32[]{:S(2)}) collective-permute-start(bf16[528,128]{1,0:T(8,128)(2,1)S(1)} %get-tuple-element.18.refs_0_.own_ref), channel_id=1, source_target_pairs={{0,1},{1,0},{2,3},{3,2},{4,5},{5,4},{6,7},{7,6},{8,9},{9,8},{10,11... | collective-permute-start | bytes 405512 | tf_op jit(solution)/shard_map/ppermute | solution.py:445
  7.9 9.5 %collective-permute-start.2 = (bf16[528,128]{1,0:T(8,128)(2,1)S(1)}, bf16[528,128]{1,0:T(8,128)(2,1)S(1)}, u32[]{:S(2)}, u32[]{:S(2)}) collective-permute-start(bf16[528,128]{1,0:T(8,128)(2,1)S(1)} %get-tuple-element.18.refs_0_.own_ref), channel_id=1, source_target_pairs={{0,2},{2,0},{1,3},{3,1},{4,6},{6,4},{5,7},{7,5},{8,10},{10,8},{9,1... | collective-permute-start | bytes 405512 | tf_op jit(solution)/shard_map/ppermute | solution.py:445
  8.1 11.3 %collective-permute-start.4 = (bf16[2,4,64,128]{3,2,1,0:T(8,128)(2,1)S(1)}, bf16[2,4,64,128]{3,2,1,0:T(8,128)(2,1)S(1)}, u32[]{:S(2)}, u32[]{:S(2)}) collective-permute-start(bf16[2,4,64,128]{3,2,1,0:T(8,128)(2,1)S(1)} %get-tuple-element.28), channel_id=1, source_target_pairs={{0,8},{4,12},{8,0},{12,4},{16,24},{20,28},{24,16},{28,20},{1,9},{5... | collective-permute-start | bytes 393224 | tf_op jit(solution)/shard_map/ppermute | solution.py:457
  9.6 9.8 %collective-permute-start.5 = (bf16[2,4,64,128]{3,2,1,0:T(8,128)(2,1)S(1)}, bf16[2,4,64,128]{3,2,1,0:T(8,128)(2,1)S(1)}, u32[]{:S(2)}, u32[]{:S(2)}) collective-permute-start(bf16[2,4,64,128]{3,2,1,0:T(8,128)(2,1)S(1)} %get-tuple-element.29), channel_id=1, source_target_pairs={{0,16},{4,20},{8,24},{12,28},{16,0},{20,4},{24,8},{28,12},{1,17},{... | collective-permute-start | bytes 393224 | tf_op jit(solution)/shard_map/ppermute | solution.py:457
  11.2 8.3 %collective-permute-start.6 = (bf16[2,4,64,128]{3,2,1,0:T(8,128)(2,1)S(1)}, bf16[2,4,64,128]{3,2,1,0:T(8,128)(2,1)S(1)}, u32[]{:S(2)}, u32[]{:S(2)}) collective-permute-start(bf16[2,4,64,128]{3,2,1,0:T(8,128)(2,1)S(1)} %get-tuple-element.30), channel_id=1, source_target_pairs={{0,24},{4,28},{8,16},{12,20},{16,8},{20,12},{24,0},{28,4},{1,25},{... | collective-permute-start | bytes 393224 | tf_op jit(solution)/shard_map/ppermute | solution.py:457

commit v5 on v4

--- a/solution.py
+++ b/solution.py
@@ -11,7 +11,6 @@
 PAD = 16
 MIB = 1 << 20
 NEAR_FLOPS = 180
-FAR_FLOPS = 2
 
 VMEM = pl.BlockSpec(memory_space=pltpu.VMEM)
 HBM = pl.BlockSpec(memory_space=pltpu.HBM)
@@ -145,7 +144,8 @@
     )
 
 
-def point_weights(points, count, radius, gram_ref, square_ref, last_ref, rest_ref):
+def point_weights(points, count, radius, gram_ref, square_ref, last_ref, rest_ref, between=()):
+    pieces = iter(between)
     share = 1.0 / (count - 1.0)
     slots = range(len(points))
     block = min(count, 128)
@@ -177,6 +177,7 @@
         gram_ref[slot] = gram.astype(jnp.bfloat16)
         sizes = jnp.sum(jnp.abs(gram), axis=0, keepdims=True)
         bounds.append(1.0 + share * jnp.max(sizes, axis=1, keepdims=True))
+    next(pieces, int)()
     factors = []
     for slot in slots:
         s = 1.0 / bounds[slot]
@@ -194,7 +195,7 @@
         square_ref[slot] = square.astype(jnp.bfloat16)
         last = third * gram.astype(jnp.float32) + fourth * square
         last_ref[slot] = last.astype(jnp.bfloat16)
-    firsts = []
+    next(pieces, int)()
     for slot in slots:
         linear, quadratic, scalar_part, _ = factors[slot]
         product = jnp.dot(square_ref[slot], last_ref[slot], preferred_element_type=jnp.float32)
@@ -205,6 +206,7 @@
         )
         rest_ref[slot] = rest.astype(jnp.bfloat16)
 
+    next(pieces, int)()
     results = []
     for slot in slots:
         _, _, scalar_part, g = factors[slot]
@@ -212,6 +214,7 @@
         for _ in range(2):
             out = jnp.dot(two_rows(mean_weights), rest_ref[slot], preferred_element_type=jnp.float32)
             mean_weights = out[0:1] + out[1:2] + scalar_part * mean_weights
+            next(pieces, int)()
         mean_weights = mean_weights * g
         results.append((scalar_part, mean_weights))
     return results
@@ -265,11 +268,15 @@
         return Point(left, centre, bases, [self.present(offset) for offset in offsets])
 
 
+def mix_rows(mix_ref, terms, count):
+    mixed = sum(share * rest.astype(jnp.float32) for share, rest, _, _ in terms)
+    mix_ref[0:count, :] = mixed.astype(jnp.bfloat16)
+    mix_ref[count:, :] = two_rows(sum(share * mean for share, _, _, mean in terms))
+    return sum(share * diag for share, _, diag, _ in terms)
+
+
 def write_mix(mix_ref, diag_ref, row, terms, count):
-    mixed = sum(share * rest.astype(jnp.float32) for share, rest, _, _ in terms)
-    mix_ref[row, 0:count, :] = mixed.astype(jnp.bfloat16)
-    mix_ref[row, count:, :] = two_rows(sum(share * mean for share, _, _, mean in terms))
-    diag_ref[row] = jnp.broadcast_to(sum(share * diag for share, _, diag, _ in terms), (8, 128))
+    diag_ref[row] = jnp.broadcast_to(mix_rows(mix_ref.at[row], terms, count), (8, 128))
 
 
 def near_kernel(size, rows, has_far, *refs):
@@ -312,27 +319,8 @@
         small_ref[point, 8:16, :] = jnp.broadcast_to(mean_weights, (8, count))
 
 
-def far_kernel(size, rows, own_ref, first_ref, other_ref, far_ref, beside_ref, small_ref, *refs):
-    mix_ref, diag_ref, left, gram, square, last, rest = refs
-    count, obs = own_ref.shape[0] - PAD, own_ref.shape[1]
-    at = Place(size, rows)
-    left[:, 0:obs] = jnp.where(at.even == at.upward, first_ref[...], other_ref[...])
-    left[:, obs : 2 * obs] = far_ref[...]
-    left[:, 2 * obs :] = own_ref[...]
-    points = [at.side(left, True)]
-    results = point_weights(points, count, float(rows), gram, square, last, rest)
-    for step in range(at.edge):
-        row = at.edge_row(True, step)
-        terms = [(at.share(row, at.side_point(True)), rest[0], *results[0])]
-        for point in range(CP):
-            small = (small_ref[point, 0:1, 0:1], small_ref[point, 8:9, :])
-            terms.append((at.share(row, point), beside_ref[point], *small))
-        write_mix(mix_ref, diag_ref, step, terms, count)
-
-
-def weights(own, first, other, far, beyond, size, rows):
+def weights(own, first, other, beyond, size, rows):
     count, obs = own.shape[0] - PAD, own.shape[1]
-    edge = rows // CP // 2
     near_inputs = [own, first, other] + ([] if beyond is None else [beyond])
     mix, diag, beside, small = pl.pallas_call(
         functools.partial(near_kernel, size, rows, beyond is not None),
@@ -352,78 +340,85 @@
         ),
         name="near",
     )(*near_inputs)
-    edge_mix, edge_diag = pl.pallas_call(
-        functools.partial(far_kernel, size, rows),
-        out_shape=(
-            pltpu.VMEM((edge, count + PAD, count), jnp.bfloat16),
-            pltpu.VMEM((edge, 8, 128), jnp.float32),
-        ),
-        in_specs=[VMEM] * 6,
-        out_specs=(VMEM,) * 2,
-        scratch_shapes=[pltpu.VMEM((count + PAD, 3 * obs), jnp.bfloat16)]
-        + [pltpu.VMEM((1, count, count), jnp.bfloat16)] * 4,
-        compiler_params=pltpu.CompilerParams(vmem_limit_bytes=32 * MIB),
-        cost_estimate=pl.CostEstimate(
-            flops=FAR_FLOPS * count**3, bytes_accessed=8 * count * count, transcendentals=0
-        ),
-        name="far",
-    )(own, first, other, far, beside, small)
-    return mix, diag, edge_mix, edge_diag
-
-
-def analyse_kernel(size, *refs):
-    mix_ref, diag_ref, edge_mix_ref, edge_diag_ref = refs[:4]
-    block_refs = refs[4:-3]
-    out_ref, deviations, wide = refs[-3:]
+    return mix, diag, beside, small
+
+
+def finish_kernel(size, rows, *refs):
+    own_ref, first_ref, other_ref, far_ref, mix_ref, diag_ref, beside_ref, small_ref = refs[:8]
+    block_refs = refs[8:-9]
+    out_ref, left, gram, square, last, rest, edge_mix, deviations, wide = refs[-9:]
     chips = len(block_refs)
-    _, rows, members, width = block_refs[0].shape
-    count = 2 * chips * members
+    _, _, members, width = block_refs[0].shape
+    count, obs = own_ref.shape[0] - PAD, own_ref.shape[1]
     at = Place(size, rows)
     chip = lax.axis_index("gx") // 2
-
-    def one_row(row, mix, diag):
-        halves = [(step, side) for step in range(chips) for side in range(2)]
+    halves = [(step, side) for step in range(chips) for side in range(2)]
+
+    def deviate(row):
         blocks = [block_refs[step][side, row].astype(jnp.float32) for step, side in halves]
-        total = sum(jnp.sum(block, axis=0, keepdims=True) for block in blocks)
-        mean = total / count
+        mean = sum(jnp.sum(block, axis=0, keepdims=True) for block in blocks) / count
         for (step, side), block in zip(halves, blocks):
             first = (2 * source_chip(chip, step, chips) + side) * members
-            deviations[pl.ds(pl.multiple_of(first, members), members), :] = (block - mean).astype(
-                jnp.bfloat16
-            )
-        deviation = deviations[...]
+            deviations[row, pl.ds(pl.multiple_of(first, members), members), :] = (
+                block - mean
+            ).astype(jnp.bfloat16)
+        return mean
+
+    def apply(row, mean, mix, diag):
+        deviation = deviations[row]
         term = jnp.dot(mix, deviation, preferred_element_type=jnp.float32)
         shift = mean + term[count : count + 1] + term[count + 1 : count + 2]
         wide[pl.ds(row, count, stride=rows), :] = (
             term[0:count] + diag * deviation.astype(jnp.float32) + shift
         )
 
-    for row in range(at.edge, rows - at.edge):
-        one_row(row, mix_ref[row], diag_ref[row, 0:1, 0:width])
-    for step in range(at.edge):
-        row = at.edge_row(False, step)
-        one_row(row, mix_ref[row], diag_ref[row, 0:1, 0:width])
-    for step in range(at.edge):
-        row = at.edge_row(True, step)
-        one_row(row, edge_mix_ref[step], edge_diag_ref[step, 0:1, 0:width])
+    def whole_row(row):
+        apply(row, deviate(row), mix_ref[row], diag_ref[row, 0:1, 0:width])
+
+    behind = [at.edge_row(False, step) for step in range(at.edge)]
+    ahead = [at.edge_row(True, step) for step in range(at.edge)]
+    means = []
+    between = [functools.partial(whole_row, row) for row in range(at.edge, rows - at.edge)]
+    between += [functools.partial(whole_row, row) for row in behind]
+    between += [lambda: means.extend([deviate(row) for row in ahead])]
+
+    left[:, 0:obs] = jnp.where(at.even == at.upward, first_ref[...], other_ref[...])
+    left[:, obs : 2 * obs] = far_ref[...]
+    left[:, 2 * obs :] = own_ref[...]
+    points = [at.side(left, True)]
+    results = point_weights(points, count, float(rows), gram, square, last, rest, between)
+    for step, row in enumerate(ahead):
+        terms = [(at.share(row, at.side_point(True)), rest[0], *results[0])]
+        for point in range(CP):
+            small = (small_ref[point, 0:1, 0:1], small_ref[point, 8:9, :])
+            terms.append((at.share(row, point), beside_ref[point], *small))
+        diag = mix_rows(edge_mix.at[step], terms, count)
+        apply(row, means[step], edge_mix[step], diag)
     out_ref[...] = wide[...].astype(jnp.bfloat16)
 
 
-def analyse(blocks, mixes, size):
+def finish(tiles, mixes, blocks, size):
     _, rows, members, width = blocks[0].shape
-    count = 2 * len(blocks) * members
+    count, obs = tiles[0].shape[0] - PAD, tiles[0].shape[1]
+    square = pltpu.VMEM((1, count, count), jnp.bfloat16)
     flat = pl.pallas_call(
-        functools.partial(analyse_kernel, size),
+        functools.partial(finish_kernel, size, rows),
         out_shape=jax.ShapeDtypeStruct((count * rows, width), jnp.bfloat16),
-        in_specs=[VMEM] * (4 + len(blocks)),
+        in_specs=[VMEM] * (8 + len(blocks)),
         out_specs=VMEM,
         scratch_shapes=[
-            pltpu.VMEM((count, width), jnp.bfloat16),
+            pltpu.VMEM((count + PAD, 3 * obs), jnp.bfloat16),
+            square,
+            square,
+            square,
+            square,
+            pltpu.VMEM((rows // CP // 2, count + PAD, count), jnp.bfloat16),
+            pltpu.VMEM((rows, count, width), jnp.bfloat16),
             pltpu.VMEM((count * rows, width), jnp.float32),
         ],
-        compiler_params=pltpu.CompilerParams(vmem_limit_bytes=24 * MIB),
-        name="analyse",
-    )(*mixes, *blocks)
+        compiler_params=pltpu.CompilerParams(vmem_limit_bytes=40 * MIB),
+        name="finish",
+    )(*tiles, *mixes, *blocks)
     return flat.reshape(count, rows, width)
 
 
@@ -455,8 +450,8 @@
             (index, 2 * target_chip(index // 2, step, chips) + index % 2) for index in range(parts)
         ]
         blocks.append(lax.ppermute(block, "gx", pairs))
-    mixes = weights(packed, first, other, far, beyond, size, rows)
-    return analyse(blocks, mixes, size)
+    mixes = weights(packed, first, other, beyond, size, rows)
+    return finish((packed, first, other, far), mixes, blocks, size)
 
 
 def solution(mesh):

time: 21.4 us -> 21 us (0.981)
  Pallas kernels: 9.57 us -> 9.12 us
    pallas_call x2 -> x1, Pallas kernels: 3.78 us -> 3.33 us  [finish(): pl.pallas_call(functools.partial(finish_kernel, size, rows), out_shape=ja...]
  transfers between devices with their start and end apart: 7 -> 7, of which waited for: 2 -> 2; matrix products, arithmetic and copies ran while one was open for 0% -> 0% of each run, Pallas kernels for 30% -> 22%
where the time goes in v5:
time: 21 us; the launch traced here: 20.8 us
  starting transfers between devices  10.2 us (49%)
  Pallas kernels  9.12 us (43%)
  waiting for transfers between devices  1.46 us (7%)
    ppermute x3, starting transfers between devices, trade(): return lax.ppermute(packed, 'gy', pairs) if pairs else None  6.14 us
    pallas_call x1, Pallas kernels, weights(): pl.pallas_call(functools.partial(near_kernel, size, rows, beyond is not N...  4.39 us
    ppermute x3, starting transfers between devices, on_device(): blocks.append(lax.ppermute(block, 'gx', pairs))  3.55 us
    pallas_call x1, Pallas kernels, finish(): pl.pallas_call(functools.partial(finish_kernel, size, rows), out_shape=ja...  3.33 us
    ppermute x3, waiting for transfers between devices, trade(): return lax.ppermute(packed, 'gy', pairs) if pairs else None  1.44 us
    pallas_call x1, Pallas kernels, split(): pl.pallas_call(functools.partial(split_kernel, chips), out_shape=(pltpu.V...  1.27 us
    ppermute x1, starting transfers between devices, on_device(): lax.ppermute(give, 'gx', [(index, index ^ 1) for index in range(parts)])  0.52 us
  transfers between devices with their start and end apart: 7, of which 2 were waited for; matrix products, arithmetic and copies ran while one was open for 0% of the time, Pallas kernels for 22%

profile of v5, /device:TPU:0, one launch (start us, length us, event | category | flops | bytes accessed | tf_op | source)
XLA Modules:
  0.0 20.8 jit_solution(9880994008205175628)
XLA Ops:
  0.0 1.3 %split.1 = (bf16[528,128]{1,0:T(8,128)(2,1)S(1)}, bf16[4,64,4,128]{3,2,1,0:T(4,128)(2,1)S(1)}, bf16[4,64,4,128]{3,2,1,0:T(4,128)(2,1)S(1)}) custom-call(bf16[64,4,1024]{2,1,0:T(4,128)(2,1)} %prior_ref.1, bf16[512,128]{1,0:T(8,128)(2,1)} %bitcast.6, bf16[1,128]{1,0:T(2,128)(2,1)} %misfit_ref.1, s32[1,128]{1,0:T(1,128)} %line_ref.1), custom_call_target="tpu_custom_call" | custom-call | tf_op jit(solution)/shard_map/split/pallas_call | solution.py:73
  1.3 0.5 %collective-permute-start.3 = (bf16[4,64,4,128]{3,2,1,0:T(4,128)(2,1)S(1)}, bf16[4,64,4,128]{3,2,1,0:T(4,128)(2,1)S(1)}, u32[]{:S(2)}, u32[]{:S(2)}) collective-permute-start(bf16[4,64,4,128]{3,2,1,0:T(4,128)(2,1)S(1)} %get-tuple-element.22), channel_id=1, source_target_pairs={{0,4},{4,0},{8,12},{12,8},{16,20},{20,16},{24,28},{28,24},{1,5},{5... | collective-permute-start | bytes 786440 | tf_op jit(solution)/shard_map/ppermute | solution.py:442
  1.8 0.7 %collective-permute-start.1 = (bf16[528,128]{1,0:T(8,128)(2,1)S(1)}, bf16[528,128]{1,0:T(8,128)(2,1)S(1)}, u32[]{:S(2)}, u32[]{:S(2)}) collective-permute-start(bf16[528,128]{1,0:T(8,128)(2,1)S(1)} %get-tuple-element.16.refs_0_), channel_id=1, source_target_pairs={{1,2},{2,1},{5,6},{6,5},{9,10},{10,9},{13,14},{14,13},{17,18},{18,... | collective-permute-start | bytes 405512 | tf_op jit(solution)/shard_map/ppermute | solution.py:440
  2.5 5.5 %collective-permute-start = (bf16[528,128]{1,0:T(8,128)(2,1)S(1)}, bf16[528,128]{1,0:T(8,128)(2,1)S(1)}, u32[]{:S(2)}, u32[]{:S(2)}) collective-permute-start(bf16[528,128]{1,0:T(8,128)(2,1)S(1)} %get-tuple-element.16.refs_0_), channel_id=1, source_target_pairs={{0,1},{1,0},{2,3},{3,2},{4,5},{5,4},{6,7},{7,6},{8,9},{9,8},{10,11... | collective-permute-start | bytes 405512 | tf_op jit(solution)/shard_map/ppermute | solution.py:440
  7.9 0.0 collective-permute-start.2
  7.9 0.0 collective-permute-done.3
  7.9 0.1 sort.1
  8.1 1.6 %collective-permute-start.4 = (bf16[2,4,64,128]{3,2,1,0:T(8,128)(2,1)S(1)}, bf16[2,4,64,128]{3,2,1,0:T(8,128)(2,1)S(1)}, u32[]{:S(2)}, u32[]{:S(2)}) collective-permute-start(bf16[2,4,64,128]{3,2,1,0:T(8,128)(2,1)S(1)} %get-tuple-element.24), channel_id=1, source_target_pairs={{0,8},{4,12},{8,0},{12,4},{16,24},{20,28},{24,16},{28,20},{1,9},{5... | collective-permute-start | bytes 393224 | tf_op jit(solution)/shard_map/ppermute | solution.py:452
  9.6 1.5 %collective-permute-start.5 = (bf16[2,4,64,128]{3,2,1,0:T(8,128)(2,1)S(1)}, bf16[2,4,64,128]{3,2,1,0:T(8,128)(2,1)S(1)}, u32[]{:S(2)}, u32[]{:S(2)}) collective-permute-start(bf16[2,4,64,128]{3,2,1,0:T(8,128)(2,1)S(1)} %get-tuple-element.25), channel_id=1, source_target_pairs={{0,16},{4,20},{8,24},{12,28},{16,0},{20,4},{24,8},{28,12},{1,17},{... | collective-permute-start | bytes 393224 | tf_op jit(solution)/shard_map/ppermute | solution.py:452
  11.2 0.0 collective-permute-done.1.refs_2_
  11.2 0.5 %collective-permute-start.6 = (bf16[2,4,64,128]{3,2,1,0:T(8,128)(2,1)S(1)}, bf16[2,4,64,128]{3,2,1,0:T(8,128)(2,1)S(1)}, u32[]{:S(2)}, u32[]{:S(2)}) collective-permute-start(bf16[2,4,64,128]{3,2,1,0:T(8,128)(2,1)S(1)} %get-tuple-element.26), channel_id=1, source_target_pairs={{0,24},{4,28},{8,16},{12,20},{16,8},{20,12},{24,0},{28,4},{1,25},{... | collective-permute-start | bytes 393224 | tf_op jit(solution)/shard_map/ppermute | solution.py:452
  11.6 1.0 %collective-permute-done.refs_1_ = bf16[528,128]{1,0:T(8,128)(2,1)S(1)} collective-permute-done((bf16[528,128]{1,0:T(8,128)(2,1)S(1)}, bf16[528,128]{1,0:T(8,128)(2,1)S(1)}, u32[]{:S(2)}, u32[]{:S(2)}) %collective-permute-start) | collective-permute-done | bytes 135200 | tf_op jit(solution)/shard_map/ppermute | solution.py:440
  12.6 4.4 %near.1 = (bf16[4,528,512]{2,1,0:T(8,128)(2,1)S(1)}, f32[4,8,128]{2,1,0:T(8,128)S(1)}, bf16[2,512,512]{2,1,0:T(8,128)(2,1)S(1)}, f32[2,16,512]{2,1,0:T(8,128)S(1)}) custom-call(bf16[528,128]{1,0:T(8,128)(2,1)S(1)} %get-tuple-element.16.refs_0_, bf16[528,128]{1,0:T(8,128)(2,1)S(1)} %collective-permute-done.refs_1_, ...), custom_call_target="tpu_custom_call" | custom-call | flops 24159191040 | bytes 2097152 | tf_op jit(solution)/shard_map/near/pallas_call | solution.py:325
  17.0 0.4 %collective-permute-done.2.refs_3_ = bf16[528,128]{1,0:T(8,128)(2,1)S(1)} collective-permute-done((bf16[528,128]{1,0:T(8,128)(2,1)S(1)}, bf16[528,128]{1,0:T(8,128)(2,1)S(1)}, u32[]{:S(2)}, u32[]{:S(2)}) %collective-permute-start.2) | collective-permute-done | bytes 135200 | tf_op jit(solution)/shard_map/ppermute | solution.py:440
  17.5 0.0 collective-permute-done.4.refs_9_
  17.5 0.0 collective-permute-done.5.refs_10_
  17.5 0.0 collective-permute-done.6.refs_11_
  17.5 3.3 %finish.1 = bf16[2048,128]{1,0:T(8,128)(2,1)} custom-call(bf16[528,128]{1,0:T(8,128)(2,1)S(1)} %get-tuple-element.16.refs_0_, bf16[528,128]{1,0:T(8,128)(2,1)S(1)} %collective-permute-done.refs_1_, bf16[528,128]{1,0:T(8,128)(2,1)S(1)} %collective-permute-done.1.refs_2_, bf16[528,128]{1,0:T(8,128)(2,1)S(1)} %collective-permute-done.2.refs_3_, ...), custom_call_target="tpu_custom_call" | custom-call | tf_op jit(solution)/shard_map/finish/pallas_call | solution.py:404
Async XLA Ops:
  1.3 6.7 %collective-permute-start.3 = (bf16[4,64,4,128]{3,2,1,0:T(4,128)(2,1)S(1)}, bf16[4,64,4,128]{3,2,1,0:T(4,128)(2,1)S(1)}, u32[]{:S(2)}, u32[]{:S(2)}) collective-permute-start(bf16[4,64,4,128]{3,2,1,0:T(4,128)(2,1)S(1)} %get-tuple-element.22), channel_id=1, source_target_pairs={{0,4},{4,0},{8,12},{12,8},{16,20},{20,16},{24,28},{28,24},{1,5},{5... | collective-permute-start | bytes 786440 | tf_op jit(solution)/shard_map/ppermute | solution.py:442
  1.8 9.4 %collective-permute-start.1 = (bf16[528,128]{1,0:T(8,128)(2,1)S(1)}, bf16[528,128]{1,0:T(8,128)(2,1)S(1)}, u32[]{:S(2)}, u32[]{:S(2)}) collective-permute-start(bf16[528,128]{1,0:T(8,128)(2,1)S(1)} %get-tuple-element.16.refs_0_), channel_id=1, source_target_pairs={{1,2},{2,1},{5,6},{6,5},{9,10},{10,9},{13,14},{14,13},{17,18},{18,... | collective-permute-start | bytes 405512 | tf_op jit(solution)/shard_map/ppermute | solution.py:440
  2.5 10.2 %collective-permute-start = (bf16[528,128]{1,0:T(8,128)(2,1)S(1)}, bf16[528,128]{1,0:T(8,128)(2,1)S(1)}, u32[]{:S(2)}, u32[]{:S(2)}) collective-permute-start(bf16[528,128]{1,0:T(8,128)(2,1)S(1)} %get-tuple-element.16.refs_0_), channel_id=1, source_target_pairs={{0,1},{1,0},{2,3},{3,2},{4,5},{5,4},{6,7},{7,6},{8,9},{9,8},{10,11... | collective-permute-start | bytes 405512 | tf_op jit(solution)/shard_map/ppermute | solution.py:440
  7.9 9.5 %collective-permute-start.2 = (bf16[528,128]{1,0:T(8,128)(2,1)S(1)}, bf16[528,128]{1,0:T(8,128)(2,1)S(1)}, u32[]{:S(2)}, u32[]{:S(2)}) collective-permute-start(bf16[528,128]{1,0:T(8,128)(2,1)S(1)} %get-tuple-element.16.refs_0_), channel_id=1, source_target_pairs={{0,2},{2,0},{1,3},{3,1},{4,6},{6,4},{5,7},{7,5},{8,10},{10,8},{9,1... | collective-permute-start | bytes 405512 | tf_op jit(solution)/shard_map/ppermute | solution.py:440
  8.1 9.4 %collective-permute-start.4 = (bf16[2,4,64,128]{3,2,1,0:T(8,128)(2,1)S(1)}, bf16[2,4,64,128]{3,2,1,0:T(8,128)(2,1)S(1)}, u32[]{:S(2)}, u32[]{:S(2)}) collective-permute-start(bf16[2,4,64,128]{3,2,1,0:T(8,128)(2,1)S(1)} %get-tuple-element.24), channel_id=1, source_target_pairs={{0,8},{4,12},{8,0},{12,4},{16,24},{20,28},{24,16},{28,20},{1,9},{5... | collective-permute-start | bytes 393224 | tf_op jit(solution)/shard_map/ppermute | solution.py:452
  9.6 7.9 %collective-permute-start.5 = (bf16[2,4,64,128]{3,2,1,0:T(8,128)(2,1)S(1)}, bf16[2,4,64,128]{3,2,1,0:T(8,128)(2,1)S(1)}, u32[]{:S(2)}, u32[]{:S(2)}) collective-permute-start(bf16[2,4,64,128]{3,2,1,0:T(8,128)(2,1)S(1)} %get-tuple-element.25), channel_id=1, source_target_pairs={{0,16},{4,20},{8,24},{12,28},{16,0},{20,4},{24,8},{28,12},{1,17},{... | collective-permute-start | bytes 393224 | tf_op jit(solution)/shard_map/ppermute | solution.py:452
  11.2 6.3 %collective-permute-start.6 = (bf16[2,4,64,128]{3,2,1,0:T(8,128)(2,1)S(1)}, bf16[2,4,64,128]{3,2,1,0:T(8,128)(2,1)S(1)}, u32[]{:S(2)}, u32[]{:S(2)}) collective-permute-start(bf16[2,4,64,128]{3,2,1,0:T(8,128)(2,1)S(1)} %get-tuple-element.26), channel_id=1, source_target_pairs={{0,24},{4,28},{8,16},{12,20},{16,8},{20,12},{24,0},{28,4},{1,25},{... | collective-permute-start | bytes 393224 | tf_op jit(solution)/shard_map/ppermute | solution.py:452

commit v6 on v5

--- a/solution.py
+++ b/solution.py
@@ -19,6 +19,12 @@
 def swap_pairs(size, reach, phase):
     lows = [i for i in range(size - reach) if (i // reach) % 2 == phase]
     return [pair for i in lows for pair in ((i, i + reach), (i + reach, i))]
+
+
+def everyone(pairs, parts, size):
+    idle = set(range(size)) - {place for pair in pairs for place in pair}
+    moves = [(c * size + i, c * size + j) for c in range(parts) for i, j in pairs]
+    return moves + [(c * size + i, (c ^ 1) * size + i) for c in range(parts) for i in sorted(idle)]
 
 
 def target_chip(chip, step, chips):
@@ -437,7 +443,9 @@
     )
 
     def trade(pairs):
-        return lax.ppermute(packed, "gy", pairs) if pairs else None
+        if not pairs:
+            return None
+        return lax.ppermute(packed, ("gx", "gy"), everyone(pairs, parts, size))
 
     got = lax.ppermute(give, "gx", [(index, index ^ 1) for index in range(parts)])
     first = trade(swap_pairs(size, 1, 0))

time: 21 us -> 20.4 us (0.971)
  starting transfers between devices: 10.2 us -> 9.74 us
    ppermute x3, waiting for transfers between devices: 1.44 us -> 0.04 us  [trade(): return lax.ppermute(packed, ('gx', 'gy'), everyone(pairs, parts, size))]
    ppermute x3, waiting for transfers between devices: 0.02 us -> 1.33 us  [on_device(): blocks.append(lax.ppermute(block, 'gx', pairs))]
    ppermute x3, starting transfers between devices: 6.14 us -> 5.67 us  [trade(): return lax.ppermute(packed, ('gx', 'gy'), everyone(pairs, parts, size))]
  transfers between devices with their start and end apart: 7 -> 7, of which waited for: 2 -> 1; matrix products, arithmetic and copies ran while one was open for 0% -> 0% of each run, Pallas kernels for 22% -> 22%
where the time goes in v6:
time: 20.4 us; the launch traced here: 20.3 us
  starting transfers between devices  9.74 us (48%)
  Pallas kernels  9.11 us (45%)
  waiting for transfers between devices  1.38 us (7%)
    ppermute x3, starting transfers between devices, trade(): return lax.ppermute(packed, ('gx', 'gy'), everyone(pairs, parts, size))  5.67 us
    pallas_call x1, Pallas kernels, weights(): pl.pallas_call(functools.partial(near_kernel, size, rows, beyond is not N...  4.4 us
    ppermute x3, starting transfers between devices, on_device(): blocks.append(lax.ppermute(block, 'gx', pairs))  3.55 us
    pallas_call x1, Pallas kernels, finish(): pl.pallas_call(functools.partial(finish_kernel, size, rows), out_shape=ja...  3.32 us
    ppermute x3, waiting for transfers between devices, on_device(): blocks.append(lax.ppermute(block, 'gx', pairs))  1.33 us
    pallas_call x1, Pallas kernels, split(): pl.pallas_call(functools.partial(split_kernel, chips), out_shape=(pltpu.V...  1.27 us
    ppermute x1, starting transfers between devices, on_device(): lax.ppermute(give, 'gx', [(index, index ^ 1) for index in range(parts)])  0.52 us
  transfers between devices with their start and end apart: 7, of which 1 were waited for; matrix products, arithmetic and copies ran while one was open for 0% of the time, Pallas kernels for 22%

profile of v6, /device:TPU:0, one launch (start us, length us, event | category | flops | bytes accessed | tf_op | source)
XLA Modules:
  0.0 20.3 jit_solution(9735387757841727112)
XLA Ops:
  0.0 1.3 %split.1 = (bf16[528,128]{1,0:T(8,128)(2,1)S(1)}, bf16[4,64,4,128]{3,2,1,0:T(4,128)(2,1)S(1)}, bf16[4,64,4,128]{3,2,1,0:T(4,128)(2,1)S(1)}) custom-call(bf16[64,4,1024]{2,1,0:T(4,128)(2,1)} %prior_ref.1, bf16[512,128]{1,0:T(8,128)(2,1)} %bitcast.6, bf16[1,128]{1,0:T(2,128)(2,1)} %misfit_ref.1, s32[1,128]{1,0:T(1,128)} %line_ref.1), custom_call_target="tpu_custom_call" | custom-call | tf_op jit(solution)/shard_map/split/pallas_call | solution.py:79
  1.3 0.5 %collective-permute-start.3 = (bf16[4,64,4,128]{3,2,1,0:T(4,128)(2,1)S(1)}, bf16[4,64,4,128]{3,2,1,0:T(4,128)(2,1)S(1)}, u32[]{:S(2)}, u32[]{:S(2)}) collective-permute-start(bf16[4,64,4,128]{3,2,1,0:T(4,128)(2,1)S(1)} %get-tuple-element.22), channel_id=1, source_target_pairs={{0,4},{4,0},{8,12},{12,8},{16,20},{20,16},{24,28},{28,24},{1,5},{5... | collective-permute-start | bytes 786440 | tf_op jit(solution)/shard_map/ppermute | solution.py:450
  1.8 0.1 collective-permute-start.1
  1.9 4.1 %collective-permute-start = (bf16[528,128]{1,0:T(8,128)(2,1)S(1)}, bf16[528,128]{1,0:T(8,128)(2,1)S(1)}, u32[]{:S(2)}, u32[]{:S(2)}) collective-permute-start(bf16[528,128]{1,0:T(8,128)(2,1)S(1)} %get-tuple-element.16.refs_0_), channel_id=1, source_target_pairs={{0,1},{1,0},{2,3},{3,2},{4,5},{5,4},{6,7},{7,6},{8,9},{9,8},{10,11... | collective-permute-start | bytes 405512 | tf_op jit(solution)/shard_map/ppermute | solution.py:448
  6.0 1.4 %collective-permute-start.2 = (bf16[528,128]{1,0:T(8,128)(2,1)S(1)}, bf16[528,128]{1,0:T(8,128)(2,1)S(1)}, u32[]{:S(2)}, u32[]{:S(2)}) collective-permute-start(bf16[528,128]{1,0:T(8,128)(2,1)S(1)} %get-tuple-element.16.refs_0_), channel_id=1, source_target_pairs={{0,2},{2,0},{1,3},{3,1},{4,6},{6,4},{5,7},{7,5},{8,10},{10,8},{9,1... | collective-permute-start | bytes 405512 | tf_op jit(solution)/shard_map/ppermute | solution.py:448
  7.5 0.0 collective-permute-done.3
  7.5 0.1 sort.1
  7.6 1.6 %collective-permute-start.4 = (bf16[2,4,64,128]{3,2,1,0:T(8,128)(2,1)S(1)}, bf16[2,4,64,128]{3,2,1,0:T(8,128)(2,1)S(1)}, u32[]{:S(2)}, u32[]{:S(2)}) collective-permute-start(bf16[2,4,64,128]{3,2,1,0:T(8,128)(2,1)S(1)} %get-tuple-element.24), channel_id=1, source_target_pairs={{0,8},{4,12},{8,0},{12,4},{16,24},{20,28},{24,16},{28,20},{1,9},{5... | collective-permute-start | bytes 393224 | tf_op jit(solution)/shard_map/ppermute | solution.py:460
  9.2 1.5 %collective-permute-start.5 = (bf16[2,4,64,128]{3,2,1,0:T(8,128)(2,1)S(1)}, bf16[2,4,64,128]{3,2,1,0:T(8,128)(2,1)S(1)}, u32[]{:S(2)}, u32[]{:S(2)}) collective-permute-start(bf16[2,4,64,128]{3,2,1,0:T(8,128)(2,1)S(1)} %get-tuple-element.25), channel_id=1, source_target_pairs={{0,16},{4,20},{8,24},{12,28},{16,0},{20,4},{24,8},{28,12},{1,17},{... | collective-permute-start | bytes 393224 | tf_op jit(solution)/shard_map/ppermute | solution.py:460
  10.7 0.0 collective-permute-done.1.refs_2_
  10.7 0.5 %collective-permute-start.6 = (bf16[2,4,64,128]{3,2,1,0:T(8,128)(2,1)S(1)}, bf16[2,4,64,128]{3,2,1,0:T(8,128)(2,1)S(1)}, u32[]{:S(2)}, u32[]{:S(2)}) collective-permute-start(bf16[2,4,64,128]{3,2,1,0:T(8,128)(2,1)S(1)} %get-tuple-element.26), channel_id=1, source_target_pairs={{0,24},{4,28},{8,16},{12,20},{16,8},{20,12},{24,0},{28,4},{1,25},{... | collective-permute-start | bytes 393224 | tf_op jit(solution)/shard_map/ppermute | solution.py:460
  11.2 0.0 collective-permute-done.refs_1_
  11.2 4.4 %near.1 = (bf16[4,528,512]{2,1,0:T(8,128)(2,1)S(1)}, f32[4,8,128]{2,1,0:T(8,128)S(1)}, bf16[2,512,512]{2,1,0:T(8,128)(2,1)S(1)}, f32[2,16,512]{2,1,0:T(8,128)S(1)}) custom-call(bf16[528,128]{1,0:T(8,128)(2,1)S(1)} %get-tuple-element.16.refs_0_, bf16[528,128]{1,0:T(8,128)(2,1)S(1)} %collective-permute-done.refs_1_, ...), custom_call_target="tpu_custom_call" | custom-call | flops 24159191040 | bytes 2097152 | tf_op jit(solution)/shard_map/near/pallas_call | solution.py:331
  15.6 0.0 collective-permute-done.2.refs_3_
  15.6 0.0 collective-permute-done.4.refs_9_
  15.6 1.3 %collective-permute-done.5.refs_10_ = bf16[2,4,64,128]{3,2,1,0:T(8,128)(2,1)S(1)} collective-permute-done((bf16[2,4,64,128]{3,2,1,0:T(8,128)(2,1)S(1)}, bf16[2,4,64,128]{3,2,1,0:T(8,128)(2,1)S(1)}, u32[]{:S(2)}, u32[]{:S(2)}) %collective-permute-start.5) | collective-permute-done | bytes 131104 | tf_op jit(solution)/shard_map/ppermute | solution.py:460
  16.9 0.0 collective-permute-done.6.refs_11_
  16.9 3.3 %finish.1 = bf16[2048,128]{1,0:T(8,128)(2,1)} custom-call(bf16[528,128]{1,0:T(8,128)(2,1)S(1)} %get-tuple-element.16.refs_0_, bf16[528,128]{1,0:T(8,128)(2,1)S(1)} %collective-permute-done.refs_1_, bf16[528,128]{1,0:T(8,128)(2,1)S(1)} %collective-permute-done.1.refs_2_, bf16[528,128]{1,0:T(8,128)(2,1)S(1)} %collective-permute-done.2.refs_3_, ...), custom_call_target="tpu_custom_call" | custom-call | tf_op jit(solution)/shard_map/finish/pallas_call | solution.py:410
Async XLA Ops:
  1.3 6.2 %collective-permute-start.3 = (bf16[4,64,4,128]{3,2,1,0:T(4,128)(2,1)S(1)}, bf16[4,64,4,128]{3,2,1,0:T(4,128)(2,1)S(1)}, u32[]{:S(2)}, u32[]{:S(2)}) collective-permute-start(bf16[4,64,4,128]{3,2,1,0:T(4,128)(2,1)S(1)} %get-tuple-element.22), channel_id=1, source_target_pairs={{0,4},{4,0},{8,12},{12,8},{16,20},{20,16},{24,28},{28,24},{1,5},{5... | collective-permute-start | bytes 786440 | tf_op jit(solution)/shard_map/ppermute | solution.py:450
  1.8 8.9 %collective-permute-start.1 = (bf16[528,128]{1,0:T(8,128)(2,1)S(1)}, bf16[528,128]{1,0:T(8,128)(2,1)S(1)}, u32[]{:S(2)}, u32[]{:S(2)}) collective-permute-start(bf16[528,128]{1,0:T(8,128)(2,1)S(1)} %get-tuple-element.16.refs_0_), channel_id=1, source_target_pairs={{1,2},{2,1},{5,6},{6,5},{9,10},{10,9},{13,14},{14,13},{17,18},{18,... | collective-permute-start | bytes 405512 | tf_op jit(solution)/shard_map/ppermute | solution.py:448
  1.9 9.3 %collective-permute-start = (bf16[528,128]{1,0:T(8,128)(2,1)S(1)}, bf16[528,128]{1,0:T(8,128)(2,1)S(1)}, u32[]{:S(2)}, u32[]{:S(2)}) collective-permute-start(bf16[528,128]{1,0:T(8,128)(2,1)S(1)} %get-tuple-element.16.refs_0_), channel_id=1, source_target_pairs={{0,1},{1,0},{2,3},{3,2},{4,5},{5,4},{6,7},{7,6},{8,9},{9,8},{10,11... | collective-permute-start | bytes 405512 | tf_op jit(solution)/shard_map/ppermute | solution.py:448
  6.0 9.6 %collective-permute-start.2 = (bf16[528,128]{1,0:T(8,128)(2,1)S(1)}, bf16[528,128]{1,0:T(8,128)(2,1)S(1)}, u32[]{:S(2)}, u32[]{:S(2)}) collective-permute-start(bf16[528,128]{1,0:T(8,128)(2,1)S(1)} %get-tuple-element.16.refs_0_), channel_id=1, source_target_pairs={{0,2},{2,0},{1,3},{3,1},{4,6},{6,4},{5,7},{7,5},{8,10},{10,8},{9,1... | collective-permute-start | bytes 405512 | tf_op jit(solution)/shard_map/ppermute | solution.py:448
  7.6 8.0 %collective-permute-start.4 = (bf16[2,4,64,128]{3,2,1,0:T(8,128)(2,1)S(1)}, bf16[2,4,64,128]{3,2,1,0:T(8,128)(2,1)S(1)}, u32[]{:S(2)}, u32[]{:S(2)}) collective-permute-start(bf16[2,4,64,128]{3,2,1,0:T(8,128)(2,1)S(1)} %get-tuple-element.24), channel_id=1, source_target_pairs={{0,8},{4,12},{8,0},{12,4},{16,24},{20,28},{24,16},{28,20},{1,9},{5... | collective-permute-start | bytes 393224 | tf_op jit(solution)/shard_map/ppermute | solution.py:460
  9.2 7.8 %collective-permute-start.5 = (bf16[2,4,64,128]{3,2,1,0:T(8,128)(2,1)S(1)}, bf16[2,4,64,128]{3,2,1,0:T(8,128)(2,1)S(1)}, u32[]{:S(2)}, u32[]{:S(2)}) collective-permute-start(bf16[2,4,64,128]{3,2,1,0:T(8,128)(2,1)S(1)} %get-tuple-element.25), channel_id=1, source_target_pairs={{0,16},{4,20},{8,24},{12,28},{16,0},{20,4},{24,8},{28,12},{1,17},{... | collective-permute-start | bytes 393224 | tf_op jit(solution)/shard_map/ppermute | solution.py:460
  10.7 6.3 %collective-permute-start.6 = (bf16[2,4,64,128]{3,2,1,0:T(8,128)(2,1)S(1)}, bf16[2,4,64,128]{3,2,1,0:T(8,128)(2,1)S(1)}, u32[]{:S(2)}, u32[]{:S(2)}) collective-permute-start(bf16[2,4,64,128]{3,2,1,0:T(8,128)(2,1)S(1)} %get-tuple-element.26), channel_id=1, source_target_pairs={{0,24},{4,28},{8,16},{12,20},{16,8},{20,12},{24,0},{28,4},{1,25},{... | collective-permute-start | bytes 393224 | tf_op jit(solution)/shard_map/ppermute | solution.py:460

commit v7 on v6

--- a/solution.py
+++ b/solution.py
@@ -31,6 +31,10 @@
     if chips & (chips - 1) == 0:
         return chip ^ step
     return (chip + step) % chips if isinstance(chip, int) else lax.rem(chip + step, chips)
+
+
+def exchange_steps(chips):
+    return [0] + sorted(range(1, chips), key=lambda step: -step.bit_count())
 
 
 def source_chip(chip, step, chips):
@@ -358,12 +362,13 @@
     count, obs = own_ref.shape[0] - PAD, own_ref.shape[1]
     at = Place(size, rows)
     chip = lax.axis_index("gx") // 2
-    halves = [(step, side) for step in range(chips) for side in range(2)]
+    steps = exchange_steps(chips)
+    halves = [(place, step, side) for place, step in enumerate(steps) for side in range(2)]
 
     def deviate(row):
-        blocks = [block_refs[step][side, row].astype(jnp.float32) for step, side in halves]
+        blocks = [block_refs[place][side, row].astype(jnp.float32) for place, _, side in halves]
         mean = sum(jnp.sum(block, axis=0, keepdims=True) for block in blocks) / count
-        for (step, side), block in zip(halves, blocks):
+        for (_, step, side), block in zip(halves, blocks):
             first = (2 * source_chip(chip, step, chips) + side) * members
             deviations[row, pl.ds(pl.multiple_of(first, members), members), :] = (
                 block - mean
@@ -451,13 +456,13 @@
     first = trade(swap_pairs(size, 1, 0))
     other = trade(swap_pairs(size, 1, 1))
     far, beyond = trade(swap_pairs(size, 2, 0)), trade(swap_pairs(size, 2, 1))
-    own, *sent = sort(keep, got)
-    blocks = [own]
-    for step, block in enumerate(sent, 1):
+    own_blocks = sort(keep, got)
+    blocks = [own_blocks[0]]
+    for step in exchange_steps(chips)[1:]:
         pairs = [
             (index, 2 * target_chip(index // 2, step, chips) + index % 2) for index in range(parts)
         ]
-        blocks.append(lax.ppermute(block, "gx", pairs))
+        blocks.append(lax.ppermute(own_blocks[step], "gx", pairs))
     mixes = weights(packed, first, other, beyond, size, rows)
     return finish((packed, first, other, far), mixes, blocks, size)
 

time: 20.4 us -> 19.9 us (0.975)
  waiting for transfers between devices: 1.38 us -> 0.85 us
    ppermute x3, waiting for transfers between devices: 1.33 us -> 0.8 us  [on_device(): blocks.append(lax.ppermute(own_blocks[step], 'gx', pairs))]
  transfers between devices with their start and end apart: 7 -> 7, of which waited for: 1 -> 2; matrix products, arithmetic and copies ran while one was open for 0% -> 0% of each run, Pallas kernels for 22% -> 23%
where the time goes in v7:
time: 19.9 us; the launch traced here: 19.7 us
  starting transfers between devices  9.74 us (49%)
  Pallas kernels  9.12 us (46%)
  waiting for transfers between devices  0.85 us (4%)
    ppermute x3, starting transfers between devices, trade(): return lax.ppermute(packed, ('gx', 'gy'), everyone(pairs, parts, size))  5.67 us
    pallas_call x1, Pallas kernels, weights(): pl.pallas_call(functools.partial(near_kernel, size, rows, beyond is not N...  4.39 us
    ppermute x3, starting transfers between devices, on_device(): blocks.append(lax.ppermute(own_blocks[step], 'gx', pairs))  3.55 us
    pallas_call x1, Pallas kernels, finish(): pl.pallas_call(functools.partial(finish_kernel, size, rows), out_shape=ja...  3.33 us
    pallas_call x1, Pallas kernels, split(): pl.pallas_call(functools.partial(split_kernel, chips), out_shape=(pltpu.V...  1.27 us
    ppermute x3, waiting for transfers between devices, on_device(): blocks.append(lax.ppermute(own_blocks[step], 'gx', pairs))  0.8 us
    ppermute x1, starting transfers between devices, on_device(): lax.ppermute(give, 'gx', [(index, index ^ 1) for index in range(parts)])  0.52 us
  transfers between devices with their start and end apart: 7, of which 2 were waited for; matrix products, arithmetic and copies ran while one was open for 0% of the time, Pallas kernels for 23%

profile of v7, /device:TPU:0, one launch (start us, length us, event | category | flops | bytes accessed | tf_op | source)
XLA Modules:
  0.0 19.7 jit_solution(7977132499185600252)
XLA Ops:
  0.0 1.3 %split.1 = (bf16[528,128]{1,0:T(8,128)(2,1)S(1)}, bf16[4,64,4,128]{3,2,1,0:T(4,128)(2,1)S(1)}, bf16[4,64,4,128]{3,2,1,0:T(4,128)(2,1)S(1)}) custom-call(bf16[64,4,1024]{2,1,0:T(4,128)(2,1)} %prior_ref.1, bf16[512,128]{1,0:T(8,128)(2,1)} %bitcast.6, bf16[1,128]{1,0:T(2,128)(2,1)} %misfit_ref.1, s32[1,128]{1,0:T(1,128)} %line_ref.1), custom_call_target="tpu_custom_call" | custom-call | tf_op jit(solution)/shard_map/split/pallas_call | solution.py:83
  1.3 0.5 %collective-permute-start.3 = (bf16[4,64,4,128]{3,2,1,0:T(4,128)(2,1)S(1)}, bf16[4,64,4,128]{3,2,1,0:T(4,128)(2,1)S(1)}, u32[]{:S(2)}, u32[]{:S(2)}) collective-permute-start(bf16[4,64,4,128]{3,2,1,0:T(4,128)(2,1)S(1)} %get-tuple-element.22), channel_id=1, source_target_pairs={{0,4},{4,0},{8,12},{12,8},{16,20},{20,16},{24,28},{28,24},{1,5},{5... | collective-permute-start | bytes 786440 | tf_op jit(solution)/shard_map/ppermute | solution.py:455
  1.8 0.1 collective-permute-start.1
  1.9 4.1 %collective-permute-start = (bf16[528,128]{1,0:T(8,128)(2,1)S(1)}, bf16[528,128]{1,0:T(8,128)(2,1)S(1)}, u32[]{:S(2)}, u32[]{:S(2)}) collective-permute-start(bf16[528,128]{1,0:T(8,128)(2,1)S(1)} %get-tuple-element.16.refs_0_), channel_id=1, source_target_pairs={{0,1},{1,0},{2,3},{3,2},{4,5},{5,4},{6,7},{7,6},{8,9},{9,8},{10,11... | collective-permute-start | bytes 405512 | tf_op jit(solution)/shard_map/ppermute | solution.py:453
  6.0 1.4 %collective-permute-start.2 = (bf16[528,128]{1,0:T(8,128)(2,1)S(1)}, bf16[528,128]{1,0:T(8,128)(2,1)S(1)}, u32[]{:S(2)}, u32[]{:S(2)}) collective-permute-start(bf16[528,128]{1,0:T(8,128)(2,1)S(1)} %get-tuple-element.16.refs_0_), channel_id=1, source_target_pairs={{0,2},{2,0},{1,3},{3,1},{4,6},{6,4},{5,7},{7,5},{8,10},{10,8},{9,1... | collective-permute-start | bytes 405512 | tf_op jit(solution)/shard_map/ppermute | solution.py:453
  7.5 0.0 collective-permute-done.3
  7.5 0.1 sort.1
  7.6 2.5 %collective-permute-start.4 = (bf16[2,4,64,128]{3,2,1,0:T(8,128)(2,1)S(1)}, bf16[2,4,64,128]{3,2,1,0:T(8,128)(2,1)S(1)}, u32[]{:S(2)}, u32[]{:S(2)}) collective-permute-start(bf16[2,4,64,128]{3,2,1,0:T(8,128)(2,1)S(1)} %get-tuple-element.24), channel_id=1, source_target_pairs={{0,24},{4,28},{8,16},{12,20},{16,8},{20,12},{24,0},{28,4},{1,25},{... | collective-permute-start | bytes 393224 | tf_op jit(solution)/shard_map/ppermute | solution.py:465
  10.1 0.5 %collective-permute-start.5 = (bf16[2,4,64,128]{3,2,1,0:T(8,128)(2,1)S(1)}, bf16[2,4,64,128]{3,2,1,0:T(8,128)(2,1)S(1)}, u32[]{:S(2)}, u32[]{:S(2)}) collective-permute-start(bf16[2,4,64,128]{3,2,1,0:T(8,128)(2,1)S(1)} %get-tuple-element.25), channel_id=1, source_target_pairs={{0,8},{4,12},{8,0},{12,4},{16,24},{20,28},{24,16},{28,20},{1,9},{5... | collective-permute-start | bytes 393224 | tf_op jit(solution)/shard_map/ppermute | solution.py:465
  10.7 0.0 collective-permute-done.1.refs_2_
  10.7 0.5 %collective-permute-start.6 = (bf16[2,4,64,128]{3,2,1,0:T(8,128)(2,1)S(1)}, bf16[2,4,64,128]{3,2,1,0:T(8,128)(2,1)S(1)}, u32[]{:S(2)}, u32[]{:S(2)}) collective-permute-start(bf16[2,4,64,128]{3,2,1,0:T(8,128)(2,1)S(1)} %get-tuple-element.26), channel_id=1, source_target_pairs={{0,16},{4,20},{8,24},{12,28},{16,0},{20,4},{24,8},{28,12},{1,17},{... | collective-permute-start | bytes 393224 | tf_op jit(solution)/shard_map/ppermute | solution.py:465
  11.2 0.0 collective-permute-done.refs_1_
  11.2 4.4 %near.1 = (bf16[4,528,512]{2,1,0:T(8,128)(2,1)S(1)}, f32[4,8,128]{2,1,0:T(8,128)S(1)}, bf16[2,512,512]{2,1,0:T(8,128)(2,1)S(1)}, f32[2,16,512]{2,1,0:T(8,128)S(1)}) custom-call(bf16[528,128]{1,0:T(8,128)(2,1)S(1)} %get-tuple-element.16.refs_0_, bf16[528,128]{1,0:T(8,128)(2,1)S(1)} %collective-permute-done.refs_1_, ...), custom_call_target="tpu_custom_call" | custom-call | flops 24159191040 | bytes 2097152 | tf_op jit(solution)/shard_map/near/pallas_call | solution.py:335
  15.6 0.0 collective-permute-done.2.refs_3_
  15.6 0.0 collective-permute-done.4.refs_9_
  15.6 0.7 %collective-permute-done.5.refs_10_ = bf16[2,4,64,128]{3,2,1,0:T(8,128)(2,1)S(1)} collective-permute-done((bf16[2,4,64,128]{3,2,1,0:T(8,128)(2,1)S(1)}, bf16[2,4,64,128]{3,2,1,0:T(8,128)(2,1)S(1)}, u32[]{:S(2)}, u32[]{:S(2)}) %collective-permute-start.5) | collective-permute-done | bytes 131104 | tf_op jit(solution)/shard_map/ppermute | solution.py:465
  16.4 0.1 collective-permute-done.6.refs_11_
  16.4 3.3 %finish.1 = bf16[2048,128]{1,0:T(8,128)(2,1)} custom-call(bf16[528,128]{1,0:T(8,128)(2,1)S(1)} %get-tuple-element.16.refs_0_, bf16[528,128]{1,0:T(8,128)(2,1)S(1)} %collective-permute-done.refs_1_, bf16[528,128]{1,0:T(8,128)(2,1)S(1)} %collective-permute-done.1.refs_2_, bf16[528,128]{1,0:T(8,128)(2,1)S(1)} %collective-permute-done.2.refs_3_, ...), custom_call_target="tpu_custom_call" | custom-call | tf_op jit(solution)/shard_map/finish/pallas_call | solution.py:415
Async XLA Ops:
  1.3 6.2 %collective-permute-start.3 = (bf16[4,64,4,128]{3,2,1,0:T(4,128)(2,1)S(1)}, bf16[4,64,4,128]{3,2,1,0:T(4,128)(2,1)S(1)}, u32[]{:S(2)}, u32[]{:S(2)}) collective-permute-start(bf16[4,64,4,128]{3,2,1,0:T(4,128)(2,1)S(1)} %get-tuple-element.22), channel_id=1, source_target_pairs={{0,4},{4,0},{8,12},{12,8},{16,20},{20,16},{24,28},{28,24},{1,5},{5... | collective-permute-start | bytes 786440 | tf_op jit(solution)/shard_map/ppermute | solution.py:455
  1.8 8.9 %collective-permute-start.1 = (bf16[528,128]{1,0:T(8,128)(2,1)S(1)}, bf16[528,128]{1,0:T(8,128)(2,1)S(1)}, u32[]{:S(2)}, u32[]{:S(2)}) collective-permute-start(bf16[528,128]{1,0:T(8,128)(2,1)S(1)} %get-tuple-element.16.refs_0_), channel_id=1, source_target_pairs={{1,2},{2,1},{5,6},{6,5},{9,10},{10,9},{13,14},{14,13},{17,18},{18,... | collective-permute-start | bytes 405512 | tf_op jit(solution)/shard_map/ppermute | solution.py:453
  1.9 9.3 %collective-permute-start = (bf16[528,128]{1,0:T(8,128)(2,1)S(1)}, bf16[528,128]{1,0:T(8,128)(2,1)S(1)}, u32[]{:S(2)}, u32[]{:S(2)}) collective-permute-start(bf16[528,128]{1,0:T(8,128)(2,1)S(1)} %get-tuple-element.16.refs_0_), channel_id=1, source_target_pairs={{0,1},{1,0},{2,3},{3,2},{4,5},{5,4},{6,7},{7,6},{8,9},{9,8},{10,11... | collective-permute-start | bytes 405512 | tf_op jit(solution)/shard_map/ppermute | solution.py:453
  6.0 9.6 %collective-permute-start.2 = (bf16[528,128]{1,0:T(8,128)(2,1)S(1)}, bf16[528,128]{1,0:T(8,128)(2,1)S(1)}, u32[]{:S(2)}, u32[]{:S(2)}) collective-permute-start(bf16[528,128]{1,0:T(8,128)(2,1)S(1)} %get-tuple-element.16.refs_0_), channel_id=1, source_target_pairs={{0,2},{2,0},{1,3},{3,1},{4,6},{6,4},{5,7},{7,5},{8,10},{10,8},{9,1... | collective-permute-start | bytes 405512 | tf_op jit(solution)/shard_map/ppermute | solution.py:453
  7.6 8.0 %collective-permute-start.4 = (bf16[2,4,64,128]{3,2,1,0:T(8,128)(2,1)S(1)}, bf16[2,4,64,128]{3,2,1,0:T(8,128)(2,1)S(1)}, u32[]{:S(2)}, u32[]{:S(2)}) collective-permute-start(bf16[2,4,64,128]{3,2,1,0:T(8,128)(2,1)S(1)} %get-tuple-element.24), channel_id=1, source_target_pairs={{0,24},{4,28},{8,16},{12,20},{16,8},{20,12},{24,0},{28,4},{1,25},{... | collective-permute-start | bytes 393224 | tf_op jit(solution)/shard_map/ppermute | solution.py:465
  10.1 6.2 %collective-permute-start.5 = (bf16[2,4,64,128]{3,2,1,0:T(8,128)(2,1)S(1)}, bf16[2,4,64,128]{3,2,1,0:T(8,128)(2,1)S(1)}, u32[]{:S(2)}, u32[]{:S(2)}) collective-permute-start(bf16[2,4,64,128]{3,2,1,0:T(8,128)(2,1)S(1)} %get-tuple-element.25), channel_id=1, source_target_pairs={{0,8},{4,12},{8,0},{12,4},{16,24},{20,28},{24,16},{28,20},{1,9},{5... | collective-permute-start | bytes 393224 | tf_op jit(solution)/shard_map/ppermute | solution.py:465
  10.7 5.8 %collective-permute-start.6 = (bf16[2,4,64,128]{3,2,1,0:T(8,128)(2,1)S(1)}, bf16[2,4,64,128]{3,2,1,0:T(8,128)(2,1)S(1)}, u32[]{:S(2)}, u32[]{:S(2)}) collective-permute-start(bf16[2,4,64,128]{3,2,1,0:T(8,128)(2,1)S(1)} %get-tuple-element.26), channel_id=1, source_target_pairs={{0,16},{4,20},{8,24},{12,28},{16,0},{20,4},{24,8},{28,12},{1,17},{... | collective-permute-start | bytes 393224 | tf_op jit(solution)/shard_map/ppermute | solution.py:465

commit v8 on v7

--- a/solution.py
+++ b/solution.py
@@ -264,8 +264,10 @@
     def side_point(self, ahead):
         return jnp.where(self.upward == ahead, jnp.float32(CP), jnp.float32(-1))
 
-    def own_point(self, ahead):
-        return jnp.where(self.upward == ahead, jnp.float32(CP - 1), jnp.float32(0))
+    def beside_term(self, row, ahead, rest_ref, small_ref):
+        point = jnp.where(self.upward == ahead, CP - 1, 0)
+        share = self.share(row, point.astype(jnp.float32))
+        return share, rest_ref[point], small_ref[point, 0:1, 0:1], small_ref[point, 8:9, :]
 
     def side(self, left, ahead):
         sign = self.sign if ahead else -self.sign
@@ -291,9 +293,7 @@
 
 def near_kernel(size, rows, has_far, *refs):
     own_ref, first_ref, other_ref = refs[:3]
-    mix_ref, diag_ref, beside_ref, small_ref, left, gram, square, last, rest = refs[
-        4 if has_far else 3 :
-    ]
+    mix_ref, diag_ref, rest, small_ref, left, gram, square, last = refs[4 if has_far else 3 :]
     count, obs = own_ref.shape[0] - PAD, own_ref.shape[1]
     at = Place(size, rows)
     ahead_is_first = at.even == at.upward
@@ -310,23 +310,23 @@
     points.append(at.side(left.at[:, 2 * obs :], False))
     results = point_weights(points, count, float(rows), gram, square, last, rest)
 
-    def term(row, point, slot):
-        return (at.share(row, point), rest[slot], *results[slot])
-
+    for point in range(CP):
+        scalar_part, mean_weights = results[point]
+        small_ref[point, 0:8, :] = jnp.broadcast_to(scalar_part, (8, count))
+        small_ref[point, 8:16, :] = jnp.broadcast_to(mean_weights, (8, count))
     for row in range(at.edge, rows - at.edge):
         low = int((row + 0.5) / at.spacing - 0.5)
-        terms = [term(row, low + step, low + step) for step in (0, 1)]
+        terms = [
+            (at.share(row, point), rest[point], *results[point]) for point in (low, low + 1)
+        ]
         write_mix(mix_ref, diag_ref, row, terms, count)
     for step in range(at.edge):
         row = at.edge_row(False, step)
-        terms = [term(row, point, point) for point in range(CP)]
-        terms.append(term(row, at.side_point(False), CP))
+        terms = [
+            at.beside_term(row, False, rest, small_ref),
+            (at.share(row, at.side_point(False)), rest[CP], *results[CP]),
+        ]
         write_mix(mix_ref, diag_ref, row, terms, count)
-    for point in range(CP):
-        beside_ref[point] = rest[point]
-        scalar_part, mean_weights = results[point]
-        small_ref[point, 0:8, :] = jnp.broadcast_to(scalar_part, (8, count))
-        small_ref[point, 8:16, :] = jnp.broadcast_to(mean_weights, (8, count))
 
 
 def weights(own, first, other, beyond, size, rows):
@@ -337,13 +337,13 @@
         out_shape=(
             pltpu.VMEM((rows, count + PAD, count), jnp.bfloat16),
             pltpu.VMEM((rows, 8, 128), jnp.float32),
-            pltpu.VMEM((CP, count, count), jnp.bfloat16),
+            pltpu.VMEM((CP + 1, count, count), jnp.bfloat16),
             pltpu.VMEM((CP, 16, count), jnp.float32),
         ),
         in_specs=[VMEM] * len(near_inputs),
         out_specs=(VMEM,) * 4,
         scratch_shapes=[pltpu.VMEM((count + PAD, 5 * obs), jnp.bfloat16)]
-        + [pltpu.VMEM((CP + 1, count, count), jnp.bfloat16)] * 4,
+        + [pltpu.VMEM((CP + 1, count, count), jnp.bfloat16)] * 3,
         compiler_params=pltpu.CompilerParams(vmem_limit_bytes=40 * MIB),
         cost_estimate=pl.CostEstimate(
             flops=NEAR_FLOPS * count**3, bytes_accessed=8 * count * count, transcendentals=0
@@ -399,10 +399,10 @@
     points = [at.side(left, True)]
     results = point_weights(points, count, float(rows), gram, square, last, rest, between)
     for step, row in enumerate(ahead):
-        terms = [(at.share(row, at.side_point(True)), rest[0], *results[0])]
-        for point in range(CP):
-            small = (small_ref[point, 0:1, 0:1], small_ref[point, 8:9, :])
-            terms.append((at.share(row, point), beside_ref[point], *small))
+        terms = [
+            (at.share(row, at.side_point(True)), rest[0], *results[0]),
+            at.beside_term(row, True, beside_ref, small_ref),
+        ]
         diag = mix_rows(edge_mix.at[step], terms, count)
         apply(row, means[step], edge_mix[step], diag)
     out_ref[...] = wide[...].astype(jnp.bfloat16)

time: 19.9 us -> 19.8 us (level)
  transfers between devices with their start and end apart: 7 -> 7, of which waited for: 2 -> 3; matrix products, arithmetic and copies ran while one was open for 0% -> 0% of each run, Pallas kernels for 23% -> 22%
where the time goes in v8:
time: 19.8 us; the launch traced here: 19.7 us
  starting transfers between devices  9.74 us (49%)
  Pallas kernels  8.98 us (45%)
  waiting for transfers between devices  0.95 us (5%)
    ppermute x3, starting transfers between devices, trade(): return lax.ppermute(packed, ('gx', 'gy'), everyone(pairs, parts, size))  5.67 us
    pallas_call x1, Pallas kernels, weights(): pl.pallas_call(functools.partial(near_kernel, size, rows, beyond is not N...  4.3 us
    ppermute x3, starting transfers between devices, on_device(): blocks.append(lax.ppermute(own_blocks[step], 'gx', pairs))  3.55 us
    pallas_call x1, Pallas kernels, finish(): pl.pallas_call(functools.partial(finish_kernel, size, rows), out_shape=ja...  3.29 us
    pallas_call x1, Pallas kernels, split(): pl.pallas_call(functools.partial(split_kernel, chips), out_shape=(pltpu.V...  1.27 us
    ppermute x3, waiting for transfers between devices, on_device(): blocks.append(lax.ppermute(own_blocks[step], 'gx', pairs))  0.8 us
    ppermute x1, starting transfers between devices, on_device(): lax.ppermute(give, 'gx', [(index, index ^ 1) for index in range(parts)])  0.52 us
  transfers between devices with their start and end apart: 7, of which 3 were waited for; matrix products, arithmetic and copies ran while one was open for 0% of the time, Pallas kernels for 22%

profile of v8, /device:TPU:0, one launch (start us, length us, event | category | flops | bytes accessed | tf_op | source)
XLA Modules:
  0.0 19.7 jit_solution(5257166489815776508)
XLA Ops:
  0.0 1.3 %split.1 = (bf16[528,128]{1,0:T(8,128)(2,1)S(1)}, bf16[4,64,4,128]{3,2,1,0:T(4,128)(2,1)S(1)}, bf16[4,64,4,128]{3,2,1,0:T(4,128)(2,1)S(1)}) custom-call(bf16[64,4,1024]{2,1,0:T(4,128)(2,1)} %prior_ref.1, bf16[512,128]{1,0:T(8,128)(2,1)} %bitcast.6, bf16[1,128]{1,0:T(2,128)(2,1)} %misfit_ref.1, s32[1,128]{1,0:T(1,128)} %line_ref.1), custom_call_target="tpu_custom_call" | custom-call | tf_op jit(solution)/shard_map/split/pallas_call | solution.py:83
  1.3 0.5 %collective-permute-start.3 = (bf16[4,64,4,128]{3,2,1,0:T(4,128)(2,1)S(1)}, bf16[4,64,4,128]{3,2,1,0:T(4,128)(2,1)S(1)}, u32[]{:S(2)}, u32[]{:S(2)}) collective-permute-start(bf16[4,64,4,128]{3,2,1,0:T(4,128)(2,1)S(1)} %get-tuple-element.22), channel_id=1, source_target_pairs={{0,4},{4,0},{8,12},{12,8},{16,20},{20,16},{24,28},{28,24},{1,5},{5... | collective-permute-start | bytes 786440 | tf_op jit(solution)/shard_map/ppermute | solution.py:455
  1.8 0.1 collective-permute-start.1
  1.9 4.1 %collective-permute-start = (bf16[528,128]{1,0:T(8,128)(2,1)S(1)}, bf16[528,128]{1,0:T(8,128)(2,1)S(1)}, u32[]{:S(2)}, u32[]{:S(2)}) collective-permute-start(bf16[528,128]{1,0:T(8,128)(2,1)S(1)} %get-tuple-element.16.refs_0_), channel_id=1, source_target_pairs={{0,1},{1,0},{2,3},{3,2},{4,5},{5,4},{6,7},{7,6},{8,9},{9,8},{10,11... | collective-permute-start | bytes 405512 | tf_op jit(solution)/shard_map/ppermute | solution.py:453
  6.0 1.4 %collective-permute-start.2 = (bf16[528,128]{1,0:T(8,128)(2,1)S(1)}, bf16[528,128]{1,0:T(8,128)(2,1)S(1)}, u32[]{:S(2)}, u32[]{:S(2)}) collective-permute-start(bf16[528,128]{1,0:T(8,128)(2,1)S(1)} %get-tuple-element.16.refs_0_), channel_id=1, source_target_pairs={{0,2},{2,0},{1,3},{3,1},{4,6},{6,4},{5,7},{7,5},{8,10},{10,8},{9,1... | collective-permute-start | bytes 405512 | tf_op jit(solution)/shard_map/ppermute | solution.py:453
  7.5 0.0 collective-permute-done.3
  7.5 0.1 sort.1
  7.6 2.5 %collective-permute-start.4 = (bf16[2,4,64,128]{3,2,1,0:T(8,128)(2,1)S(1)}, bf16[2,4,64,128]{3,2,1,0:T(8,128)(2,1)S(1)}, u32[]{:S(2)}, u32[]{:S(2)}) collective-permute-start(bf16[2,4,64,128]{3,2,1,0:T(8,128)(2,1)S(1)} %get-tuple-element.24), channel_id=1, source_target_pairs={{0,24},{4,28},{8,16},{12,20},{16,8},{20,12},{24,0},{28,4},{1,25},{... | collective-permute-start | bytes 393224 | tf_op jit(solution)/shard_map/ppermute | solution.py:465
  10.1 0.5 %collective-permute-start.5 = (bf16[2,4,64,128]{3,2,1,0:T(8,128)(2,1)S(1)}, bf16[2,4,64,128]{3,2,1,0:T(8,128)(2,1)S(1)}, u32[]{:S(2)}, u32[]{:S(2)}) collective-permute-start(bf16[2,4,64,128]{3,2,1,0:T(8,128)(2,1)S(1)} %get-tuple-element.25), channel_id=1, source_target_pairs={{0,8},{4,12},{8,0},{12,4},{16,24},{20,28},{24,16},{28,20},{1,9},{5... | collective-permute-start | bytes 393224 | tf_op jit(solution)/shard_map/ppermute | solution.py:465
  10.7 0.0 collective-permute-done.1.refs_2_
  10.7 0.5 %collective-permute-start.6 = (bf16[2,4,64,128]{3,2,1,0:T(8,128)(2,1)S(1)}, bf16[2,4,64,128]{3,2,1,0:T(8,128)(2,1)S(1)}, u32[]{:S(2)}, u32[]{:S(2)}) collective-permute-start(bf16[2,4,64,128]{3,2,1,0:T(8,128)(2,1)S(1)} %get-tuple-element.26), channel_id=1, source_target_pairs={{0,16},{4,20},{8,24},{12,28},{16,0},{20,4},{24,8},{28,12},{1,17},{... | collective-permute-start | bytes 393224 | tf_op jit(solution)/shard_map/ppermute | solution.py:465
  11.2 0.0 collective-permute-done.refs_1_
  11.2 4.3 %near.1 = (bf16[4,528,512]{2,1,0:T(8,128)(2,1)S(1)}, f32[4,8,128]{2,1,0:T(8,128)S(1)}, bf16[3,512,512]{2,1,0:T(8,128)(2,1)S(1)}, f32[2,16,512]{2,1,0:T(8,128)S(1)}) custom-call(bf16[528,128]{1,0:T(8,128)(2,1)S(1)} %get-tuple-element.16.refs_0_, bf16[528,128]{1,0:T(8,128)(2,1)S(1)} %collective-permute-done.refs_1_, ...), custom_call_target="tpu_custom_call" | custom-call | flops 24159191040 | bytes 2097152 | tf_op jit(solution)/shard_map/near/pallas_call | solution.py:335
  15.5 0.1 collective-permute-done.2.refs_3_
  15.6 0.0 collective-permute-done.4.refs_9_
  15.6 0.7 %collective-permute-done.5.refs_10_ = bf16[2,4,64,128]{3,2,1,0:T(8,128)(2,1)S(1)} collective-permute-done((bf16[2,4,64,128]{3,2,1,0:T(8,128)(2,1)S(1)}, bf16[2,4,64,128]{3,2,1,0:T(8,128)(2,1)S(1)}, u32[]{:S(2)}, u32[]{:S(2)}) %collective-permute-start.5) | collective-permute-done | bytes 131104 | tf_op jit(solution)/shard_map/ppermute | solution.py:465
  16.4 0.1 collective-permute-done.6.refs_11_
  16.4 3.3 %finish.1 = bf16[2048,128]{1,0:T(8,128)(2,1)} custom-call(bf16[528,128]{1,0:T(8,128)(2,1)S(1)} %get-tuple-element.16.refs_0_, bf16[528,128]{1,0:T(8,128)(2,1)S(1)} %collective-permute-done.refs_1_, bf16[528,128]{1,0:T(8,128)(2,1)S(1)} %collective-permute-done.1.refs_2_, bf16[528,128]{1,0:T(8,128)(2,1)S(1)} %collective-permute-done.2.refs_3_, ...), custom_call_target="tpu_custom_call" | custom-call | tf_op jit(solution)/shard_map/finish/pallas_call | solution.py:415
Async XLA Ops:
  1.3 6.2 %collective-permute-start.3 = (bf16[4,64,4,128]{3,2,1,0:T(4,128)(2,1)S(1)}, bf16[4,64,4,128]{3,2,1,0:T(4,128)(2,1)S(1)}, u32[]{:S(2)}, u32[]{:S(2)}) collective-permute-start(bf16[4,64,4,128]{3,2,1,0:T(4,128)(2,1)S(1)} %get-tuple-element.22), channel_id=1, source_target_pairs={{0,4},{4,0},{8,12},{12,8},{16,20},{20,16},{24,28},{28,24},{1,5},{5... | collective-permute-start | bytes 786440 | tf_op jit(solution)/shard_map/ppermute | solution.py:455
  1.8 8.9 %collective-permute-start.1 = (bf16[528,128]{1,0:T(8,128)(2,1)S(1)}, bf16[528,128]{1,0:T(8,128)(2,1)S(1)}, u32[]{:S(2)}, u32[]{:S(2)}) collective-permute-start(bf16[528,128]{1,0:T(8,128)(2,1)S(1)} %get-tuple-element.16.refs_0_), channel_id=1, source_target_pairs={{1,2},{2,1},{5,6},{6,5},{9,10},{10,9},{13,14},{14,13},{17,18},{18,... | collective-permute-start | bytes 405512 | tf_op jit(solution)/shard_map/ppermute | solution.py:453
  1.9 9.3 %collective-permute-start = (bf16[528,128]{1,0:T(8,128)(2,1)S(1)}, bf16[528,128]{1,0:T(8,128)(2,1)S(1)}, u32[]{:S(2)}, u32[]{:S(2)}) collective-permute-start(bf16[528,128]{1,0:T(8,128)(2,1)S(1)} %get-tuple-element.16.refs_0_), channel_id=1, source_target_pairs={{0,1},{1,0},{2,3},{3,2},{4,5},{5,4},{6,7},{7,6},{8,9},{9,8},{10,11... | collective-permute-start | bytes 405512 | tf_op jit(solution)/shard_map/ppermute | solution.py:453
  6.0 9.6 %collective-permute-start.2 = (bf16[528,128]{1,0:T(8,128)(2,1)S(1)}, bf16[528,128]{1,0:T(8,128)(2,1)S(1)}, u32[]{:S(2)}, u32[]{:S(2)}) collective-permute-start(bf16[528,128]{1,0:T(8,128)(2,1)S(1)} %get-tuple-element.16.refs_0_), channel_id=1, source_target_pairs={{0,2},{2,0},{1,3},{3,1},{4,6},{6,4},{5,7},{7,5},{8,10},{10,8},{9,1... | collective-permute-start | bytes 405512 | tf_op jit(solution)/shard_map/ppermute | solution.py:453
  7.6 8.0 %collective-permute-start.4 = (bf16[2,4,64,128]{3,2,1,0:T(8,128)(2,1)S(1)}, bf16[2,4,64,128]{3,2,1,0:T(8,128)(2,1)S(1)}, u32[]{:S(2)}, u32[]{:S(2)}) collective-permute-start(bf16[2,4,64,128]{3,2,1,0:T(8,128)(2,1)S(1)} %get-tuple-element.24), channel_id=1, source_target_pairs={{0,24},{4,28},{8,16},{12,20},{16,8},{20,12},{24,0},{28,4},{1,25},{... | collective-permute-start | bytes 393224 | tf_op jit(solution)/shard_map/ppermute | solution.py:465
  10.1 6.2 %collective-permute-start.5 = (bf16[2,4,64,128]{3,2,1,0:T(8,128)(2,1)S(1)}, bf16[2,4,64,128]{3,2,1,0:T(8,128)(2,1)S(1)}, u32[]{:S(2)}, u32[]{:S(2)}) collective-permute-start(bf16[2,4,64,128]{3,2,1,0:T(8,128)(2,1)S(1)} %get-tuple-element.25), channel_id=1, source_target_pairs={{0,8},{4,12},{8,0},{12,4},{16,24},{20,28},{24,16},{28,20},{1,9},{5... | collective-permute-start | bytes 393224 | tf_op jit(solution)/shard_map/ppermute | solution.py:465
  10.7 5.8 %collective-permute-start.6 = (bf16[2,4,64,128]{3,2,1,0:T(8,128)(2,1)S(1)}, bf16[2,4,64,128]{3,2,1,0:T(8,128)(2,1)S(1)}, u32[]{:S(2)}, u32[]{:S(2)}) collective-permute-start(bf16[2,4,64,128]{3,2,1,0:T(8,128)(2,1)S(1)} %get-tuple-element.26), channel_id=1, source_target_pairs={{0,16},{4,20},{8,24},{12,28},{16,0},{20,4},{24,8},{28,12},{1,17},{... | collective-permute-start | bytes 393224 | tf_op jit(solution)/shard_map/ppermute | solution.py:465

commit v9 on v8

--- a/solution.py
+++ b/solution.py
@@ -389,9 +389,15 @@
     behind = [at.edge_row(False, step) for step in range(at.edge)]
     ahead = [at.edge_row(True, step) for step in range(at.edge)]
     means = []
-    between = [functools.partial(whole_row, row) for row in range(at.edge, rows - at.edge)]
-    between += [functools.partial(whole_row, row) for row in behind]
-    between += [lambda: means.extend([deviate(row) for row in ahead])]
+    near_rows = list(range(at.edge, rows - at.edge)) + behind
+    near_means = [deviate(row) for row in near_rows]
+    means.extend([deviate(row) for row in ahead])
+
+    def near_row(place):
+        row = near_rows[place]
+        apply(row, near_means[place], mix_ref[row], diag_ref[row, 0:1, 0:width])
+
+    between = [functools.partial(near_row, place) for place in range(len(near_rows))]
 
     left[:, 0:obs] = jnp.where(at.even == at.upward, first_ref[...], other_ref[...])
     left[:, obs : 2 * obs] = far_ref[...]
@@ -405,7 +411,10 @@
         ]
         diag = mix_rows(edge_mix.at[step], terms, count)
         apply(row, means[step], edge_mix[step], diag)
-    out_ref[...] = wide[...].astype(jnp.bfloat16)
+    quarter = count * rows // 4
+    for part in range(4):
+        lines = pl.ds(part * quarter, quarter)
+        out_ref[lines, :] = wide[lines, :].astype(jnp.bfloat16)
 
 
 def finish(tiles, mixes, blocks, size):

time: 19.8 us -> 19.8 us (level)
  no operation moved by 1% of the time
where the time goes in v9:
time: 19.8 us; the launch traced here: 19.7 us
  starting transfers between devices  9.74 us (49%)
  Pallas kernels  8.97 us (45%)
  waiting for transfers between devices  0.95 us (5%)
    ppermute x3, starting transfers between devices, trade(): return lax.ppermute(packed, ('gx', 'gy'), everyone(pairs, parts, size))  5.67 us
    pallas_call x1, Pallas kernels, weights(): pl.pallas_call(functools.partial(near_kernel, size, rows, beyond is not N...  4.3 us
    ppermute x3, starting transfers between devices, on_device(): blocks.append(lax.ppermute(own_blocks[step], 'gx', pairs))  3.55 us
    pallas_call x1, Pallas kernels, finish(): pl.pallas_call(functools.partial(finish_kernel, size, rows), out_shape=ja...  3.28 us
    pallas_call x1, Pallas kernels, split(): pl.pallas_call(functools.partial(split_kernel, chips), out_shape=(pltpu.V...  1.27 us
    ppermute x3, waiting for transfers between devices, on_device(): blocks.append(lax.ppermute(own_blocks[step], 'gx', pairs))  0.8 us
    ppermute x1, starting transfers between devices, on_device(): lax.ppermute(give, 'gx', [(index, index ^ 1) for index in range(parts)])  0.52 us
  transfers between devices with their start and end apart: 7, of which 3 were waited for; matrix products, arithmetic and copies ran while one was open for 0% of the time, Pallas kernels for 22%

profile of v9, /device:TPU:0, one launch (start us, length us, event | category | flops | bytes accessed | tf_op | source)
XLA Modules:
  0.0 19.7 jit_solution(1714056665694019257)
XLA Ops:
  0.0 1.3 %split.1 = (bf16[528,128]{1,0:T(8,128)(2,1)S(1)}, bf16[4,64,4,128]{3,2,1,0:T(4,128)(2,1)S(1)}, bf16[4,64,4,128]{3,2,1,0:T(4,128)(2,1)S(1)}) custom-call(bf16[64,4,1024]{2,1,0:T(4,128)(2,1)} %prior_ref.1, bf16[512,128]{1,0:T(8,128)(2,1)} %bitcast.6, bf16[1,128]{1,0:T(2,128)(2,1)} %misfit_ref.1, s32[1,128]{1,0:T(1,128)} %line_ref.1), custom_call_target="tpu_custom_call" | custom-call | tf_op jit(solution)/shard_map/split/pallas_call | solution.py:83
  1.3 0.5 %collective-permute-start.3 = (bf16[4,64,4,128]{3,2,1,0:T(4,128)(2,1)S(1)}, bf16[4,64,4,128]{3,2,1,0:T(4,128)(2,1)S(1)}, u32[]{:S(2)}, u32[]{:S(2)}) collective-permute-start(bf16[4,64,4,128]{3,2,1,0:T(4,128)(2,1)S(1)} %get-tuple-element.22), channel_id=1, source_target_pairs={{0,4},{4,0},{8,12},{12,8},{16,20},{20,16},{24,28},{28,24},{1,5},{5... | collective-permute-start | bytes 786440 | tf_op jit(solution)/shard_map/ppermute | solution.py:464
  1.8 0.1 collective-permute-start.1
  1.9 4.1 %collective-permute-start = (bf16[528,128]{1,0:T(8,128)(2,1)S(1)}, bf16[528,128]{1,0:T(8,128)(2,1)S(1)}, u32[]{:S(2)}, u32[]{:S(2)}) collective-permute-start(bf16[528,128]{1,0:T(8,128)(2,1)S(1)} %get-tuple-element.16.refs_0_), channel_id=1, source_target_pairs={{0,1},{1,0},{2,3},{3,2},{4,5},{5,4},{6,7},{7,6},{8,9},{9,8},{10,11... | collective-permute-start | bytes 405512 | tf_op jit(solution)/shard_map/ppermute | solution.py:462
  6.0 1.4 %collective-permute-start.2 = (bf16[528,128]{1,0:T(8,128)(2,1)S(1)}, bf16[528,128]{1,0:T(8,128)(2,1)S(1)}, u32[]{:S(2)}, u32[]{:S(2)}) collective-permute-start(bf16[528,128]{1,0:T(8,128)(2,1)S(1)} %get-tuple-element.16.refs_0_), channel_id=1, source_target_pairs={{0,2},{2,0},{1,3},{3,1},{4,6},{6,4},{5,7},{7,5},{8,10},{10,8},{9,1... | collective-permute-start | bytes 405512 | tf_op jit(solution)/shard_map/ppermute | solution.py:462
  7.5 0.0 collective-permute-done.3
  7.5 0.1 sort.1
  7.6 2.5 %collective-permute-start.4 = (bf16[2,4,64,128]{3,2,1,0:T(8,128)(2,1)S(1)}, bf16[2,4,64,128]{3,2,1,0:T(8,128)(2,1)S(1)}, u32[]{:S(2)}, u32[]{:S(2)}) collective-permute-start(bf16[2,4,64,128]{3,2,1,0:T(8,128)(2,1)S(1)} %get-tuple-element.24), channel_id=1, source_target_pairs={{0,24},{4,28},{8,16},{12,20},{16,8},{20,12},{24,0},{28,4},{1,25},{... | collective-permute-start | bytes 393224 | tf_op jit(solution)/shard_map/ppermute | solution.py:474
  10.1 0.5 %collective-permute-start.5 = (bf16[2,4,64,128]{3,2,1,0:T(8,128)(2,1)S(1)}, bf16[2,4,64,128]{3,2,1,0:T(8,128)(2,1)S(1)}, u32[]{:S(2)}, u32[]{:S(2)}) collective-permute-start(bf16[2,4,64,128]{3,2,1,0:T(8,128)(2,1)S(1)} %get-tuple-element.25), channel_id=1, source_target_pairs={{0,8},{4,12},{8,0},{12,4},{16,24},{20,28},{24,16},{28,20},{1,9},{5... | collective-permute-start | bytes 393224 | tf_op jit(solution)/shard_map/ppermute | solution.py:474
  10.7 0.0 collective-permute-done.1.refs_2_
  10.7 0.5 %collective-permute-start.6 = (bf16[2,4,64,128]{3,2,1,0:T(8,128)(2,1)S(1)}, bf16[2,4,64,128]{3,2,1,0:T(8,128)(2,1)S(1)}, u32[]{:S(2)}, u32[]{:S(2)}) collective-permute-start(bf16[2,4,64,128]{3,2,1,0:T(8,128)(2,1)S(1)} %get-tuple-element.26), channel_id=1, source_target_pairs={{0,16},{4,20},{8,24},{12,28},{16,0},{20,4},{24,8},{28,12},{1,17},{... | collective-permute-start | bytes 393224 | tf_op jit(solution)/shard_map/ppermute | solution.py:474
  11.2 0.0 collective-permute-done.refs_1_
  11.2 4.3 %near.1 = (bf16[4,528,512]{2,1,0:T(8,128)(2,1)S(1)}, f32[4,8,128]{2,1,0:T(8,128)S(1)}, bf16[3,512,512]{2,1,0:T(8,128)(2,1)S(1)}, f32[2,16,512]{2,1,0:T(8,128)S(1)}) custom-call(bf16[528,128]{1,0:T(8,128)(2,1)S(1)} %get-tuple-element.16.refs_0_, bf16[528,128]{1,0:T(8,128)(2,1)S(1)} %collective-permute-done.refs_1_, ...), custom_call_target="tpu_custom_call" | custom-call | flops 24159191040 | bytes 2097152 | tf_op jit(solution)/shard_map/near/pallas_call | solution.py:335
  15.5 0.1 collective-permute-done.2.refs_3_
  15.6 0.0 collective-permute-done.4.refs_9_
  15.6 0.7 %collective-permute-done.5.refs_10_ = bf16[2,4,64,128]{3,2,1,0:T(8,128)(2,1)S(1)} collective-permute-done((bf16[2,4,64,128]{3,2,1,0:T(8,128)(2,1)S(1)}, bf16[2,4,64,128]{3,2,1,0:T(8,128)(2,1)S(1)}, u32[]{:S(2)}, u32[]{:S(2)}) %collective-permute-start.5) | collective-permute-done | bytes 131104 | tf_op jit(solution)/shard_map/ppermute | solution.py:474
  16.4 0.1 collective-permute-done.6.refs_11_
  16.4 3.3 %finish.1 = bf16[2048,128]{1,0:T(8,128)(2,1)} custom-call(bf16[528,128]{1,0:T(8,128)(2,1)S(1)} %get-tuple-element.16.refs_0_, bf16[528,128]{1,0:T(8,128)(2,1)S(1)} %collective-permute-done.refs_1_, bf16[528,128]{1,0:T(8,128)(2,1)S(1)} %collective-permute-done.1.refs_2_, bf16[528,128]{1,0:T(8,128)(2,1)S(1)} %collective-permute-done.2.refs_3_, ...), custom_call_target="tpu_custom_call" | custom-call | tf_op jit(solution)/shard_map/finish/pallas_call | solution.py:424
Async XLA Ops:
  1.3 6.2 %collective-permute-start.3 = (bf16[4,64,4,128]{3,2,1,0:T(4,128)(2,1)S(1)}, bf16[4,64,4,128]{3,2,1,0:T(4,128)(2,1)S(1)}, u32[]{:S(2)}, u32[]{:S(2)}) collective-permute-start(bf16[4,64,4,128]{3,2,1,0:T(4,128)(2,1)S(1)} %get-tuple-element.22), channel_id=1, source_target_pairs={{0,4},{4,0},{8,12},{12,8},{16,20},{20,16},{24,28},{28,24},{1,5},{5... | collective-permute-start | bytes 786440 | tf_op jit(solution)/shard_map/ppermute | solution.py:464
  1.8 8.9 %collective-permute-start.1 = (bf16[528,128]{1,0:T(8,128)(2,1)S(1)}, bf16[528,128]{1,0:T(8,128)(2,1)S(1)}, u32[]{:S(2)}, u32[]{:S(2)}) collective-permute-start(bf16[528,128]{1,0:T(8,128)(2,1)S(1)} %get-tuple-element.16.refs_0_), channel_id=1, source_target_pairs={{1,2},{2,1},{5,6},{6,5},{9,10},{10,9},{13,14},{14,13},{17,18},{18,... | collective-permute-start | bytes 405512 | tf_op jit(solution)/shard_map/ppermute | solution.py:462
  1.9 9.3 %collective-permute-start = (bf16[528,128]{1,0:T(8,128)(2,1)S(1)}, bf16[528,128]{1,0:T(8,128)(2,1)S(1)}, u32[]{:S(2)}, u32[]{:S(2)}) collective-permute-start(bf16[528,128]{1,0:T(8,128)(2,1)S(1)} %get-tuple-element.16.refs_0_), channel_id=1, source_target_pairs={{0,1},{1,0},{2,3},{3,2},{4,5},{5,4},{6,7},{7,6},{8,9},{9,8},{10,11... | collective-permute-start | bytes 405512 | tf_op jit(solution)/shard_map/ppermute | solution.py:462
  6.0 9.6 %collective-permute-start.2 = (bf16[528,128]{1,0:T(8,128)(2,1)S(1)}, bf16[528,128]{1,0:T(8,128)(2,1)S(1)}, u32[]{:S(2)}, u32[]{:S(2)}) collective-permute-start(bf16[528,128]{1,0:T(8,128)(2,1)S(1)} %get-tuple-element.16.refs_0_), channel_id=1, source_target_pairs={{0,2},{2,0},{1,3},{3,1},{4,6},{6,4},{5,7},{7,5},{8,10},{10,8},{9,1... | collective-permute-start | bytes 405512 | tf_op jit(solution)/shard_map/ppermute | solution.py:462
  7.6 8.0 %collective-permute-start.4 = (bf16[2,4,64,128]{3,2,1,0:T(8,128)(2,1)S(1)}, bf16[2,4,64,128]{3,2,1,0:T(8,128)(2,1)S(1)}, u32[]{:S(2)}, u32[]{:S(2)}) collective-permute-start(bf16[2,4,64,128]{3,2,1,0:T(8,128)(2,1)S(1)} %get-tuple-element.24), channel_id=1, source_target_pairs={{0,24},{4,28},{8,16},{12,20},{16,8},{20,12},{24,0},{28,4},{1,25},{... | collective-permute-start | bytes 393224 | tf_op jit(solution)/shard_map/ppermute | solution.py:474
  10.1 6.2 %collective-permute-start.5 = (bf16[2,4,64,128]{3,2,1,0:T(8,128)(2,1)S(1)}, bf16[2,4,64,128]{3,2,1,0:T(8,128)(2,1)S(1)}, u32[]{:S(2)}, u32[]{:S(2)}) collective-permute-start(bf16[2,4,64,128]{3,2,1,0:T(8,128)(2,1)S(1)} %get-tuple-element.25), channel_id=1, source_target_pairs={{0,8},{4,12},{8,0},{12,4},{16,24},{20,28},{24,16},{28,20},{1,9},{5... | collective-permute-start | bytes 393224 | tf_op jit(solution)/shard_map/ppermute | solution.py:474
  10.7 5.8 %collective-permute-start.6 = (bf16[2,4,64,128]{3,2,1,0:T(8,128)(2,1)S(1)}, bf16[2,4,64,128]{3,2,1,0:T(8,128)(2,1)S(1)}, u32[]{:S(2)}, u32[]{:S(2)}) collective-permute-start(bf16[2,4,64,128]{3,2,1,0:T(8,128)(2,1)S(1)} %get-tuple-element.26), channel_id=1, source_target_pairs={{0,16},{4,20},{8,24},{12,28},{16,0},{20,4},{24,8},{28,12},{1,17},{... | collective-permute-start | bytes 393224 | tf_op jit(solution)/shard_map/ppermute | solution.py:474
